TPU v7x, 512 devices: a whole 4x8x8 slice. The times are simulated.
512 devices in a mesh: tm: 16 (over x, z_lo), tp: 32 (over z_hi, y, core).
Axes of the slice: x: 4, y: 8, z: 8 (z_hi: 2, z_lo: 4; z = z_hi * 4 + z_lo), core: 2. Of those that a mesh axis runs over, the one named last changes fastest.
Arguments:
- pixels: bfloat16 [32, 32, 32, 1176], P('tm', 'tp'), may hold values from -6 to 6
- conv_weight: bfloat16 [1176, 1280], P(None, 'tm'), may hold values from -0.1875 to 0.1875
- norm_gain: float32 [1280], replicated, may hold values from 0.1 to 1.9
- norm_bias: float32 [1280], replicated, may hold values from -3 to 3
- proj_in: bfloat16 [5120, 5120], P(None, 'tp'), may hold values from -0.078125 to 0.078125
- bias_in: float32 [5120], P('tp'), may hold values from -3 to 3
- proj_out: bfloat16 [5120, 8192], P(None, 'tp'), may hold values from -0.078125 to 0.078125
- bias_out: float32 [8192], P('tp'), may hold values from -3 to 3
Outputs:
- tokens_out: bfloat16 [32, 16, 16, 8192], P('tm', None, None, 'tp')
All inputs are finite; a program needn't handle non-finite values.
Results may differ from a plain program's by a relative error of at most 0.0052.
Values may be sent and summed in bfloat16 or wider, within the bound.
No kernel may reach another device: no remote copies, remote signals or barrier semaphores. Data moves between devices by JAX's collectives and lax.ppermute only.
A program may use at most 64 MiB of HBM per device.

v0:
```python
import jax
import jax.numpy as jnp
from jax import lax
from jax.sharding import PartitionSpec as P


def per_device(pixels, conv_weight, norm_gain, norm_bias, proj_in, bias_in, proj_out, bias_out):
    kernel = lax.all_gather(conv_weight, "tm", axis=1, tiled=True)
    pairs_here, rows_here, cols_all, patch_len = pixels.shape
    channels = kernel.shape[1]
    embed = jnp.dot(pixels.reshape(-1, patch_len), kernel, preferred_element_type=jnp.float32)
    mean = jnp.mean(embed, axis=-1, keepdims=True)
    centred = embed - mean
    variance = jnp.mean(centred * centred, axis=-1, keepdims=True)
    normed = (centred * lax.rsqrt(variance + 1e-06) * norm_gain + norm_bias).astype(jnp.bfloat16)
    normed = normed.reshape(pairs_here, rows_here, cols_all, channels)
    items = normed.reshape(pairs_here, rows_here, cols_all // 2, 2, channels)
    items = items.transpose(0, 2, 1, 3, 4).reshape(
        pairs_here * (cols_all // 2), rows_here, 2, channels
    )
    moved = lax.all_to_all(items, "tp", split_axis=0, concat_axis=1, tiled=True)
    owned = moved.shape[0]
    rows_full = moved.shape[1]
    merged = moved.reshape(owned, rows_full // 2, 2, 2, channels).reshape(
        owned * (rows_full // 2), 4 * channels
    )
    pre = (
        jnp.dot(
            lax.all_gather(merged, "tp", axis=0, tiled=True),
            proj_in,
            preferred_element_type=jnp.float32,
        )
        + bias_in
    )
    hidden = jax.nn.gelu(pre, approximate=False).astype(jnp.bfloat16)
    out_cols = proj_out.shape[1]
    summed = jnp.dot(
        lax.all_gather(hidden, "tp", axis=1, tiled=True),
        proj_out,
        preferred_element_type=jnp.float32,
    )
    result = (summed + bias_out).astype(jnp.bfloat16)
    result = result.reshape(pairs_here, cols_all // 2, rows_full // 2, out_cols).transpose(
        0, 2, 1, 3
    )
    return result


def solution(mesh):
    return jax.shard_map(
        per_device,
        mesh=mesh,
        in_specs=(
            P("tm", "tp", None, None),
            P(None, "tm"),
            P(),
            P(),
            P(None, "tp"),
            P("tp"),
            P(None, "tp"),
            P("tp"),
        ),
        out_specs=P("tm", None, None, "tp"),
        check_vma=False,
    )
```

profile of v0, /device:TPU:1, one launch (start us, length us, event | category | flops | bytes accessed | tf_op | source)
XLA Modules:
  0.0 372.9 jit_solution(11863369991544413464)
XLA Ops:
  6.5 0.0 copy-start
  6.5 0.0 copy-start.1
  6.5 0.0 copy-start.2
  6.5 0.0 copy-start.4
  6.5 0.0 all-gather.4.cloned.1.call-start
  6.6 0.7 all-gather.4.cloned.1.call-update
  7.3 0.0 all-gather.6.cloned.1.call-start
  7.3 96.3 %all-gather.4.cloned.1.call-done = bf16[1176,1280]{0,1:T(8,128)(2,1)} async-done(((bf16[1176,80]{0,1:T(8,128)(2,1)}), bf16[1176,1280]{0,1:T(8,128)(2,1)}) %all-gather.4.cloned.1.call-update) | async-done | bytes 3010576 | tf_op jit(solution)/shard_map/all_gather | solution.py:8
  103.6 3.2 fusion.11
  106.9 0.2 multiply_reduce_fusion
  107.1 0.0 copy-done.1
  107.1 0.0 copy-done.2
  107.1 0.1 add_convert_fusion
  107.3 0.1 reshape_transpose_reshape_reshape.3
  107.3 32.1 %all_to_all.4 = bf16[32,1,2,1280]{3,2,1,0:T(2,128)(2,1)S(1)} all-to-all(bf16[32,1,2,1280]{3,2,1,0:T(2,128)(2,1)S(1)} %bitcast.13), channel_id=1, replica_groups=mesh['tm'=16,'tp'=32] {'tp'}, dimensions={0} | all-to-all | bytes 327680 | tf_op jit(solution)/shard_map/all_to_all | solution.py:21
  139.5 0.8 reshape_reshape.3
  140.2 0.0 all-gather.6.cloned.1.call-update
  140.3 0.0 copy-start.3
  140.3 0.0 all-gather.8.cloned.1.call-start
  140.3 107.1 %all-gather.6.cloned.1.call-done = bf16[512,5120]{1,0:T(8,128)(2,1)} async-done(((bf16[16,5120]{1,0:T(8,128)(2,1)}), bf16[512,5120]{1,0:T(8,128)(2,1)}) %all-gather.6.cloned.1.call-update) | async-done | bytes 5242896 | tf_op jit(solution)/shard_map/all_gather | solution.py:29
  247.4 0.0 copy-done.4
  247.4 6.2 %fusion.3 = bf16[512,160]{0,1:T(8,128)(2,1)} fusion(bf16[512,5120]{1,0:T(8,128)(2,1)} %all-gather.6.cloned.1.call-done, bf16[5120,160]{0,1:T(8,128)(2,1)} %param.12, f32[160]{0:T(256)S(1)} %copy-done.4), kind=kOutput, calls=%fused_computation.6 | convolution fusion | flops 844267520 | bytes 7045760 | tf_op jit(solution)/shard_map/dot_general | solution.py:28
  253.6 0.0 all-gather.8.cloned.1.call-update
  253.6 107.9 %all-gather.8.cloned.1.call-done = bf16[512,5120]{0,1:T(8,128)(2,1)} async-done(((bf16[512,160]{0,1:T(8,128)(2,1)}), bf16[512,5120]{0,1:T(8,128)(2,1)}) %all-gather.8.cloned.1.call-update) | async-done | bytes 5242896 | tf_op jit(solution)/shard_map/all_gather | solution.py:38
  361.5 0.0 copy-done
  361.5 0.0 copy-done.3
  361.5 4.1 %fusion = bf16[512,256]{1,0:T(8,128)(2,1)S(1)} fusion(bf16[512,5120]{0,1:T(8,128)(2,1)} %all-gather.8.cloned.1.call-done, bf16[5120,256]{1,0:T(8,128)(2,1)S(1)} %copy-done, f32[256]{0:T(256)S(1)} %copy-done.3), kind=kOutput, calls=%fused_computation.1 | convolution fusion | flops 1342439424 | bytes 8127488 | tf_op jit(solution)/shard_map/dot_general | solution.py:37
  365.6 0.8 copy.13
  (2 shorter events, 0.0 us)
Async XLA Ops:
  6.5 355.0 %copy-start = (bf16[5120,256]{1,0:T(8,128)(2,1)S(1)}, bf16[5120,256]{1,0:T(8,128)(2,1)}, u32[]{:S(2)}) copy-start(bf16[5120,256]{1,0:T(8,128)(2,1)} %param.14) | copy-start | bytes 7864324
  6.5 100.6 %copy-start.1 = (f32[1280]{0:T(1024)S(1)}, f32[1280]{0:T(1024)}, u32[]{:S(2)}) copy-start(f32[1280]{0:T(1024)} %param.11) | copy-start | bytes 15364
  6.5 100.6 %copy-start.2 = (f32[1280]{0:T(1024)S(1)}, f32[1280]{0:T(1024)}, u32[]{:S(2)}) copy-start(f32[1280]{0:T(1024)} %param.10) | copy-start | bytes 15364
  6.5 240.8 %copy-start.4 = (f32[160]{0:T(256)S(1)}, f32[160]{0:T(256)}, u32[]{:S(2)}) copy-start(f32[160]{0:T(256)} %param.13) | copy-start | bytes 1924
  6.5 97.1 %all-gather.4.cloned.1.call-start = ((), (), s32[]{:S(2)}) async-start(), calls=%async_computation.1 | async-start | bytes 3481600 | tf_op jit(solution)/shard_map/all_gather | solution.py:8
  7.3 240.1 %all-gather.6.cloned.1.call-start = ((), (), s32[]{:S(2)}) async-start(), calls=%async_computation.2 | async-start | bytes 5406720 | tf_op jit(solution)/shard_map/all_gather | solution.py:29
  140.3 221.2 %copy-start.3 = (f32[256]{0:T(256)S(1)}, f32[256]{0:T(256)}, u32[]{:S(2)}) copy-start(f32[256]{0:T(256)} %param.15) | copy-start | bytes 3076
  140.3 221.2 %all-gather.8.cloned.1.call-start = ((), (), s32[]{:S(2)}) async-start(), calls=%async_computation.3 | async-start | bytes 5406720 | tf_op jit(solution)/shard_map/all_gather | solution.py:38
Sparse Core Ops, SparseCore 0:
  9.5 94.1 all-gather.3
  140.4 106.9 all-gather.5
  253.7 107.7 all-gather.7
where the time goes:
time: 373 us
  waiting for transfers between devices  312 us (84%)
  blocking collectives  32.1 us (9%)
  matrix products  13.5 us (4%)
  between operations  13.2 us (4%)
    all_gather x1, waiting for transfers between devices, per_device(): lax.all_gather(hidden, 'tp', axis=1, tiled=True)  108 us
    all_gather x1, waiting for transfers between devices, per_device(): lax.all_gather(merged, 'tp', axis=0, tiled=True)  107 us
    all_gather x1, waiting for transfers between devices, per_device(): kernel = lax.all_gather(conv_weight, 'tm', axis=1, tiled=True)  96.3 us
    all_to_all x1, blocking collectives, per_device(): moved = lax.all_to_all(items, 'tp', split_axis=0, concat_axis=1, tiled=True)  32.1 us
  transfers between devices with their start and end apart: 3, of which 3 were waited for; matrix products, arithmetic and copies ran while one was open for 0% of the time, Pallas kernels for 0%

commit v1 on v0

v1 whole, which is shorter than its diff:
```python
import functools

import jax
import jax.numpy as jnp
from jax import lax
from jax.experimental import pallas as pl
from jax.experimental.pallas import tpu as pltpu
from jax.sharding import Mesh, PartitionSpec as P

BF = jnp.bfloat16
F32 = jnp.float32
KP, C, HID = 1176, 1280, 5120
NX, NZ, NY = 4, 4, 8
PART = 320
TOK = 256


def shift(v, axis, n, by):
    return lax.ppermute(v, axis, [(i, (i + by) % n) for i in range(n)])


def shift_cores(v, axis, by):
    if axis == "x":
        pairs = [
            (2 * x + c, 2 * ((x + (by if c else -by)) % NX) + c) for x in range(NX) for c in range(2)
        ]
        return lax.ppermute(v, ("x", "c"), pairs)

    def at(z, c):
        z = z % 8
        return ((z % 4) * 2 + z // 4) * 2 + c

    pairs = [(at(z, c), at(z + (by if c else -by), c)) for z in range(8) for c in range(2)]
    return lax.ppermute(v, ("zl", "zh", "c"), pairs)


def embed_kernel(where, px, wt, *refs):
    sets = refs[:8]
    gain, beta, p_own, p_oth, b_in, out, xs, ws, ps, acc, sems = refs[8:]
    x, zl, core = where[0], where[2], where[3]
    copies = []

    def load(src, dst):
        c = pltpu.make_async_copy(src, dst, sems.at[len(copies)])
        c.start()
        copies.append(c)

    load(px, xs)
    for n in range(8):
        ahead = (0, 3, 1, 2)[n // 2]
        holder = core if n % 2 == 0 else 1 - core
        base = lax.rem(x + ahead, NX) * PART
        near = base + lax.rem(zl + 1 + 2 * holder, NZ) * 80
        load(sets[n].at[pl.ds(0, 80)], ws.at[pl.ds(pl.multiple_of(near, 16), 80)])
        for k in range(2):
            blk = base + lax.rem(zl + 2 * (1 - k), NZ) * 80
            src = pl.multiple_of(80 + 48 * k + 16 * holder, 16)
            dst = pl.multiple_of(blk + 48 * holder, 16)
            load(sets[n].at[pl.ds(src, 32)], ws.at[pl.ds(dst, 32)])
            if n % 2 == 0:
                src = pl.multiple_of(80 + 48 * k + 32 * (1 - core), 16)
                dst = pl.multiple_of(blk + 32, 16)
                load(sets[n].at[pl.ds(src, 16)], ws.at[pl.ds(dst, 16)])
    first_use = len(copies)
    load(p_own, ps.at[pl.ds(pl.multiple_of(core * 160, 32), 160)])
    load(p_oth, ps.at[pl.ds(pl.multiple_of((1 - core) * 160, 32), 160)])
    for c in copies[:first_use]:
        c.wait()
    g = gain[...]
    b = beta[...]
    for ij in range(4):
        patches = xs[:, ij].reshape(TOK, KP)
        e = lax.dot_general(patches, ws[...], (((1,), (1,)), ((), ())), preferred_element_type=F32)
        mean = jnp.sum(e, axis=-1, keepdims=True) * (1.0 / C)
        cen = e - mean
        var = jnp.sum(cen * cen, axis=-1, keepdims=True) * (1.0 / C)
        normed = (cen * lax.rsqrt(var + 1e-06) * g + b).astype(BF)
        if ij == 0:
            for c in copies[first_use:]:
                c.wait()
        part = lax.dot_general(
            normed,
            ps[:, ij * C : (ij + 1) * C],
            (((1,), (1,)), ((), ())),
            preferred_element_type=F32,
        )
        if ij == 0:
            acc[...] = part
        else:
            acc[...] += part
    pre = acc[...] + b_in[...]
    h = 0.5 * pre * (1.0 + lax.erf(pre * (0.5**0.5)))
    hs = [h[n * 16 : n * 16 + 16] for n in range(16)]
    top = jnp.concatenate(hs[0::2], axis=0)
    low = jnp.concatenate(hs[1::2], axis=0)
    out[:, :256] = top[:, :256].astype(BF)
    out[:, 256:320] = top[:, 256:].astype(BF)
    out[:, 320:384] = low[:, 256:].astype(BF)
    out[:, 384:] = low[:, :256].astype(BF)


def embed_hidden(where, px, wt, sets, gain, beta, p_own, p_oth, b_in):
    any_ = pl.BlockSpec(memory_space=pl.ANY)
    vmem = pl.BlockSpec(memory_space=pltpu.VMEM)
    return pl.pallas_call(
        embed_kernel,
        out_shape=jax.ShapeDtypeStruct((TOK // 2, 2 * PART), BF),
        in_specs=[pl.BlockSpec(memory_space=pltpu.SMEM)]
        + [any_] * 10
        + [vmem, vmem, any_, any_, vmem],
        out_specs=vmem,
        scratch_shapes=[
            pltpu.VMEM((16, 4, 16, KP), BF),
            pltpu.VMEM((C, KP), BF),
            pltpu.VMEM((PART, HID), BF),
            pltpu.VMEM((TOK, PART), F32),
            pltpu.SemaphoreType.DMA((40,)),
        ],
        compiler_params=pltpu.CompilerParams(vmem_limit_bytes=48 << 20),
        cost_estimate=pl.CostEstimate(
            flops=2 * (1024 * KP * C + TOK * HID * PART), bytes_accessed=12 << 20, transcendentals=0
        ),
        name="embed_hidden",
    )(where, px, wt, *sets, gain, beta, p_own, p_oth, b_in)


def out_kernel(where, near, *refs):
    hs = refs[:NY]
    p_own, p_oth, b_own, b_oth, o_own, o_oth, hv, pv0, pv1, acc, sems = refs[NY:]
    y, zh = where[1], where[4]
    loads = []
    for n, d in enumerate((0, -1, -2, -3, -4, 1, 2, 3) + tuple(range(NY))):
        if n < NY:
            shard = (1 - zh) * NY + lax.rem(y + (d + NY), NY)
            src = hs[n]
        else:
            shard = zh * NY + d
            src = near.at[d]
        rows = pl.ds(pl.multiple_of(shard * PART, 64), PART)
        loads.append(
            [
                pltpu.make_async_copy(p_own.at[rows], pv0.at[n], sems.at[3 * n]),
                pltpu.make_async_copy(p_oth.at[rows], pv1.at[n], sems.at[3 * n + 1]),
                pltpu.make_async_copy(src, hv.at[n], sems.at[3 * n + 2]),
            ]
        )
        for c in loads[n]:
            c.start()
    lane = lax.broadcasted_iota(jnp.int32, (TOK // 2, 128), 1)
    for n in range(2 * NY):
        for c in loads[n]:
            c.wait()
        h = hv[n]
        both = jnp.concatenate([h[:, :256], h[:, 384:]], axis=0)
        mid = h[:, 256:384]
        top = jnp.where(lane < 64, mid.astype(F32), 0.0).astype(BF)[:, :64]
        low = jnp.where(lane >= 64, mid.astype(F32), 0.0).astype(BF)
        for k, pv in enumerate((pv0, pv1)):
            part = jnp.dot(both, pv[n, :256, :], preferred_element_type=F32)
            rest = [
                jnp.dot(top, pv[n, 256:, :], preferred_element_type=F32),
                jnp.dot(low, pv[n, 192:, :], preferred_element_type=F32),
            ]
            part = part + jnp.concatenate(rest, axis=0)
            if n == 0:
                acc[k] = part
            else:
                acc[k] += part
    o_own[...] = (acc[0] + b_own[...]).astype(BF)
    o_oth[...] = (acc[1] + b_oth[...]).astype(BF)


def project_out(where, near, hs, p_own, p_oth, b_own, b_oth):
    any_ = pl.BlockSpec(memory_space=pl.ANY)
    vmem = pl.BlockSpec(memory_space=pltpu.VMEM)
    return pl.pallas_call(
        out_kernel,
        out_shape=[jax.ShapeDtypeStruct((TOK, 256), BF)] * 2,
        in_specs=[pl.BlockSpec(memory_space=pltpu.SMEM)] + [any_] * 11 + [vmem] * 2,
        out_specs=[vmem] * 2,
        scratch_shapes=[
            pltpu.VMEM((2 * NY, TOK // 2, 2 * PART), BF),
            pltpu.VMEM((2 * NY, PART, 256), BF),
            pltpu.VMEM((2 * NY, PART, 256), BF),
            pltpu.VMEM((2, TOK, 256), F32),
            pltpu.SemaphoreType.DMA((6 * NY,)),
        ],
        compiler_params=pltpu.CompilerParams(vmem_limit_bytes=40 << 20),
        cost_estimate=pl.CostEstimate(
            flops=2 * TOK * HID * 512, bytes_accessed=9 << 20, transcendentals=0
        ),
        name="project_out",
    )(where, near, *hs, p_own, p_oth, b_own, b_oth)


def per_device(pixels, conv_weight, norm_gain, norm_bias, proj_in, bias_in, proj_out, bias_out):
    core = lax.axis_index("c")
    first = core == 0
    where = jnp.stack([lax.axis_index(a) for a in ("x", "y", "zl", "c", "zh")]).astype(jnp.int32)

    rows = pixels.reshape(2, 32, KP)
    keep = jnp.where(first, rows[0], rows[1])
    give = jnp.where(first, rows[1], rows[0])
    got = shift(give, "c", 2, 1)
    mine = jnp.stack([jnp.where(first, keep, got), jnp.where(first, got, keep)])
    mine = mine.reshape(2, 16, 2, KP).transpose(0, 2, 1, 3).reshape(4, 16, KP)
    half = lax.all_gather(mine, "zh", axis=0)
    px = lax.all_gather(half, "y", axis=0).reshape(16, 4, 16, KP)

    wt = conv_weight.T
    wt, _ = lax.optimization_barrier((wt, half))
    part = jnp.where(first, wt[:48], wt[32:])
    near = shift_cores(wt, "z", 1)
    two = shift_cores(part, "z", 2)
    held = jnp.concatenate([near, two, part], axis=0)
    prev = shift(held, "x", NX, 1)
    nxt = shift(held, "x", NX, -1)
    far = shift_cores(jnp.where(first, nxt, prev), "x", 1)
    sets = []
    for s in (held, prev, nxt, far):
        sets += [s, shift(s, "c", 2, 1)]

    p_in = proj_in.T
    p_in_o = shift(p_in, "c", 2, 1)
    p_out_o = shift(proj_out, "c", 2, 1)
    bias = jnp.concatenate([bias_in, bias_out]).reshape(1, -1)
    bias_o = shift(bias, "c", 2, 1)
    b0, b1 = bias[:, :160], bias_o[:, :160]
    b_in = jnp.concatenate([jnp.where(first, b0, b1), jnp.where(first, b1, b0)], axis=1)
    hid = embed_hidden(
        where,
        px,
        wt,
        sets,
        norm_gain.reshape(1, C),
        norm_bias.reshape(1, C),
        p_in,
        p_in_o,
        b_in,
    )
    g_near = lax.all_gather(hid, "y", axis=0)
    partner = shift(hid, "zh", 2, 1)
    right, left = [partner], [partner]
    for step in range(4):
        right.append(shift(right[-1], "y", NY, 1))
        if step < 3:
            left.append(shift(left[-1], "y", NY, -1))
    o_own, o_oth = project_out(
        where, g_near, right + left[1:], proj_out, p_out_o, bias[:, 160:], bias_o[:, 160:]
    )
    o_got = shift(o_oth, "c", 2, 1)
    result = jnp.stack([jnp.where(first, o_own, o_got), jnp.where(first, o_got, o_own)])
    return result.reshape(2, 16, 16, 256)


def solution(mesh):
    fine = Mesh(mesh.devices.reshape(NX, NZ, 2, NY, 2), ("x", "zl", "zh", "y", "c"))
    tm, tp = ("x", "zl"), ("zh", "y", "c")
    return jax.shard_map(
        per_device,
        mesh=fine,
        in_specs=(
            P(tm, tp, None, None),
            P(None, tm),
            P(),
            P(),
            P(None, tp),
            P(tp),
            P(None, tp),
            P(tp),
        ),
        out_specs=P(tm, None, None, tp),
        check_vma=False,
    )
```

time: 373 us -> 178 us (0.48)
  waiting for transfers between devices: 312 us -> 39.7 us
  starting transfers between devices: 0.11 us -> 77.8 us
  blocking collectives: 32.1 us -> 10.1 us
  Pallas kernels: 0 us -> 21.6 us
  matrix products: 13.5 us -> 0 us
  local copies, waits for them, and re-layouts: 1.64 us -> 10.1 us
    all_gather x3 -> x2, waiting for transfers between devices: 311 us -> 0.02 us  [the longest x1 0.02 us: per_device(): px = lax.all_gather(half, 'y', axis=0).reshape(16, 4, 16, KP)]
    ppermute x0 -> x22, starting transfers between devices: none -> 77.7 us  [the longest x19 68.4 us: shift(): return lax.ppermute(v, axis, [(i, (i + by) % n) for i in range(n)])]
    ppermute x0 -> x22, waiting for transfers between devices: none -> 39.6 us  [the longest x19 33.1 us: shift(): return lax.ppermute(v, axis, [(i, (i + by) % n) for i in range(n)])]
    all_to_all x1 -> x0, blocking collectives: 32.1 us -> none  [per_device(): moved = lax.all_to_all(items, 'tp', split_axis=0, concat_axis=1, tiled=True)]
    pallas_call x0 -> x2, Pallas kernels: none -> 21.6 us  [the longest x1 11.3 us: embed_hidden(): pl.pallas_call(embed_kernel, out_shape=jax.ShapeDtypeStruct((TOK // 2, 2...]
    dot_general x3 -> x0, matrix products: 13.5 us -> none  [the longest x1 6.21 us: per_device(): jnp.dot(lax.all_gather(merged, 'tp', axis=0, tiled=True), proj_in, prefer...]
    all_gather x0 -> x1, blocking collectives: none -> 10.1 us  [per_device(): half = lax.all_gather(mine, 'zh', axis=0)]
    unnamed x10 -> x30, local copies, waits for them, and re-layouts: 0.02 us -> 9.11 us
  transfers between devices with their start and end apart: 3 -> 24, of which waited for: 3 -> 10; matrix products, arithmetic and copies ran while one was open for 0% -> 1% of each run, Pallas kernels for 0% -> 6%
where the time goes in v1:
time: 178 us; the launch traced here: 177 us
  starting transfers between devices  77.8 us (44%)
  waiting for transfers between devices  39.7 us (22%)
  Pallas kernels  21.6 us (12%)
  between operations  13.8 us (8%)
  local copies, waits for them, and re-layouts  10.1 us (6%)
  blocking collectives  10.1 us (6%)
  other arithmetic  3.86 us (2%)
    ppermute x19, starting transfers between devices, shift(): return lax.ppermute(v, axis, [(i, (i + by) % n) for i in range(n)])  68.4 us
    ppermute x19, waiting for transfers between devices, shift(): return lax.ppermute(v, axis, [(i, (i + by) % n) for i in range(n)])  33.1 us
    pallas_call x1, Pallas kernels, embed_hidden(): pl.pallas_call(embed_kernel, out_shape=jax.ShapeDtypeStruct((TOK // 2, 2...  11.3 us
    pallas_call x1, Pallas kernels, project_out(): pl.pallas_call(out_kernel, out_shape=[jax.ShapeDtypeStruct((TOK, 256), BF...  10.4 us
    all_gather x1, blocking collectives, per_device(): half = lax.all_gather(mine, 'zh', axis=0)  10.1 us
    unnamed x30, local copies, waits for them, and re-layouts  9.11 us
    ppermute x2, starting transfers between devices, shift_cores(): return lax.ppermute(v, ('zl', 'zh', 'c'), pairs)  7.4 us
    ppermute x2, waiting for transfers between devices, shift_cores(): return lax.ppermute(v, ('zl', 'zh', 'c'), pairs)  6.48 us
  transfers between devices with their start and end apart: 24, of which 10 were waited for; matrix products, arithmetic and copies ran while one was open for 1% of the time, Pallas kernels for 6%

profile of v1, /device:TPU:1, one launch (start us, length us, event | category | flops | bytes accessed | tf_op | source)
XLA Modules:
  0.0 177.1 jit_solution(13464352205878446747)
XLA Ops:
  6.5 0.0 all-gather.5.cloned.1.call-start
  6.6 1.1 select_bitcast_fusion
  7.7 8.8 %collective-permute-start = (bf16[32,1176]{1,0:T(8,128)(2,1)S(1)}, bf16[32,1176]{1,0:T(8,128)(2,1)S(1)}, u32[]{:S(2)}, u32[]{:S(2)}) collective-permute-start(bf16[32,1176]{1,0:T(8,128)(2,1)S(1)} %select_bitcast_fusion), channel_id=1, source_target_pairs={{0,1},{1,0},{2,3},{3,2},{4,5},{5,4},{6,7},{7,6},{8,9},{9,8},{10,11... | collective-permute-start | bytes 225800 | tf_op jit(solution)/shard_map/ppermute | solution.py:19
  16.5 0.9 collective-permute-done
  17.4 0.9 bitcast_select_fusion.1
  18.5 10.1 %all_gather.15 = bf16[2,4,16,1176]{3,2,1,0:T(8,128)(2,1)} all-gather(bf16[1,4,16,1176]{3,2,1,0:T(8,128)(2,1)S(1)} %bitcast.25), channel_id=1, replica_groups=mesh['x'=4,'zl'=4,'zh'=2,'y'=8,'c'=2] {'zh'}, dimensions={0}, use_global_device_ids=true | all-gather | bytes 451584 | tf_op jit(solution)/shard_map/all_gather | solution.py:207
  28.6 0.0 all-gather.5.cloned.1.call-update
  28.6 0.0 all-gather.7.cloned.1.call-start
  28.7 4.8 %collective-permute-start.1 = (bf16[80,1176]{1,0:T(8,128)(2,1)}, bf16[80,1176]{1,0:T(8,128)(2,1)S(1)}, u32[]{:S(2)}, u32[]{:S(2)}) collective-permute-start(bf16[80,1176]{1,0:T(8,128)(2,1)} %bitcast.20), channel_id=1, source_target_pairs={{0,112},{1,33},{32,0},{33,65},{64,32},{65,97},{96,64},{97,17},{16,... | collective-permute-start | bytes 564488 | tf_op jit(solution)/shard_map/ppermute | solution.py:34
  33.5 2.6 %collective-permute-start.2 = (bf16[48,1176]{1,0:T(8,128)(2,1)S(1)}, bf16[48,1176]{1,0:T(8,128)(2,1)S(1)}, u32[]{:S(2)}, u32[]{:S(2)}) collective-permute-start(bf16[48,1176]{1,0:T(8,128)(2,1)S(1)} %slice_select_fusion), channel_id=1, source_target_pairs={{0,80},{1,65},{32,112},{33,97},{64,0},{65,17},{96,32},{97,49},{16,... | collective-permute-start | bytes 338696 | tf_op jit(solution)/shard_map/ppermute | solution.py:34
  36.1 6.5 %collective-permute-done.2 = bf16[48,1176]{1,0:T(8,128)(2,1)S(1)} collective-permute-done((bf16[48,1176]{1,0:T(8,128)(2,1)S(1)}, bf16[48,1176]{1,0:T(8,128)(2,1)S(1)}, u32[]{:S(2)}, u32[]{:S(2)}) %collective-permute-start.2) | collective-permute-done | bytes 112928 | tf_op jit(solution)/shard_map/ppermute | solution.py:34
  42.6 0.0 collective-permute-done.1
  42.6 0.8 pad_maximum_fusion.refs_0_
  43.4 5.0 %collective-permute-start.6 = (bf16[176,1176]{1,0:T(8,128)(2,1)}, bf16[176,1176]{1,0:T(8,128)(2,1)S(1)}, u32[]{:S(2)}, u32[]{:S(2)}) collective-permute-start(bf16[176,1176]{1,0:T(8,128)(2,1)} %pad_maximum_fusion.refs_0_), channel_id=1, source_target_pairs={{0,384},{128,0},{256,128},{384,256},{1,385},{129,1},{257,129},{385... | collective-permute-start | bytes 1241864 | tf_op jit(solution)/shard_map/ppermute | solution.py:19
  48.5 1.9 %collective-permute-start.4 = (bf16[176,1176]{1,0:T(8,128)(2,1)}, bf16[176,1176]{1,0:T(8,128)(2,1)S(1)}, u32[]{:S(2)}, u32[]{:S(2)}) collective-permute-start(bf16[176,1176]{1,0:T(8,128)(2,1)} %pad_maximum_fusion.refs_0_), channel_id=1, source_target_pairs={{0,128},{128,256},{256,384},{384,0},{1,129},{129,257},{257,385},{3... | collective-permute-start | bytes 1241864 | tf_op jit(solution)/shard_map/ppermute | solution.py:19
  50.4 3.8 %collective-permute-start.10 = (bf16[160,5120]{1,0:T(8,128)(2,1)}, bf16[160,5120]{1,0:T(8,128)(2,1)}, u32[]{:S(2)}, u32[]{:S(2)}) collective-permute-start(bf16[160,5120]{1,0:T(8,128)(2,1)} %bitcast.23), channel_id=1, source_target_pairs={{0,1},{1,0},{2,3},{3,2},{4,5},{5,4},{6,7},{7,6},{8,9},{9,8},{10,11... | collective-permute-start | bytes 4915208 | tf_op jit(solution)/shard_map/ppermute | solution.py:19
  54.2 2.5 %collective-permute-done.6.refs_4_ = bf16[176,1176]{1,0:T(8,128)(2,1)S(1)} collective-permute-done((bf16[176,1176]{1,0:T(8,128)(2,1)}, bf16[176,1176]{1,0:T(8,128)(2,1)S(1)}, u32[]{:S(2)}, u32[]{:S(2)}) %collective-permute-start.6) | collective-permute-done | bytes 413984 | tf_op jit(solution)/shard_map/ppermute | solution.py:19
  56.7 4.9 %collective-permute-done.4.refs_2_ = bf16[176,1176]{1,0:T(8,128)(2,1)S(1)} collective-permute-done((bf16[176,1176]{1,0:T(8,128)(2,1)}, bf16[176,1176]{1,0:T(8,128)(2,1)S(1)}, u32[]{:S(2)}, u32[]{:S(2)}) %collective-permute-start.4) | collective-permute-done | bytes 413984 | tf_op jit(solution)/shard_map/ppermute | solution.py:19
  61.7 0.1 broadcast_select_fusion
  61.8 1.9 %collective-permute-start.8 = (bf16[176,1176]{1,0:T(8,128)(2,1)S(1)}, bf16[176,1176]{1,0:T(8,128)(2,1)}, u32[]{:S(2)}, u32[]{:S(2)}) collective-permute-start(bf16[176,1176]{1,0:T(8,128)(2,1)S(1)} %broadcast_select_fusion), channel_id=1, source_target_pairs={{0,384},{1,129},{128,0},{129,257},{256,128},{257,385},{384,256},{3... | collective-permute-start | bytes 1241864 | tf_op jit(solution)/shard_map/ppermute | solution.py:27
  63.7 0.1 pad_maximum_fusion.3
  63.8 4.7 %collective-permute-start.11 = (f32[1,416]{1,0:T(1,128)S(1)}, f32[1,416]{1,0:T(1,128)S(1)}, u32[]{:S(2)}, u32[]{:S(2)}) collective-permute-start(f32[1,416]{1,0:T(1,128)S(1)} %bitcast.28), channel_id=1, source_target_pairs={{0,1},{1,0},{2,3},{3,2},{4,5},{5,4},{6,7},{7,6},{8,9},{9,8},{10,11... | collective-permute-start | bytes 5000 | tf_op jit(solution)/shard_map/ppermute | solution.py:19
  68.5 1.9 %collective-permute-start.3 = (bf16[176,1176]{1,0:T(8,128)(2,1)}, bf16[176,1176]{1,0:T(8,128)(2,1)}, u32[]{:S(2)}, u32[]{:S(2)}) collective-permute-start(bf16[176,1176]{1,0:T(8,128)(2,1)} %pad_maximum_fusion.refs_0_), channel_id=1, source_target_pairs={{0,1},{1,0},{2,3},{3,2},{4,5},{5,4},{6,7},{7,6},{8,9},{9,8},{10,11... | collective-permute-start | bytes 1241864 | tf_op jit(solution)/shard_map/ppermute | solution.py:19
  70.5 2.4 %collective-permute-start.7 = (bf16[176,1176]{1,0:T(8,128)(2,1)S(1)}, bf16[176,1176]{1,0:T(8,128)(2,1)}, u32[]{:S(2)}, u32[]{:S(2)}) collective-permute-start(bf16[176,1176]{1,0:T(8,128)(2,1)S(1)} %collective-permute-done.6.refs_4_), channel_id=1, source_target_pairs={{0,1},{1,0},{2,3},{3,2},{4,5},{5,4},{6,7},{7,6},{8,9},{9,8},{10,11... | collective-permute-start | bytes 1241864 | tf_op jit(solution)/shard_map/ppermute | solution.py:19
  72.9 1.9 %collective-permute-start.5 = (bf16[176,1176]{1,0:T(8,128)(2,1)S(1)}, bf16[176,1176]{1,0:T(8,128)(2,1)}, u32[]{:S(2)}, u32[]{:S(2)}) collective-permute-start(bf16[176,1176]{1,0:T(8,128)(2,1)S(1)} %collective-permute-done.4.refs_2_), channel_id=1, source_target_pairs={{0,1},{1,0},{2,3},{3,2},{4,5},{5,4},{6,7},{7,6},{8,9},{9,8},{10,11... | collective-permute-start | bytes 1241864 | tf_op jit(solution)/shard_map/ppermute | solution.py:19
  74.8 2.4 %collective-permute-start.9 = (bf16[176,1176]{1,0:T(8,128)(2,1)}, bf16[176,1176]{1,0:T(8,128)(2,1)}, u32[]{:S(2)}, u32[]{:S(2)}) collective-permute-start(bf16[176,1176]{1,0:T(8,128)(2,1)} %collective-permute-done.8.refs_6_), channel_id=1, source_target_pairs={{0,1},{1,0},{2,3},{3,2},{4,5},{5,4},{6,7},{7,6},{8,9},{9,8},{10,11... | collective-permute-start | bytes 1241864 | tf_op jit(solution)/shard_map/ppermute | solution.py:19
  77.3 0.7 reshape.33.refs_9_
  78.0 0.1 stack.41.where
  78.1 0.1 pad_maximum_fusion.4.refs_12_
  78.2 1.9 %collective-permute-start.20 = (bf16[5120,256]{1,0:T(8,128)(2,1)S(1)}, bf16[5120,256]{1,0:T(8,128)(2,1)}, u32[]{:S(2)}, u32[]{:S(2)}) collective-permute-start(bf16[5120,256]{1,0:T(8,128)(2,1)S(1)} %copy-done), channel_id=1, source_target_pairs={{0,1},{1,0},{2,3},{3,2},{4,5},{5,4},{6,7},{7,6},{8,9},{9,8},{10,11... | collective-permute-start | bytes 7864328 | tf_op jit(solution)/shard_map/ppermute | solution.py:19
  80.1 0.0 all-gather.5.cloned.1.call-done.px
  80.1 0.0 copy-start.3
  80.2 0.9 copy-done.3
  81.1 1.4 copy-done.11
  82.5 11.3 %embed_hidden.1 = bf16[128,640]{1,0:T(8,128)(2,1)S(1)} custom-call(s32[5]{0:T(128)S(1)} %stack.41.where, bf16[16,4,16,1176]{3,2,1,0:T(8,128)(2,1)} %all-gather.5.cloned.1.call-done.px, bf16[80,1176]{1,0:T(8,128)(2,1)S(1)} %bitcast.22, bf16[176,1176]{1,0:T(8,128)(2,1)} %pad_maximum_fusion.refs_0_, bf16[176,1176]{1,0:T(8,128)(2,1)} %collective-permute-done.3.refs_1_, ...), custom_call_target="tpu_custom_call" | custom-call | flops 3921674240 | bytes 12582912 | tf_op jit(solution)/shard_map/embed_hidden/pallas_call | solution.py:105
  93.8 0.0 copy-start.4
  93.8 0.7 copy-done.4
  94.4 0.0 all-gather.7.cloned.1.call-update
  94.5 5.4 %collective-permute-start.12 = (bf16[128,640]{1,0:T(8,128)(2,1)}, bf16[128,640]{1,0:T(8,128)(2,1)S(1)}, u32[]{:S(2)}, u32[]{:S(2)}) collective-permute-start(bf16[128,640]{1,0:T(8,128)(2,1)} %copy-done.4), channel_id=1, source_target_pairs={{0,16},{16,0},{1,17},{17,1},{2,18},{18,2},{3,19},{19,3},{4,20},{20... | collective-permute-start | bytes 491528 | tf_op jit(solution)/shard_map/ppermute | solution.py:19
  99.9 9.4 %collective-permute-done.12.refs_0_ = bf16[128,640]{1,0:T(8,128)(2,1)S(1)} collective-permute-done((bf16[128,640]{1,0:T(8,128)(2,1)}, bf16[128,640]{1,0:T(8,128)(2,1)S(1)}, u32[]{:S(2)}, u32[]{:S(2)}) %collective-permute-start.12) | collective-permute-done | bytes 163872 | tf_op jit(solution)/shard_map/ppermute | solution.py:19
  109.3 3.2 %collective-permute-start.13 = (bf16[128,640]{1,0:T(8,128)(2,1)S(1)}, bf16[128,640]{1,0:T(8,128)(2,1)S(1)}, u32[]{:S(2)}, u32[]{:S(2)}) collective-permute-start(bf16[128,640]{1,0:T(8,128)(2,1)S(1)} %collective-permute-done.12.refs_0_), channel_id=1, source_target_pairs={{0,2},{2,4},{4,6},{6,8},{8,10},{10,12},{12,14},{14,0},{1,3},{3,5},... | collective-permute-start | bytes 491528 | tf_op jit(solution)/shard_map/ppermute | solution.py:19
  112.5 3.8 %collective-permute-start.17 = (bf16[128,640]{1,0:T(8,128)(2,1)S(1)}, bf16[128,640]{1,0:T(8,128)(2,1)S(1)}, u32[]{:S(2)}, u32[]{:S(2)}) collective-permute-start(bf16[128,640]{1,0:T(8,128)(2,1)S(1)} %collective-permute-done.12.refs_0_), channel_id=1, source_target_pairs={{0,14},{2,0},{4,2},{6,4},{8,6},{10,8},{12,10},{14,12},{1,15},{3,1}... | collective-permute-start | bytes 491528 | tf_op jit(solution)/shard_map/ppermute | solution.py:19
  116.3 5.4 %collective-permute-done.13.refs_1_ = bf16[128,640]{1,0:T(8,128)(2,1)S(1)} collective-permute-done((bf16[128,640]{1,0:T(8,128)(2,1)S(1)}, bf16[128,640]{1,0:T(8,128)(2,1)S(1)}, u32[]{:S(2)}, u32[]{:S(2)}) %collective-permute-start.13) | collective-permute-done | bytes 163872 | tf_op jit(solution)/shard_map/ppermute | solution.py:19
  121.6 1.9 %collective-permute-start.14 = (bf16[128,640]{1,0:T(8,128)(2,1)S(1)}, bf16[128,640]{1,0:T(8,128)(2,1)S(1)}, u32[]{:S(2)}, u32[]{:S(2)}) collective-permute-start(bf16[128,640]{1,0:T(8,128)(2,1)S(1)} %collective-permute-done.13.refs_1_), channel_id=1, source_target_pairs={{0,2},{2,4},{4,6},{6,8},{8,10},{10,12},{12,14},{14,0},{1,3},{3,5},... | collective-permute-start | bytes 491528 | tf_op jit(solution)/shard_map/ppermute | solution.py:19
  123.6 4.6 %collective-permute-start.18 = (bf16[128,640]{1,0:T(8,128)(2,1)S(1)}, bf16[128,640]{1,0:T(8,128)(2,1)S(1)}, u32[]{:S(2)}, u32[]{:S(2)}) collective-permute-start(bf16[128,640]{1,0:T(8,128)(2,1)S(1)} %collective-permute-done.17.refs_5_), channel_id=1, source_target_pairs={{0,14},{2,0},{4,2},{6,4},{8,6},{10,8},{12,10},{14,12},{1,15},{3,1}... | collective-permute-start | bytes 491528 | tf_op jit(solution)/shard_map/ppermute | solution.py:19
  128.2 4.5 %collective-permute-done.14.refs_2_ = bf16[128,640]{1,0:T(8,128)(2,1)S(1)} collective-permute-done((bf16[128,640]{1,0:T(8,128)(2,1)S(1)}, bf16[128,640]{1,0:T(8,128)(2,1)S(1)}, u32[]{:S(2)}, u32[]{:S(2)}) %collective-permute-start.14) | collective-permute-done | bytes 163872 | tf_op jit(solution)/shard_map/ppermute | solution.py:19
  132.6 1.9 %collective-permute-start.15 = (bf16[128,640]{1,0:T(8,128)(2,1)S(1)}, bf16[128,640]{1,0:T(8,128)(2,1)S(1)}, u32[]{:S(2)}, u32[]{:S(2)}) collective-permute-start(bf16[128,640]{1,0:T(8,128)(2,1)S(1)} %collective-permute-done.14.refs_2_), channel_id=1, source_target_pairs={{0,2},{2,4},{4,6},{6,8},{8,10},{10,12},{12,14},{14,0},{1,3},{3,5},... | collective-permute-start | bytes 491528 | tf_op jit(solution)/shard_map/ppermute | solution.py:19
  134.5 4.6 %collective-permute-start.19 = (bf16[128,640]{1,0:T(8,128)(2,1)S(1)}, bf16[128,640]{1,0:T(8,128)(2,1)S(1)}, u32[]{:S(2)}, u32[]{:S(2)}) collective-permute-start(bf16[128,640]{1,0:T(8,128)(2,1)S(1)} %collective-permute-done.18.refs_6_), channel_id=1, source_target_pairs={{0,14},{2,0},{4,2},{6,4},{8,6},{10,8},{12,10},{14,12},{1,15},{3,1}... | collective-permute-start | bytes 491528 | tf_op jit(solution)/shard_map/ppermute | solution.py:19
  139.1 0.8 collective-permute-done.15.refs_3_
  139.9 1.9 %collective-permute-start.16 = (bf16[128,640]{1,0:T(8,128)(2,1)S(1)}, bf16[128,640]{1,0:T(8,128)(2,1)S(1)}, u32[]{:S(2)}, u32[]{:S(2)}) collective-permute-start(bf16[128,640]{1,0:T(8,128)(2,1)S(1)} %collective-permute-done.15.refs_3_), channel_id=1, source_target_pairs={{0,2},{2,4},{4,6},{6,8},{8,10},{10,12},{12,14},{14,0},{1,3},{3,5},... | collective-permute-start | bytes 491528 | tf_op jit(solution)/shard_map/ppermute | solution.py:19
  141.8 0.7 copy-done.5
  142.5 0.1 slice.38.refs_10_
  142.6 0.1 slice.39.refs_11_
  142.6 0.7 copy-done.7
  143.3 3.8 %collective-permute-done.16.refs_4_ = bf16[128,640]{1,0:T(8,128)(2,1)S(1)} collective-permute-done((bf16[128,640]{1,0:T(8,128)(2,1)S(1)}, bf16[128,640]{1,0:T(8,128)(2,1)S(1)}, u32[]{:S(2)}, u32[]{:S(2)}) %collective-permute-start.16) | collective-permute-done | bytes 163872 | tf_op jit(solution)/shard_map/ppermute | solution.py:19
  147.1 0.7 copy-done.9
  147.8 1.3 copy-done.1
  149.1 0.9 copy-done.6
  150.0 0.9 copy-done.8
  151.0 0.9 copy-done.10
  151.9 10.4 %project_out.1 = (bf16[256,256]{1,0:T(8,128)(2,1)S(1)}, bf16[256,256]{1,0:T(8,128)(2,1)S(1)}) custom-call(s32[5]{0:T(128)S(1)} %stack.41.where, bf16[8,128,640]{2,1,0:T(8,128)(2,1)S(1)} %bitcast.19, bf16[128,640]{1,0:T(8,128)(2,1)S(1)} %collective-permute-done.12.refs_0_, bf16[128,640]{1,0:T(8,128)(2,1)S(1)} %collective-permute-done.13.refs_1_, ...), custom_call_target="tpu_custom_call" | custom-call | flops 1342177280 | bytes 9437184 | tf_op jit(solution)/shard_map/project_out/pallas_call | solution.py:176
  162.3 6.2 %collective-permute-start.21 = (bf16[256,256]{1,0:T(8,128)(2,1)S(1)}, bf16[256,256]{1,0:T(8,128)(2,1)S(1)}, u32[]{:S(2)}, u32[]{:S(2)}) collective-permute-start(bf16[256,256]{1,0:T(8,128)(2,1)S(1)} %get-tuple-element.10), channel_id=1, source_target_pairs={{0,1},{1,0},{2,3},{3,2},{4,5},{5,4},{6,7},{7,6},{8,9},{9,8},{10,11... | collective-permute-start | bytes 393224 | tf_op jit(solution)/shard_map/ppermute | solution.py:19
  168.5 1.0 collective-permute-done.21
  169.5 0.7 pad_maximum_fusion.1
  (39 shorter events, 0.2 us)
Async XLA Ops:
  6.5 26.9 %copy-start.2 = (bf16[1176,80]{0,1:T(8,128)(2,1)S(1)}, bf16[1176,80]{0,1:T(8,128)(2,1)}, u32[]{:S(2)}) copy-start(bf16[1176,80]{0,1:T(8,128)(2,1)} %param.9) | copy-start | bytes 564484
  6.5 57.1 %copy-start.13 = (f32[256]{0:T(256)S(1)}, f32[256]{0:T(256)}, u32[]{:S(2)}) copy-start(f32[256]{0:T(256)} %param.15) | copy-start | bytes 3076
  6.5 57.2 %copy-start.14 = (f32[160]{0:T(256)S(1)}, f32[160]{0:T(256)}, u32[]{:S(2)}) copy-start(f32[160]{0:T(256)} %param.13) | copy-start | bytes 1924
  6.5 70.7 %copy-start.12 = (f32[1280]{0:T(1024)S(1)}, f32[1280]{0:T(1024)}, u32[]{:S(2)}) copy-start(f32[1280]{0:T(1024)} %param.10) | copy-start | bytes 15364
  6.5 71.6 %copy-start = (bf16[5120,256]{1,0:T(8,128)(2,1)S(1)}, bf16[5120,256]{1,0:T(8,128)(2,1)}, u32[]{:S(2)}) copy-start(bf16[5120,256]{1,0:T(8,128)(2,1)} %refs_8_.1) | copy-start | bytes 7864324
  6.5 73.6 %all-gather.5.cloned.1.call-start = ((), (), s32[]{:S(2)}) async-start(), calls=%async_computation | async-start | bytes 2949120 | tf_op jit(solution)/shard_map/all_gather | solution.py:208
  7.7 9.7 %collective-permute-start = (bf16[32,1176]{1,0:T(8,128)(2,1)S(1)}, bf16[32,1176]{1,0:T(8,128)(2,1)S(1)}, u32[]{:S(2)}, u32[]{:S(2)}) collective-permute-start(bf16[32,1176]{1,0:T(8,128)(2,1)S(1)} %select_bitcast_fusion), channel_id=1, source_target_pairs={{0,1},{1,0},{2,3},{3,2},{4,5},{5,4},{6,7},{7,6},{8,9},{9,8},{10,11... | collective-permute-start | bytes 225800 | tf_op jit(solution)/shard_map/ppermute | solution.py:19
  28.6 119.2 %all-gather.7.cloned.1.call-start = ((), (), s32[]{:S(2)}) async-start(), calls=%async_computation.1 | async-start | bytes 1474560 | tf_op jit(solution)/shard_map/all_gather | solution.py:241
  28.7 13.9 %collective-permute-start.1 = (bf16[80,1176]{1,0:T(8,128)(2,1)}, bf16[80,1176]{1,0:T(8,128)(2,1)S(1)}, u32[]{:S(2)}, u32[]{:S(2)}) collective-permute-start(bf16[80,1176]{1,0:T(8,128)(2,1)} %bitcast.20), channel_id=1, source_target_pairs={{0,112},{1,33},{32,0},{33,65},{64,32},{65,97},{96,64},{97,17},{16,... | collective-permute-start | bytes 564488 | tf_op jit(solution)/shard_map/ppermute | solution.py:34
  33.5 9.1 %collective-permute-start.2 = (bf16[48,1176]{1,0:T(8,128)(2,1)S(1)}, bf16[48,1176]{1,0:T(8,128)(2,1)S(1)}, u32[]{:S(2)}, u32[]{:S(2)}) collective-permute-start(bf16[48,1176]{1,0:T(8,128)(2,1)S(1)} %slice_select_fusion), channel_id=1, source_target_pairs={{0,80},{1,65},{32,112},{33,97},{64,0},{65,17},{96,32},{97,49},{16,... | collective-permute-start | bytes 338696 | tf_op jit(solution)/shard_map/ppermute | solution.py:34
  43.4 13.3 %collective-permute-start.6 = (bf16[176,1176]{1,0:T(8,128)(2,1)}, bf16[176,1176]{1,0:T(8,128)(2,1)S(1)}, u32[]{:S(2)}, u32[]{:S(2)}) collective-permute-start(bf16[176,1176]{1,0:T(8,128)(2,1)} %pad_maximum_fusion.refs_0_), channel_id=1, source_target_pairs={{0,384},{128,0},{256,128},{384,256},{1,385},{129,1},{257,129},{385... | collective-permute-start | bytes 1241864 | tf_op jit(solution)/shard_map/ppermute | solution.py:19
  48.5 13.2 %collective-permute-start.4 = (bf16[176,1176]{1,0:T(8,128)(2,1)}, bf16[176,1176]{1,0:T(8,128)(2,1)S(1)}, u32[]{:S(2)}, u32[]{:S(2)}) collective-permute-start(bf16[176,1176]{1,0:T(8,128)(2,1)} %pad_maximum_fusion.refs_0_), channel_id=1, source_target_pairs={{0,128},{128,256},{256,384},{384,0},{1,129},{129,257},{257,385},{3... | collective-permute-start | bytes 1241864 | tf_op jit(solution)/shard_map/ppermute | solution.py:19
  50.4 29.7 %collective-permute-start.10 = (bf16[160,5120]{1,0:T(8,128)(2,1)}, bf16[160,5120]{1,0:T(8,128)(2,1)}, u32[]{:S(2)}, u32[]{:S(2)}) collective-permute-start(bf16[160,5120]{1,0:T(8,128)(2,1)} %bitcast.23), channel_id=1, source_target_pairs={{0,1},{1,0},{2,3},{3,2},{4,5},{5,4},{6,7},{7,6},{8,9},{9,8},{10,11... | collective-permute-start | bytes 4915208 | tf_op jit(solution)/shard_map/ppermute | solution.py:19
  61.8 13.1 %collective-permute-start.8 = (bf16[176,1176]{1,0:T(8,128)(2,1)S(1)}, bf16[176,1176]{1,0:T(8,128)(2,1)}, u32[]{:S(2)}, u32[]{:S(2)}) collective-permute-start(bf16[176,1176]{1,0:T(8,128)(2,1)S(1)} %broadcast_select_fusion), channel_id=1, source_target_pairs={{0,384},{1,129},{128,0},{129,257},{256,128},{257,385},{384,256},{3... | collective-permute-start | bytes 1241864 | tf_op jit(solution)/shard_map/ppermute | solution.py:27
  63.8 9.1 %collective-permute-start.11 = (f32[1,416]{1,0:T(1,128)S(1)}, f32[1,416]{1,0:T(1,128)S(1)}, u32[]{:S(2)}, u32[]{:S(2)}) collective-permute-start(f32[1,416]{1,0:T(1,128)S(1)} %bitcast.28), channel_id=1, source_target_pairs={{0,1},{1,0},{2,3},{3,2},{4,5},{5,4},{6,7},{7,6},{8,9},{9,8},{10,11... | collective-permute-start | bytes 5000 | tf_op jit(solution)/shard_map/ppermute | solution.py:19
  68.5 9.6 %collective-permute-start.3 = (bf16[176,1176]{1,0:T(8,128)(2,1)}, bf16[176,1176]{1,0:T(8,128)(2,1)}, u32[]{:S(2)}, u32[]{:S(2)}) collective-permute-start(bf16[176,1176]{1,0:T(8,128)(2,1)} %pad_maximum_fusion.refs_0_), channel_id=1, source_target_pairs={{0,1},{1,0},{2,3},{3,2},{4,5},{5,4},{6,7},{7,6},{8,9},{9,8},{10,11... | collective-permute-start | bytes 1241864 | tf_op jit(solution)/shard_map/ppermute | solution.py:19
  70.5 9.6 %collective-permute-start.7 = (bf16[176,1176]{1,0:T(8,128)(2,1)S(1)}, bf16[176,1176]{1,0:T(8,128)(2,1)}, u32[]{:S(2)}, u32[]{:S(2)}) collective-permute-start(bf16[176,1176]{1,0:T(8,128)(2,1)S(1)} %collective-permute-done.6.refs_4_), channel_id=1, source_target_pairs={{0,1},{1,0},{2,3},{3,2},{4,5},{5,4},{6,7},{7,6},{8,9},{9,8},{10,11... | collective-permute-start | bytes 1241864 | tf_op jit(solution)/shard_map/ppermute | solution.py:19
  72.9 7.2 %collective-permute-start.5 = (bf16[176,1176]{1,0:T(8,128)(2,1)S(1)}, bf16[176,1176]{1,0:T(8,128)(2,1)}, u32[]{:S(2)}, u32[]{:S(2)}) collective-permute-start(bf16[176,1176]{1,0:T(8,128)(2,1)S(1)} %collective-permute-done.4.refs_2_), channel_id=1, source_target_pairs={{0,1},{1,0},{2,3},{3,2},{4,5},{5,4},{6,7},{7,6},{8,9},{9,8},{10,11... | collective-permute-start | bytes 1241864 | tf_op jit(solution)/shard_map/ppermute | solution.py:19
  74.8 5.3 %collective-permute-start.9 = (bf16[176,1176]{1,0:T(8,128)(2,1)}, bf16[176,1176]{1,0:T(8,128)(2,1)}, u32[]{:S(2)}, u32[]{:S(2)}) collective-permute-start(bf16[176,1176]{1,0:T(8,128)(2,1)} %collective-permute-done.8.refs_6_), channel_id=1, source_target_pairs={{0,1},{1,0},{2,3},{3,2},{4,5},{5,4},{6,7},{7,6},{8,9},{9,8},{10,11... | collective-permute-start | bytes 1241864 | tf_op jit(solution)/shard_map/ppermute | solution.py:19
  78.2 64.5 %collective-permute-start.20 = (bf16[5120,256]{1,0:T(8,128)(2,1)S(1)}, bf16[5120,256]{1,0:T(8,128)(2,1)}, u32[]{:S(2)}, u32[]{:S(2)}) collective-permute-start(bf16[5120,256]{1,0:T(8,128)(2,1)S(1)} %copy-done), channel_id=1, source_target_pairs={{0,1},{1,0},{2,3},{3,2},{4,5},{5,4},{6,7},{7,6},{8,9},{9,8},{10,11... | collective-permute-start | bytes 7864328 | tf_op jit(solution)/shard_map/ppermute | solution.py:19
  80.1 0.9 copy-start.3
  81.1 1.4 copy-start.11
  93.8 0.7 copy-start.4
  94.5 14.8 %collective-permute-start.12 = (bf16[128,640]{1,0:T(8,128)(2,1)}, bf16[128,640]{1,0:T(8,128)(2,1)S(1)}, u32[]{:S(2)}, u32[]{:S(2)}) collective-permute-start(bf16[128,640]{1,0:T(8,128)(2,1)} %copy-done.4), channel_id=1, source_target_pairs={{0,16},{16,0},{1,17},{17,1},{2,18},{18,2},{3,19},{19,3},{4,20},{20... | collective-permute-start | bytes 491528 | tf_op jit(solution)/shard_map/ppermute | solution.py:19
  109.3 12.4 %collective-permute-start.13 = (bf16[128,640]{1,0:T(8,128)(2,1)S(1)}, bf16[128,640]{1,0:T(8,128)(2,1)S(1)}, u32[]{:S(2)}, u32[]{:S(2)}) collective-permute-start(bf16[128,640]{1,0:T(8,128)(2,1)S(1)} %collective-permute-done.12.refs_0_), channel_id=1, source_target_pairs={{0,2},{2,4},{4,6},{6,8},{8,10},{10,12},{12,14},{14,0},{1,3},{3,5},... | collective-permute-start | bytes 491528 | tf_op jit(solution)/shard_map/ppermute | solution.py:19
  112.5 11.1 %collective-permute-start.17 = (bf16[128,640]{1,0:T(8,128)(2,1)S(1)}, bf16[128,640]{1,0:T(8,128)(2,1)S(1)}, u32[]{:S(2)}, u32[]{:S(2)}) collective-permute-start(bf16[128,640]{1,0:T(8,128)(2,1)S(1)} %collective-permute-done.12.refs_0_), channel_id=1, source_target_pairs={{0,14},{2,0},{4,2},{6,4},{8,6},{10,8},{12,10},{14,12},{1,15},{3,1}... | collective-permute-start | bytes 491528 | tf_op jit(solution)/shard_map/ppermute | solution.py:19
  121.6 11.0 %collective-permute-start.14 = (bf16[128,640]{1,0:T(8,128)(2,1)S(1)}, bf16[128,640]{1,0:T(8,128)(2,1)S(1)}, u32[]{:S(2)}, u32[]{:S(2)}) collective-permute-start(bf16[128,640]{1,0:T(8,128)(2,1)S(1)} %collective-permute-done.13.refs_1_), channel_id=1, source_target_pairs={{0,2},{2,4},{4,6},{6,8},{8,10},{10,12},{12,14},{14,0},{1,3},{3,5},... | collective-permute-start | bytes 491528 | tf_op jit(solution)/shard_map/ppermute | solution.py:19
  123.6 11.0 %collective-permute-start.18 = (bf16[128,640]{1,0:T(8,128)(2,1)S(1)}, bf16[128,640]{1,0:T(8,128)(2,1)S(1)}, u32[]{:S(2)}, u32[]{:S(2)}) collective-permute-start(bf16[128,640]{1,0:T(8,128)(2,1)S(1)} %collective-permute-done.17.refs_5_), channel_id=1, source_target_pairs={{0,14},{2,0},{4,2},{6,4},{8,6},{10,8},{12,10},{14,12},{1,15},{3,1}... | collective-permute-start | bytes 491528 | tf_op jit(solution)/shard_map/ppermute | solution.py:19
  132.6 7.3 %collective-permute-start.15 = (bf16[128,640]{1,0:T(8,128)(2,1)S(1)}, bf16[128,640]{1,0:T(8,128)(2,1)S(1)}, u32[]{:S(2)}, u32[]{:S(2)}) collective-permute-start(bf16[128,640]{1,0:T(8,128)(2,1)S(1)} %collective-permute-done.14.refs_2_), channel_id=1, source_target_pairs={{0,2},{2,4},{4,6},{6,8},{8,10},{10,12},{12,14},{14,0},{1,3},{3,5},... | collective-permute-start | bytes 491528 | tf_op jit(solution)/shard_map/ppermute | solution.py:19
  134.5 8.1 %collective-permute-start.19 = (bf16[128,640]{1,0:T(8,128)(2,1)S(1)}, bf16[128,640]{1,0:T(8,128)(2,1)S(1)}, u32[]{:S(2)}, u32[]{:S(2)}) collective-permute-start(bf16[128,640]{1,0:T(8,128)(2,1)S(1)} %collective-permute-done.18.refs_6_), channel_id=1, source_target_pairs={{0,14},{2,0},{4,2},{6,4},{8,6},{10,8},{12,10},{14,12},{1,15},{3,1}... | collective-permute-start | bytes 491528 | tf_op jit(solution)/shard_map/ppermute | solution.py:19
  139.9 7.3 %collective-permute-start.16 = (bf16[128,640]{1,0:T(8,128)(2,1)S(1)}, bf16[128,640]{1,0:T(8,128)(2,1)S(1)}, u32[]{:S(2)}, u32[]{:S(2)}) collective-permute-start(bf16[128,640]{1,0:T(8,128)(2,1)S(1)} %collective-permute-done.15.refs_3_), channel_id=1, source_target_pairs={{0,2},{2,4},{4,6},{6,8},{8,10},{10,12},{12,14},{14,0},{1,3},{3,5},... | collective-permute-start | bytes 491528 | tf_op jit(solution)/shard_map/ppermute | solution.py:19
  141.8 0.7 copy-start.5
  142.6 0.7 copy-start.7
  147.1 0.7 copy-start.9
  147.8 1.3 copy-start.1
  149.1 0.9 copy-start.6
  150.0 0.9 copy-start.8
  151.0 0.9 copy-start.10
  162.3 7.2 %collective-permute-start.21 = (bf16[256,256]{1,0:T(8,128)(2,1)S(1)}, bf16[256,256]{1,0:T(8,128)(2,1)S(1)}, u32[]{:S(2)}, u32[]{:S(2)}) collective-permute-start(bf16[256,256]{1,0:T(8,128)(2,1)S(1)} %get-tuple-element.10), channel_id=1, source_target_pairs={{0,1},{1,0},{2,3},{3,2},{4,5},{5,4},{6,7},{7,6},{8,9},{9,8},{10,11... | collective-permute-start | bytes 393224 | tf_op jit(solution)/shard_map/ppermute | solution.py:19
Sparse Core Ops, SparseCore 0:
  28.8 45.1 all-gather.4
  94.6 39.4 all-gather.6

commit v2 on v0

v2 whole, which is shorter than its diff:
```python
import jax
import jax.numpy as jnp
from jax import lax
from jax.experimental import pallas as pl
from jax.experimental.pallas import tpu as pltpu
from jax.sharding import Mesh, PartitionSpec as P

BF = jnp.bfloat16
F32 = jnp.float32
KP, C, HID = 1176, 1280, 5120
NX, NZ, NY = 4, 4, 8
PART = 320
TOK = 256
ORDER = (0, -1, -2, -3, -4, 1, 2, 3)


def shift(v, axis, n, by):
    return lax.ppermute(v, axis, [(i, (i + by) % n) for i in range(n)])


def shift_cores(v, by):
    def at(z, c):
        z = z % 8
        return ((z % 4) * 2 + z // 4) * 2 + c

    pairs = [(at(z, c), at(z + (by if c else -by), c)) for z in range(8) for c in range(2)]
    return lax.ppermute(v, ("zl", "zh", "c"), pairs)


def embed_kernel(px, *refs):
    w_here, w_near, w_near_o, w_two, w_two_o, p_own, p_oth, gain, beta, b_own, b_oth = refs[:11]
    out, xs, ws, ps, es, gs, bs, os, ts, sems = refs[11:]
    zl, core = lax.axis_index("zl"), lax.axis_index("c")
    loads = []

    def load(src, dst):
        loads.append(pltpu.make_async_copy(src, dst, sems.at[len(loads)]))
        loads[-1].start()

    half = NY // 2
    load(px.at[pl.ds(0, half)], xs.at[pl.ds(0, half)])
    load(w_here, ws.at[:, zl])
    load(w_near, ws.at[:, lax.rem(zl + 1 + 2 * core, NZ)])
    load(w_near_o, ws.at[:, lax.rem(zl + 3 - 2 * core, NZ)])
    load(w_two, ws.at[pl.ds(2 * core, 2), lax.rem(zl + 2, NZ)])
    load(w_two_o, ws.at[pl.ds(2 - 2 * core, 2), lax.rem(zl + 2, NZ)])
    now = len(loads)
    load(px.at[pl.ds(half, half)], xs.at[pl.ds(half, half)])
    load(p_own, ps.at[core])
    load(p_oth, ps.at[1 - core])
    for src, dst in ((gain, gs), (beta, bs), (b_own, os), (b_oth, ts)):
        load(src, dst)
    for c in loads[:now]:
        c.wait()
    w = ws[...].reshape(C, KP)
    dims = (((1,), (1,)), ((), ()))
    for part in range(2):
        if part == 1:
            loads[now].wait()
        ys = slice(part * half, (part + 1) * half)
        for ij in (0, 2):
            patches = [xs[ys, :, ij + n].reshape(TOK // 2, KP) for n in range(2)]
            patches = jnp.concatenate(patches, axis=0)
            e = lax.dot_general(patches, w, dims, preferred_element_type=F32)
            es[ij, part] = e[: TOK // 2]
            es[ij + 1, part] = e[TOK // 2 :]
    for c in loads[now + 1 :]:
        c.wait()
    g = gs[...].reshape(1, C)
    b = bs[...].reshape(1, C)
    p = ps[...].reshape(PART, HID)
    pre = None
    for ij in range(4):
        e = es[ij].reshape(TOK, C)
        mean = jnp.sum(e, axis=-1, keepdims=True) * (1.0 / C)
        cen = e - mean
        var = jnp.sum(cen * cen, axis=-1, keepdims=True) * (1.0 / C)
        normed = (cen * lax.rsqrt(var + 1e-06) * g + b).astype(BF)
        part = lax.dot_general(
            normed, p[:, ij * C : (ij + 1) * C], dims, preferred_element_type=F32
        )
        pre = part if ij == 0 else pre + part
    bias = [r[...].reshape(1, -1)[:, : PART // 2] for r in (os, ts)]
    bias = [jnp.where(core == n, bias[0], bias[1]) for n in range(2)]
    pre += jnp.concatenate(bias, axis=1)
    h = 0.5 * pre * (1.0 + lax.erf(pre * (0.5**0.5)))
    for y in range(NY):
        top = h[y * 32 : y * 32 + 16]
        low = h[y * 32 + 16 : y * 32 + 32]
        row = [top[:, :256], top[:, 256:], low[:, 256:], low[:, :256]]
        out[y] = jnp.concatenate(row, axis=1).astype(BF)


def embed_hidden(px, w, p_own, p_oth, gain, beta, b_own, b_oth):
    vmem = pl.BlockSpec(memory_space=pltpu.VMEM)
    any_ = pl.BlockSpec(memory_space=pl.ANY)
    out = pl.pallas_call(
        embed_kernel,
        out_shape=jax.ShapeDtypeStruct((NY, 16, 2 * PART), BF),
        in_specs=[any_] * 12,
        out_specs=vmem,
        scratch_shapes=[
            pltpu.VMEM((NY, 2, 4, 16, KP), BF),
            pltpu.VMEM((NX, NZ, 80, KP), BF),
            pltpu.VMEM((2, PART // 2, HID), BF),
            pltpu.VMEM((4, 2, TOK // 2, C), F32),
            pltpu.VMEM((C,), F32),
            pltpu.VMEM((C,), F32),
            pltpu.VMEM((160 + 256,), F32),
            pltpu.VMEM((160 + 256,), F32),
            pltpu.SemaphoreType.DMA((13,)),
        ],
        compiler_params=pltpu.CompilerParams(vmem_limit_bytes=56 << 20),
        cost_estimate=pl.CostEstimate(
            flops=2 * (1024 * KP * C + TOK * HID * PART), bytes_accessed=9 << 20, transcendentals=0
        ),
        name="embed_hidden",
    )(px, *w, p_own, p_oth, gain, beta, b_own, b_oth)
    return out.reshape(TOK // 2, 2 * PART)


def out_kernel(*refs):
    hs = refs[:NY]
    p_own, p_oth, b_own, b_oth, o_own, o_oth, hv, acc, bs, sems = refs[NY:]
    loads = [pltpu.make_async_copy(b, bs.at[n], sems.at[n]) for n, b in enumerate((b_own, b_oth))]
    for c in loads:
        c.start()
    y = lax.axis_index("y")
    for n, d in enumerate(ORDER):
        hv[lax.rem(y + (d + NY), NY)] = hs[n][...]
    lane = lax.broadcasted_iota(jnp.int32, (TOK // 2, 128), 1)
    for zh in range(2):
        for n in range(NY):
            row = (zh * NY + n) * PART
            h = hv[n, zh]
            both = jnp.concatenate([h[:, :256], h[:, 384:]], axis=0)
            mid = h[:, 256:384]
            low = jnp.where(lane >= 64, mid.astype(F32), 0.0).astype(BF)
            for k, p in enumerate((p_own, p_oth)):
                part = jnp.dot(both, p[row : row + 256, :], preferred_element_type=F32)
                rest = [
                    jnp.dot(mid[:, :64], p[row + 256 : row + 320, :], preferred_element_type=F32),
                    jnp.dot(low, p[row + 192 : row + 320, :], preferred_element_type=F32),
                ]
                part = part + jnp.concatenate(rest, axis=0)
                if row == 0:
                    acc[k] = part
                else:
                    acc[k] += part
    for k, o in enumerate((o_own, o_oth)):
        loads[k].wait()
        bias = bs[k : k + 1, PART // 2 :]
        o[...] = (acc[k] + bias).astype(BF)


def project_out(hs, p_own, p_oth, b_own, b_oth):
    any_ = pl.BlockSpec(memory_space=pl.ANY)
    vmem = pl.BlockSpec(memory_space=pltpu.VMEM)
    return pl.pallas_call(
        out_kernel,
        out_shape=[jax.ShapeDtypeStruct((TOK, 256), BF)] * 2,
        in_specs=[vmem] * 10 + [any_] * 2,
        out_specs=[vmem] * 2,
        scratch_shapes=[
            pltpu.VMEM((NY, 2, TOK // 2, 2 * PART), BF),
            pltpu.VMEM((2, TOK, 256), F32),
            pltpu.VMEM((2, 160 + 256), F32),
            pltpu.SemaphoreType.DMA((2,)),
        ],
        compiler_params=pltpu.CompilerParams(vmem_limit_bytes=12 << 20),
        cost_estimate=pl.CostEstimate(
            flops=2 * TOK * HID * 512, bytes_accessed=1 << 20, transcendentals=0
        ),
        name="project_out",
    )(*hs, p_own, p_oth, b_own, b_oth)


def ring(v):
    right, left = [v], [v]
    for step in range(4):
        right.append(shift(right[-1], "y", NY, 1))
        if step < 3:
            left.append(shift(left[-1], "y", NY, -1))
    return right + left[1:]


def per_device(pixels, conv_weight, norm_gain, norm_bias, proj_in, bias_in, proj_out, bias_out):
    core = lax.axis_index("c")
    first = core == 0

    rows = lax.all_gather(pixels.reshape(2, 32, KP), ("zh", "c"), axis=0).reshape(2, 2, 2, 32, KP)
    rows = jnp.where(first, rows[:, :, 0], rows[:, :, 1])
    half = rows.reshape(2, 2, 16, 2, KP).transpose(0, 1, 3, 2, 4).reshape(2, 4, 16, KP)
    px = lax.all_gather(half, "y", axis=0)

    wt, _ = lax.optimization_barrier((conv_weight.T, half))
    wx = lax.all_gather(wt, "x", axis=0)

    near = shift_cores(wx, 1)
    part = jnp.where(first, wx[: NX // 2], wx[NX // 2 :])
    two = shift_cores(part, 2)
    near, two = lax.optimization_barrier((near, two))
    near_o = shift(near, "c", 2, 1)
    two_o = shift(two, "c", 2, 1)

    bias = jnp.concatenate([bias_in, bias_out])
    p_in, p_out, bias, _ = lax.optimization_barrier((proj_in.T, proj_out, bias, part))
    p_in_o, p_out_o, bias_o = [shift(v, "c", 2, 1) for v in (p_in, p_out, bias)]
    hid = embed_hidden(
        px,
        (wx, near, near_o, two, two_o),
        p_in,
        p_in_o,
        norm_gain,
        norm_bias,
        bias,
        bias_o,
    )
    hs = ring(lax.all_gather(hid, "zh", axis=0))
    o_own, o_oth = project_out(hs, p_out, p_out_o, bias, bias_o)
    o_got = shift(o_oth, "c", 2, 1)
    result = jnp.stack([jnp.where(first, o_own, o_got), jnp.where(first, o_got, o_own)])
    return result.reshape(2, 16, 16, 256)


def solution(mesh):
    fine = Mesh(mesh.devices.reshape(NX, NZ, 2, NY, 2), ("x", "zl", "zh", "y", "c"))
    tm, tp = ("x", "zl"), ("zh", "y", "c")
    return jax.shard_map(
        per_device,
        mesh=fine,
        in_specs=(
            P(tm, tp, None, None),
            P(None, tm),
            P(),
            P(),
            P(None, tp),
            P(tp),
            P(None, tp),
            P(tp),
        ),
        out_specs=P(tm, None, None, tp),
        check_vma=False,
    )
```

time: 373 us -> 164 us (0.44)
  the two profiles are of different devices: /device:TPU:1 before, /device:TPU:135 now
where the time goes in v2:
time: 164 us; the launch traced here: 163 us
  starting transfers between devices  53.3 us (32%)
  blocking collectives  44.3 us (27%)
  waiting for transfers between devices  32.8 us (20%)
  Pallas kernels  13.7 us (8%)
  between operations  13.7 us (8%)
  local copies, waits for them, and re-layouts  3.86 us (2%)
    ppermute x13, starting transfers between devices, shift(): return lax.ppermute(v, axis, [(i, (i + by) % n) for i in range(n)])  46 us
    ppermute x13, waiting for transfers between devices, shift(): return lax.ppermute(v, axis, [(i, (i + by) % n) for i in range(n)])  23.2 us
    all_gather x1, blocking collectives, per_device(): lax.all_gather(pixels.reshape(2, 32, KP), ('zh', 'c'), axis=0)  17.9 us
    all_gather x1, blocking collectives, per_device(): hs = ring(lax.all_gather(hid, 'zh', axis=0))  14.3 us
    all_gather x1, blocking collectives, per_device(): wx = lax.all_gather(wt, 'x', axis=0)  12 us
    ppermute x2, waiting for transfers between devices, shift_cores(): return lax.ppermute(v, ('zl', 'zh', 'c'), pairs)  9.5 us
    pallas_call x1, Pallas kernels, embed_hidden(): pl.pallas_call(embed_kernel, out_shape=jax.ShapeDtypeStruct((NY, 16, 2 *...  9.21 us
    ppermute x2, starting transfers between devices, shift_cores(): return lax.ppermute(v, ('zl', 'zh', 'c'), pairs)  7.26 us
  transfers between devices with their start and end apart: 16, of which 7 were waited for; matrix products, arithmetic and copies ran while one was open for 0% of the time, Pallas kernels for 6%

profile of v2, /device:TPU:135, one launch (start us, length us, event | category | flops | bytes accessed | tf_op | source)
XLA Modules:
  0.0 162.9 jit_solution(12572787663492052405)
XLA Ops:
  6.5 0.0 copy-start.6
  6.5 0.0 copy-start.7
  6.5 0.0 all-gather.4.cloned.1.call-start
  6.5 17.9 %all-gather = bf16[8,1,32,1176]{3,2,1,0:T(8,128)(2,1)S(1)} all-gather(bf16[2,1,32,1176]{3,2,1,0:T(8,128)(2,1)} %param.8), channel_id=2, replica_groups=mesh['x'=4,'zl'=4,'zh'=2,'y'=8,'c'=2] {'zh','c'}, dimensions={0}, use_global_device_ids=true | all-gather | bytes 752640 | tf_op jit(solution)/shard_map/all_gather | solution.py:191
  24.5 0.0 copy-start
  24.5 0.6 broadcast_select_fusion
  25.1 0.8 copy.16
  25.9 0.0 all-gather.4.cloned.1.call-update
  25.9 0.0 copy-done.6
  25.9 0.0 copy-done.7
  25.9 0.1 pad_maximum_fusion.1.refs_9_.refs_10_
  26.0 0.0 copy-start.1
  26.0 12.0 %all-gather.1 = bf16[320,1176]{1,0:T(8,128)(2,1)S(1)} all-gather(bf16[80,1176]{1,0:T(8,128)(2,1)} %bitcast.20), channel_id=3, replica_groups=mesh['x'=4,'zl'=4,'zh'=2,'y'=8,'c'=2] {'x'}, dimensions={0}, use_global_device_ids=true | all-gather | bytes 940800 | tf_op jit(solution)/shard_map/all_gather | solution.py:197
  38.0 0.0 copy-start.5
  38.1 4.8 %collective-permute-start.4 = (bf16[160,5120]{1,0:T(8,128)(2,1)}, bf16[160,5120]{1,0:T(8,128)(2,1)}, u32[]{:S(2)}, u32[]{:S(2)}) collective-permute-start(bf16[160,5120]{1,0:T(8,128)(2,1)} %bitcast.22), channel_id=1, source_target_pairs={{0,1},{1,0},{2,3},{3,2},{4,5},{5,4},{6,7},{7,6},{8,9},{9,8},{10,11... | collective-permute-start | bytes 4915208 | tf_op jit(solution)/shard_map/ppermute | solution.py:18
  42.9 2.0 %collective-permute-start = (bf16[4,80,1176]{2,1,0:T(8,128)(2,1)S(1)}, bf16[4,80,1176]{2,1,0:T(8,128)(2,1)S(1)}, u32[]{:S(2)}, u32[]{:S(2)}) collective-permute-start(bf16[4,80,1176]{2,1,0:T(8,128)(2,1)S(1)} %bitcast.12), channel_id=1, source_target_pairs={{0,112},{1,33},{32,0},{33,65},{64,32},{65,97},{96,64},{97,17},{16,... | collective-permute-start | bytes 2257928 | tf_op jit(solution)/shard_map/ppermute | solution.py:27
  44.9 5.2 %collective-permute-start.1 = (bf16[2,80,1176]{2,1,0:T(8,128)(2,1)S(1)}, bf16[2,80,1176]{2,1,0:T(8,128)(2,1)S(1)}, u32[]{:S(2)}, u32[]{:S(2)}) collective-permute-start(bf16[2,80,1176]{2,1,0:T(8,128)(2,1)S(1)} %bitcast.19), channel_id=1, source_target_pairs={{0,80},{1,65},{32,112},{33,97},{64,0},{65,17},{96,32},{97,49},{16,... | collective-permute-start | bytes 1128968 | tf_op jit(solution)/shard_map/ppermute | solution.py:27
  50.2 0.0 copy-done
  50.2 2.7 %collective-permute-start.13 = (bf16[5120,256]{1,0:T(8,128)(2,1)S(1)}, bf16[5120,256]{1,0:T(8,128)(2,1)}, u32[]{:S(2)}, u32[]{:S(2)}) collective-permute-start(bf16[5120,256]{1,0:T(8,128)(2,1)S(1)} %copy-done), channel_id=1, source_target_pairs={{0,1},{1,0},{2,3},{3,2},{4,5},{5,4},{6,7},{7,6},{8,9},{9,8},{10,11... | collective-permute-start | bytes 7864328 | tf_op jit(solution)/shard_map/ppermute | solution.py:18
  52.9 9.5 %collective-permute-done.1.refs_3_ = bf16[2,80,1176]{2,1,0:T(8,128)(2,1)S(1)} collective-permute-done((bf16[2,80,1176]{2,1,0:T(8,128)(2,1)S(1)}, bf16[2,80,1176]{2,1,0:T(8,128)(2,1)S(1)}, u32[]{:S(2)}, u32[]{:S(2)}) %collective-permute-start.1) | collective-permute-done | bytes 376352 | tf_op jit(solution)/shard_map/ppermute | solution.py:27
  62.4 0.0 copy-start.10
  62.4 0.0 collective-permute-done.refs_1_
  62.4 0.0 copy-start.8
  62.4 6.5 %collective-permute-start.2 = (bf16[4,80,1176]{2,1,0:T(8,128)(2,1)S(1)}, bf16[4,80,1176]{2,1,0:T(8,128)(2,1)S(1)}, u32[]{:S(2)}, u32[]{:S(2)}) collective-permute-start(bf16[4,80,1176]{2,1,0:T(8,128)(2,1)S(1)} %collective-permute-done.refs_1_), channel_id=1, source_target_pairs={{0,1},{1,0},{2,3},{3,2},{4,5},{5,4},{6,7},{7,6},{8,9},{9,8},{10,11... | collective-permute-start | bytes 2257928 | tf_op jit(solution)/shard_map/ppermute | solution.py:18
  68.9 1.9 %collective-permute-start.3 = (bf16[2,80,1176]{2,1,0:T(8,128)(2,1)S(1)}, bf16[2,80,1176]{2,1,0:T(8,128)(2,1)S(1)}, u32[]{:S(2)}, u32[]{:S(2)}) collective-permute-start(bf16[2,80,1176]{2,1,0:T(8,128)(2,1)S(1)} %collective-permute-done.1.refs_3_), channel_id=1, source_target_pairs={{0,1},{1,0},{2,3},{3,2},{4,5},{5,4},{6,7},{7,6},{8,9},{9,8},{10,11... | collective-permute-start | bytes 1128968 | tf_op jit(solution)/shard_map/ppermute | solution.py:18
  70.8 2.4 %collective-permute-start.5 = (f32[416]{0:T(512)S(1)}, f32[416]{0:T(512)S(1)}, u32[]{:S(2)}, u32[]{:S(2)}) collective-permute-start(f32[416]{0:T(512)S(1)} %pad_maximum_fusion.1.refs_9_.refs_10_), channel_id=1, source_target_pairs={{0,1},{1,0},{2,3},{3,2},{4,5},{5,4},{6,7},{7,6},{8,9},{9,8},{10,11... | collective-permute-start | bytes 5000 | tf_op jit(solution)/shard_map/ppermute | solution.py:18
  73.2 0.8 collective-permute-done.5.refs_10_.refs_11_
  74.0 0.0 copy-done.8
  74.0 0.0 copy-start.3
  74.0 0.0 collective-permute-done.3.refs_4_
  74.1 0.0 copy-start.11
  74.1 0.0 collective-permute-done.2.refs_2_
  74.1 0.0 copy-done.10
  74.1 0.7 copy-done.11
  74.8 0.0 copy-start.9
  74.8 1.0 copy-done.9
  75.8 0.0 collective-permute-done.4.refs_6_
  75.8 0.0 all-gather.4.cloned.1.call-done.px
  75.8 0.0 copy-done.1
  75.8 0.0 copy-done.5
  75.8 0.0 copy-done.3
  75.8 9.2 %embed_hidden.1 = bf16[8,16,640]{2,1,0:T(8,128)(2,1)} custom-call(bf16[8,2,4,16,1176]{4,3,2,1,0:T(8,128)(2,1)} %all-gather.4.cloned.1.call-done.px, bf16[4,80,1176]{2,1,0:T(8,128)(2,1)} %bitcast.13, bf16[4,80,1176]{2,1,0:T(8,128)(2,1)} %copy-done.8, bf16[4,80,1176]{2,1,0:T(8,128)(2,1)} %copy-done.9, bf16[2,80,1176]{2,1,0:T(8,128)(2,1)} %copy-done.10, ...), custom_call_target="tpu_custom_call" | custom-call | flops 3921674240 | bytes 9437184 | tf_op jit(solution)/shard_map/embed_hidden/pallas_call | solution.py:97
  85.0 14.3 %all_gather.19.refs_0_ = bf16[2,128,640]{2,1,0:T(8,128)(2,1)S(1)} all-gather(bf16[1,128,640]{2,1,0:T(8,128)(2,1)} %bitcast.21), channel_id=1, replica_groups=mesh['x'=4,'zl'=4,'zh'=2,'y'=8,'c'=2] {'zh'}, dimensions={0}, use_global_device_ids=true | all-gather | bytes 491520 | tf_op jit(solution)/shard_map/all_gather | solution.py:219
  99.4 3.2 %collective-permute-start.6 = (bf16[2,128,640]{2,1,0:T(8,128)(2,1)S(1)}, bf16[2,128,640]{2,1,0:T(8,128)(2,1)S(1)}, u32[]{:S(2)}, u32[]{:S(2)}) collective-permute-start(bf16[2,128,640]{2,1,0:T(8,128)(2,1)S(1)} %all_gather.19.refs_0_), channel_id=1, source_target_pairs={{0,2},{2,4},{4,6},{6,8},{8,10},{10,12},{12,14},{14,0},{1,3},{3,5},... | collective-permute-start | bytes 983048 | tf_op jit(solution)/shard_map/ppermute | solution.py:18
  102.6 3.8 %collective-permute-start.10 = (bf16[2,128,640]{2,1,0:T(8,128)(2,1)S(1)}, bf16[2,128,640]{2,1,0:T(8,128)(2,1)S(1)}, u32[]{:S(2)}, u32[]{:S(2)}) collective-permute-start(bf16[2,128,640]{2,1,0:T(8,128)(2,1)S(1)} %all_gather.19.refs_0_), channel_id=1, source_target_pairs={{0,14},{2,0},{4,2},{6,4},{8,6},{10,8},{12,10},{14,12},{1,15},{3,1}... | collective-permute-start | bytes 983048 | tf_op jit(solution)/shard_map/ppermute | solution.py:18
  106.4 5.6 %collective-permute-done.6.refs_1_ = bf16[2,128,640]{2,1,0:T(8,128)(2,1)S(1)} collective-permute-done((bf16[2,128,640]{2,1,0:T(8,128)(2,1)S(1)}, bf16[2,128,640]{2,1,0:T(8,128)(2,1)S(1)}, u32[]{:S(2)}, u32[]{:S(2)}) %collective-permute-start.6) | collective-permute-done | bytes 327712 | tf_op jit(solution)/shard_map/ppermute | solution.py:18
  112.0 1.9 %collective-permute-start.7 = (bf16[2,128,640]{2,1,0:T(8,128)(2,1)S(1)}, bf16[2,128,640]{2,1,0:T(8,128)(2,1)S(1)}, u32[]{:S(2)}, u32[]{:S(2)}) collective-permute-start(bf16[2,128,640]{2,1,0:T(8,128)(2,1)S(1)} %collective-permute-done.6.refs_1_), channel_id=1, source_target_pairs={{0,2},{2,4},{4,6},{6,8},{8,10},{10,12},{12,14},{14,0},{1,3},{3,5},... | collective-permute-start | bytes 983048 | tf_op jit(solution)/shard_map/ppermute | solution.py:18
  113.9 0.0 collective-permute-done.10.refs_5_
  113.9 4.6 %collective-permute-start.11 = (bf16[2,128,640]{2,1,0:T(8,128)(2,1)S(1)}, bf16[2,128,640]{2,1,0:T(8,128)(2,1)S(1)}, u32[]{:S(2)}, u32[]{:S(2)}) collective-permute-start(bf16[2,128,640]{2,1,0:T(8,128)(2,1)S(1)} %collective-permute-done.10.refs_5_), channel_id=1, source_target_pairs={{0,14},{2,0},{4,2},{6,4},{8,6},{10,8},{12,10},{14,12},{1,15},{3,1}... | collective-permute-start | bytes 983048 | tf_op jit(solution)/shard_map/ppermute | solution.py:18
  118.5 4.7 %collective-permute-done.7.refs_2_ = bf16[2,128,640]{2,1,0:T(8,128)(2,1)S(1)} collective-permute-done((bf16[2,128,640]{2,1,0:T(8,128)(2,1)S(1)}, bf16[2,128,640]{2,1,0:T(8,128)(2,1)S(1)}, u32[]{:S(2)}, u32[]{:S(2)}) %collective-permute-start.7) | collective-permute-done | bytes 327712 | tf_op jit(solution)/shard_map/ppermute | solution.py:18
  123.2 1.9 %collective-permute-start.8 = (bf16[2,128,640]{2,1,0:T(8,128)(2,1)S(1)}, bf16[2,128,640]{2,1,0:T(8,128)(2,1)S(1)}, u32[]{:S(2)}, u32[]{:S(2)}) collective-permute-start(bf16[2,128,640]{2,1,0:T(8,128)(2,1)S(1)} %collective-permute-done.7.refs_2_), channel_id=1, source_target_pairs={{0,2},{2,4},{4,6},{6,8},{8,10},{10,12},{12,14},{14,0},{1,3},{3,5},... | collective-permute-start | bytes 983048 | tf_op jit(solution)/shard_map/ppermute | solution.py:18
  125.1 0.0 collective-permute-done.11.refs_6_
  125.1 4.6 %collective-permute-start.12 = (bf16[2,128,640]{2,1,0:T(8,128)(2,1)S(1)}, bf16[2,128,640]{2,1,0:T(8,128)(2,1)S(1)}, u32[]{:S(2)}, u32[]{:S(2)}) collective-permute-start(bf16[2,128,640]{2,1,0:T(8,128)(2,1)S(1)} %collective-permute-done.11.refs_6_), channel_id=1, source_target_pairs={{0,14},{2,0},{4,2},{6,4},{8,6},{10,8},{12,10},{14,12},{1,15},{3,1}... | collective-permute-start | bytes 983048 | tf_op jit(solution)/shard_map/ppermute | solution.py:18
  129.7 3.8 %collective-permute-done.8.refs_3_ = bf16[2,128,640]{2,1,0:T(8,128)(2,1)S(1)} collective-permute-done((bf16[2,128,640]{2,1,0:T(8,128)(2,1)S(1)}, bf16[2,128,640]{2,1,0:T(8,128)(2,1)S(1)}, u32[]{:S(2)}, u32[]{:S(2)}) %collective-permute-start.8) | collective-permute-done | bytes 327712 | tf_op jit(solution)/shard_map/ppermute | solution.py:18
  133.5 1.9 %collective-permute-start.9 = (bf16[2,128,640]{2,1,0:T(8,128)(2,1)S(1)}, bf16[2,128,640]{2,1,0:T(8,128)(2,1)S(1)}, u32[]{:S(2)}, u32[]{:S(2)}) collective-permute-start(bf16[2,128,640]{2,1,0:T(8,128)(2,1)S(1)} %collective-permute-done.8.refs_3_), channel_id=1, source_target_pairs={{0,2},{2,4},{4,6},{6,8},{8,10},{10,12},{12,14},{14,0},{1,3},{3,5},... | collective-permute-start | bytes 983048 | tf_op jit(solution)/shard_map/ppermute | solution.py:18
  135.4 0.0 collective-permute-done.13.refs_9_
  135.4 0.0 collective-permute-done.12.refs_7_
  135.4 7.4 %collective-permute-done.9.refs_4_ = bf16[2,128,640]{2,1,0:T(8,128)(2,1)S(1)} collective-permute-done((bf16[2,128,640]{2,1,0:T(8,128)(2,1)S(1)}, bf16[2,128,640]{2,1,0:T(8,128)(2,1)S(1)}, u32[]{:S(2)}, u32[]{:S(2)}) %collective-permute-start.9) | collective-permute-done | bytes 327712 | tf_op jit(solution)/shard_map/ppermute | solution.py:18
  142.8 0.6 copy-done.2
  143.4 0.7 copy-done.4
  144.1 4.5 %project_out.1 = (bf16[256,256]{1,0:T(8,128)(2,1)S(1)}, bf16[256,256]{1,0:T(8,128)(2,1)S(1)}) custom-call(bf16[2,128,640]{2,1,0:T(8,128)(2,1)S(1)} %all_gather.19.refs_0_, bf16[2,128,640]{2,1,0:T(8,128)(2,1)S(1)} %collective-permute-done.6.refs_1_, bf16[2,128,640]{2,1,0:T(8,128)(2,1)S(1)} %collective-permute-done.7.refs_2_, ...), custom_call_target="tpu_custom_call" | custom-call | flops 1342177280 | bytes 1048576 | tf_op jit(solution)/shard_map/project_out/pallas_call | solution.py:159
  148.6 5.8 %collective-permute-start.14 = (bf16[256,256]{1,0:T(8,128)(2,1)S(1)}, bf16[256,256]{1,0:T(8,128)(2,1)S(1)}, u32[]{:S(2)}, u32[]{:S(2)}) collective-permute-start(bf16[256,256]{1,0:T(8,128)(2,1)S(1)} %get-tuple-element.18), channel_id=1, source_target_pairs={{0,1},{1,0},{2,3},{3,2},{4,5},{5,4},{6,7},{7,6},{8,9},{9,8},{10,11... | collective-permute-start | bytes 393224 | tf_op jit(solution)/shard_map/ppermute | solution.py:18
  154.4 1.0 collective-permute-done.14
  155.3 0.7 pad_maximum_fusion
  (5 shorter events, 0.1 us)
Async XLA Ops:
  6.5 19.4 %copy-start.6 = (f32[256]{0:T(256)S(1)}, f32[256]{0:T(256)}, u32[]{:S(2)}) copy-start(f32[256]{0:T(256)} %param.15) | copy-start | bytes 3076
  6.5 19.4 %copy-start.7 = (f32[160]{0:T(256)S(1)}, f32[160]{0:T(256)}, u32[]{:S(2)}) copy-start(f32[160]{0:T(256)} %param.13) | copy-start | bytes 1924
  6.5 69.2 %all-gather.4.cloned.1.call-start = ((), (), s32[]{:S(2)}) async-start(), calls=%async_computation | async-start | bytes 2949120 | tf_op jit(solution)/shard_map/all_gather | solution.py:194
  24.5 25.7 %copy-start = (bf16[5120,256]{1,0:T(8,128)(2,1)S(1)}, bf16[5120,256]{1,0:T(8,128)(2,1)}, u32[]{:S(2)}) copy-start(bf16[5120,256]{1,0:T(8,128)(2,1)} %refs_8_.2) | copy-start | bytes 7864324
  26.0 49.8 %copy-start.1 = (f32[416]{0:T(512)}, f32[416]{0:T(512)S(1)}, u32[]{:S(2)}) copy-start(f32[416]{0:T(512)S(1)} %pad_maximum_fusion.1.refs_9_.refs_10_) | copy-start | bytes 4996
  38.0 37.8 %copy-start.5 = (bf16[320,1176]{1,0:T(8,128)(2,1)}, bf16[320,1176]{1,0:T(8,128)(2,1)S(1)}, u32[]{:S(2)}) copy-start(bf16[320,1176]{1,0:T(8,128)(2,1)S(1)} %all-gather.1) | copy-start | bytes 2257924
  38.1 37.7 %collective-permute-start.4 = (bf16[160,5120]{1,0:T(8,128)(2,1)}, bf16[160,5120]{1,0:T(8,128)(2,1)}, u32[]{:S(2)}, u32[]{:S(2)}) collective-permute-start(bf16[160,5120]{1,0:T(8,128)(2,1)} %bitcast.22), channel_id=1, source_target_pairs={{0,1},{1,0},{2,3},{3,2},{4,5},{5,4},{6,7},{7,6},{8,9},{9,8},{10,11... | collective-permute-start | bytes 4915208 | tf_op jit(solution)/shard_map/ppermute | solution.py:18
  42.9 19.5 %collective-permute-start = (bf16[4,80,1176]{2,1,0:T(8,128)(2,1)S(1)}, bf16[4,80,1176]{2,1,0:T(8,128)(2,1)S(1)}, u32[]{:S(2)}, u32[]{:S(2)}) collective-permute-start(bf16[4,80,1176]{2,1,0:T(8,128)(2,1)S(1)} %bitcast.12), channel_id=1, source_target_pairs={{0,112},{1,33},{32,0},{33,65},{64,32},{65,97},{96,64},{97,17},{16,... | collective-permute-start | bytes 2257928 | tf_op jit(solution)/shard_map/ppermute | solution.py:27
  44.9 17.4 %collective-permute-start.1 = (bf16[2,80,1176]{2,1,0:T(8,128)(2,1)S(1)}, bf16[2,80,1176]{2,1,0:T(8,128)(2,1)S(1)}, u32[]{:S(2)}, u32[]{:S(2)}) collective-permute-start(bf16[2,80,1176]{2,1,0:T(8,128)(2,1)S(1)} %bitcast.19), channel_id=1, source_target_pairs={{0,80},{1,65},{32,112},{33,97},{64,0},{65,17},{96,32},{97,49},{16,... | collective-permute-start | bytes 1128968 | tf_op jit(solution)/shard_map/ppermute | solution.py:27
  50.2 85.2 %collective-permute-start.13 = (bf16[5120,256]{1,0:T(8,128)(2,1)S(1)}, bf16[5120,256]{1,0:T(8,128)(2,1)}, u32[]{:S(2)}, u32[]{:S(2)}) collective-permute-start(bf16[5120,256]{1,0:T(8,128)(2,1)S(1)} %copy-done), channel_id=1, source_target_pairs={{0,1},{1,0},{2,3},{3,2},{4,5},{5,4},{6,7},{7,6},{8,9},{9,8},{10,11... | collective-permute-start | bytes 7864328 | tf_op jit(solution)/shard_map/ppermute | solution.py:18
  62.4 11.7 %copy-start.10 = (bf16[2,80,1176]{2,1,0:T(8,128)(2,1)}, bf16[2,80,1176]{2,1,0:T(8,128)(2,1)S(1)}, u32[]{:S(2)}) copy-start(bf16[2,80,1176]{2,1,0:T(8,128)(2,1)S(1)} %collective-permute-done.1.refs_3_) | copy-start | bytes 1128964
  62.4 11.7 %copy-start.8 = (bf16[4,80,1176]{2,1,0:T(8,128)(2,1)}, bf16[4,80,1176]{2,1,0:T(8,128)(2,1)S(1)}, u32[]{:S(2)}) copy-start(bf16[4,80,1176]{2,1,0:T(8,128)(2,1)S(1)} %collective-permute-done.refs_1_) | copy-start | bytes 2257924
  62.4 11.7 %collective-permute-start.2 = (bf16[4,80,1176]{2,1,0:T(8,128)(2,1)S(1)}, bf16[4,80,1176]{2,1,0:T(8,128)(2,1)S(1)}, u32[]{:S(2)}, u32[]{:S(2)}) collective-permute-start(bf16[4,80,1176]{2,1,0:T(8,128)(2,1)S(1)} %collective-permute-done.refs_1_), channel_id=1, source_target_pairs={{0,1},{1,0},{2,3},{3,2},{4,5},{5,4},{6,7},{7,6},{8,9},{9,8},{10,11... | collective-permute-start | bytes 2257928 | tf_op jit(solution)/shard_map/ppermute | solution.py:18
  68.9 5.1 %collective-permute-start.3 = (bf16[2,80,1176]{2,1,0:T(8,128)(2,1)S(1)}, bf16[2,80,1176]{2,1,0:T(8,128)(2,1)S(1)}, u32[]{:S(2)}, u32[]{:S(2)}) collective-permute-start(bf16[2,80,1176]{2,1,0:T(8,128)(2,1)S(1)} %collective-permute-done.1.refs_3_), channel_id=1, source_target_pairs={{0,1},{1,0},{2,3},{3,2},{4,5},{5,4},{6,7},{7,6},{8,9},{9,8},{10,11... | collective-permute-start | bytes 1128968 | tf_op jit(solution)/shard_map/ppermute | solution.py:18
  70.8 3.2 %collective-permute-start.5 = (f32[416]{0:T(512)S(1)}, f32[416]{0:T(512)S(1)}, u32[]{:S(2)}, u32[]{:S(2)}) collective-permute-start(f32[416]{0:T(512)S(1)} %pad_maximum_fusion.1.refs_9_.refs_10_), channel_id=1, source_target_pairs={{0,1},{1,0},{2,3},{3,2},{4,5},{5,4},{6,7},{7,6},{8,9},{9,8},{10,11... | collective-permute-start | bytes 5000 | tf_op jit(solution)/shard_map/ppermute | solution.py:18
  74.0 1.8 %copy-start.3 = (f32[416]{0:T(512)}, f32[416]{0:T(512)S(1)}, u32[]{:S(2)}) copy-start(f32[416]{0:T(512)S(1)} %collective-permute-done.5.refs_10_.refs_11_) | copy-start | bytes 4996
  74.1 0.8 copy-start.11
  74.8 1.0 copy-start.9
  99.4 12.6 %collective-permute-start.6 = (bf16[2,128,640]{2,1,0:T(8,128)(2,1)S(1)}, bf16[2,128,640]{2,1,0:T(8,128)(2,1)S(1)}, u32[]{:S(2)}, u32[]{:S(2)}) collective-permute-start(bf16[2,128,640]{2,1,0:T(8,128)(2,1)S(1)} %all_gather.19.refs_0_), channel_id=1, source_target_pairs={{0,2},{2,4},{4,6},{6,8},{8,10},{10,12},{12,14},{14,0},{1,3},{3,5},... | collective-permute-start | bytes 983048 | tf_op jit(solution)/shard_map/ppermute | solution.py:18
  102.6 11.4 %collective-permute-start.10 = (bf16[2,128,640]{2,1,0:T(8,128)(2,1)S(1)}, bf16[2,128,640]{2,1,0:T(8,128)(2,1)S(1)}, u32[]{:S(2)}, u32[]{:S(2)}) collective-permute-start(bf16[2,128,640]{2,1,0:T(8,128)(2,1)S(1)} %all_gather.19.refs_0_), channel_id=1, source_target_pairs={{0,14},{2,0},{4,2},{6,4},{8,6},{10,8},{12,10},{14,12},{1,15},{3,1}... | collective-permute-start | bytes 983048 | tf_op jit(solution)/shard_map/ppermute | solution.py:18
  112.0 11.2 %collective-permute-start.7 = (bf16[2,128,640]{2,1,0:T(8,128)(2,1)S(1)}, bf16[2,128,640]{2,1,0:T(8,128)(2,1)S(1)}, u32[]{:S(2)}, u32[]{:S(2)}) collective-permute-start(bf16[2,128,640]{2,1,0:T(8,128)(2,1)S(1)} %collective-permute-done.6.refs_1_), channel_id=1, source_target_pairs={{0,2},{2,4},{4,6},{6,8},{8,10},{10,12},{12,14},{14,0},{1,3},{3,5},... | collective-permute-start | bytes 983048 | tf_op jit(solution)/shard_map/ppermute | solution.py:18
  113.9 11.2 %collective-permute-start.11 = (bf16[2,128,640]{2,1,0:T(8,128)(2,1)S(1)}, bf16[2,128,640]{2,1,0:T(8,128)(2,1)S(1)}, u32[]{:S(2)}, u32[]{:S(2)}) collective-permute-start(bf16[2,128,640]{2,1,0:T(8,128)(2,1)S(1)} %collective-permute-done.10.refs_5_), channel_id=1, source_target_pairs={{0,14},{2,0},{4,2},{6,4},{8,6},{10,8},{12,10},{14,12},{1,15},{3,1}... | collective-permute-start | bytes 983048 | tf_op jit(solution)/shard_map/ppermute | solution.py:18
  123.2 10.3 %collective-permute-start.8 = (bf16[2,128,640]{2,1,0:T(8,128)(2,1)S(1)}, bf16[2,128,640]{2,1,0:T(8,128)(2,1)S(1)}, u32[]{:S(2)}, u32[]{:S(2)}) collective-permute-start(bf16[2,128,640]{2,1,0:T(8,128)(2,1)S(1)} %collective-permute-done.7.refs_2_), channel_id=1, source_target_pairs={{0,2},{2,4},{4,6},{6,8},{8,10},{10,12},{12,14},{14,0},{1,3},{3,5},... | collective-permute-start | bytes 983048 | tf_op jit(solution)/shard_map/ppermute | solution.py:18
  125.1 10.3 %collective-permute-start.12 = (bf16[2,128,640]{2,1,0:T(8,128)(2,1)S(1)}, bf16[2,128,640]{2,1,0:T(8,128)(2,1)S(1)}, u32[]{:S(2)}, u32[]{:S(2)}) collective-permute-start(bf16[2,128,640]{2,1,0:T(8,128)(2,1)S(1)} %collective-permute-done.11.refs_6_), channel_id=1, source_target_pairs={{0,14},{2,0},{4,2},{6,4},{8,6},{10,8},{12,10},{14,12},{1,15},{3,1}... | collective-permute-start | bytes 983048 | tf_op jit(solution)/shard_map/ppermute | solution.py:18
  133.5 9.3 %collective-permute-start.9 = (bf16[2,128,640]{2,1,0:T(8,128)(2,1)S(1)}, bf16[2,128,640]{2,1,0:T(8,128)(2,1)S(1)}, u32[]{:S(2)}, u32[]{:S(2)}) collective-permute-start(bf16[2,128,640]{2,1,0:T(8,128)(2,1)S(1)} %collective-permute-done.8.refs_3_), channel_id=1, source_target_pairs={{0,2},{2,4},{4,6},{6,8},{8,10},{10,12},{12,14},{14,0},{1,3},{3,5},... | collective-permute-start | bytes 983048 | tf_op jit(solution)/shard_map/ppermute | solution.py:18
  142.8 0.6 copy-start.2
  143.4 0.7 copy-start.4
  148.6 6.8 %collective-permute-start.14 = (bf16[256,256]{1,0:T(8,128)(2,1)S(1)}, bf16[256,256]{1,0:T(8,128)(2,1)S(1)}, u32[]{:S(2)}, u32[]{:S(2)}) collective-permute-start(bf16[256,256]{1,0:T(8,128)(2,1)S(1)} %get-tuple-element.18), channel_id=1, source_target_pairs={{0,1},{1,0},{2,3},{3,2},{4,5},{5,4},{6,7},{7,6},{8,9},{9,8},{10,11... | collective-permute-start | bytes 393224 | tf_op jit(solution)/shard_map/ppermute | solution.py:18
Sparse Core Ops, SparseCore 0:
  26.0 42.2 all-gather.3

commit v3 on v2

--- a/solution.py
+++ b/solution.py
@@ -11,7 +11,7 @@
 NX, NZ, NY = 4, 4, 8
 PART = 320
 TOK = 256
-ORDER = (0, -1, -2, -3, -4, 1, 2, 3)
+ORDER = (0, -1, -2, -3, 1, 2, 3, -4)
 
 
 def shift(v, axis, n, by):
@@ -110,7 +110,7 @@
             pltpu.VMEM((160 + 256,), F32),
             pltpu.SemaphoreType.DMA((13,)),
         ],
-        compiler_params=pltpu.CompilerParams(vmem_limit_bytes=56 << 20),
+        compiler_params=pltpu.CompilerParams(vmem_limit_bytes=60 << 20),
         cost_estimate=pl.CostEstimate(
             flops=2 * (1024 * KP * C + TOK * HID * PART), bytes_accessed=9 << 20, transcendentals=0
         ),
@@ -119,60 +119,91 @@
     return out.reshape(TOK // 2, 2 * PART)
 
 
-def out_kernel(*refs):
-    hs = refs[:NY]
-    p_own, p_oth, b_own, b_oth, o_own, o_oth, hv, acc, bs, sems = refs[NY:]
+def hidden_dot(h, lane, w):
+    both = jnp.concatenate([h[:, :256], h[:, 384:]], axis=0)
+    mid = h[:, 256:384]
+    low = jnp.where(lane >= 64, mid.astype(F32), 0.0).astype(BF)
+    rest = [
+        jnp.dot(mid[:, :64], w(256, 320), preferred_element_type=F32),
+        jnp.dot(low, w(192, 320), preferred_element_type=F32),
+    ]
+    return jnp.dot(both, w(0, 256), preferred_element_type=F32) + jnp.concatenate(rest, axis=0)
+
+
+def most_kernel(*refs):
+    hs = refs[: NY - 1]
+    p_own, p_oth, b_own, b_oth, acc, far, hv, bs, sems = refs[NY - 1 :]
+    y = lax.axis_index("y")
     loads = [pltpu.make_async_copy(b, bs.at[n], sems.at[n]) for n, b in enumerate((b_own, b_oth))]
+    last = lax.rem(y + NY // 2, NY)
+    for k, p in enumerate((p_own, p_oth)):
+        for zh in range(2):
+            rows = pl.ds(pl.multiple_of((zh * NY + last) * PART, 64), PART)
+            loads.append(pltpu.make_async_copy(p.at[rows], far.at[k, zh], sems.at[2 + 2 * k + zh]))
     for c in loads:
         c.start()
-    y = lax.axis_index("y")
-    for n, d in enumerate(ORDER):
+    hv[last] = jnp.zeros_like(hs[0])
+    for n, d in enumerate(ORDER[:-1]):
         hv[lax.rem(y + (d + NY), NY)] = hs[n][...]
     lane = lax.broadcasted_iota(jnp.int32, (TOK // 2, 128), 1)
     for zh in range(2):
         for n in range(NY):
             row = (zh * NY + n) * PART
             h = hv[n, zh]
-            both = jnp.concatenate([h[:, :256], h[:, 384:]], axis=0)
-            mid = h[:, 256:384]
-            low = jnp.where(lane >= 64, mid.astype(F32), 0.0).astype(BF)
             for k, p in enumerate((p_own, p_oth)):
-                part = jnp.dot(both, p[row : row + 256, :], preferred_element_type=F32)
-                rest = [
-                    jnp.dot(mid[:, :64], p[row + 256 : row + 320, :], preferred_element_type=F32),
-                    jnp.dot(low, p[row + 192 : row + 320, :], preferred_element_type=F32),
-                ]
-                part = part + jnp.concatenate(rest, axis=0)
+                part = hidden_dot(h, lane, lambda a, b: p[row + a : row + b, :])
                 if row == 0:
                     acc[k] = part
                 else:
                     acc[k] += part
+    for c in loads:
+        c.wait()
+    for k in range(2):
+        acc[k] += bs[k : k + 1, PART // 2 :]
+
+
+def last_kernel(h, acc, far, o_own, o_oth):
+    lane = lax.broadcasted_iota(jnp.int32, (TOK // 2, 128), 1)
     for k, o in enumerate((o_own, o_oth)):
-        loads[k].wait()
-        bias = bs[k : k + 1, PART // 2 :]
-        o[...] = (acc[k] + bias).astype(BF)
+        total = acc[k]
+        for zh in range(2):
+            total += hidden_dot(h[zh], lane, lambda a, b: far[k, zh, a:b, :])
+        o[...] = total.astype(BF)
 
 
 def project_out(hs, p_own, p_oth, b_own, b_oth):
     any_ = pl.BlockSpec(memory_space=pl.ANY)
     vmem = pl.BlockSpec(memory_space=pltpu.VMEM)
-    return pl.pallas_call(
-        out_kernel,
-        out_shape=[jax.ShapeDtypeStruct((TOK, 256), BF)] * 2,
-        in_specs=[vmem] * 10 + [any_] * 2,
+    acc, far = pl.pallas_call(
+        most_kernel,
+        out_shape=[
+            jax.ShapeDtypeStruct((2, TOK, 256), F32),
+            jax.ShapeDtypeStruct((2, 2, PART, 256), BF),
+        ],
+        in_specs=[vmem] * 9 + [any_] * 2,
         out_specs=[vmem] * 2,
         scratch_shapes=[
             pltpu.VMEM((NY, 2, TOK // 2, 2 * PART), BF),
-            pltpu.VMEM((2, TOK, 256), F32),
             pltpu.VMEM((2, 160 + 256), F32),
-            pltpu.SemaphoreType.DMA((2,)),
+            pltpu.SemaphoreType.DMA((6,)),
         ],
         compiler_params=pltpu.CompilerParams(vmem_limit_bytes=12 << 20),
         cost_estimate=pl.CostEstimate(
             flops=2 * TOK * HID * 512, bytes_accessed=1 << 20, transcendentals=0
         ),
-        name="project_out",
-    )(*hs, p_own, p_oth, b_own, b_oth)
+        name="project_most",
+    )(*hs[:-1], p_own, p_oth, b_own, b_oth)
+    return pl.pallas_call(
+        last_kernel,
+        out_shape=[jax.ShapeDtypeStruct((TOK, 256), BF)] * 2,
+        in_specs=[vmem] * 3,
+        out_specs=[vmem] * 2,
+        compiler_params=pltpu.CompilerParams(vmem_limit_bytes=8 << 20),
+        cost_estimate=pl.CostEstimate(
+            flops=2 * TOK * 2 * PART * 512, bytes_accessed=1 << 18, transcendentals=0
+        ),
+        name="project_last",
+    )(hs[-1], acc, far)
 
 
 def ring(v):
@@ -181,7 +212,7 @@
         right.append(shift(right[-1], "y", NY, 1))
         if step < 3:
             left.append(shift(left[-1], "y", NY, -1))
-    return right + left[1:]
+    return right[:4] + left[1:] + right[4:]
 
 
 def per_device(pixels, conv_weight, norm_gain, norm_bias, proj_in, bias_in, proj_out, bias_out):
@@ -199,13 +230,12 @@
     near = shift_cores(wx, 1)
     part = jnp.where(first, wx[: NX // 2], wx[NX // 2 :])
     two = shift_cores(part, 2)
-    near, two = lax.optimization_barrier((near, two))
-    near_o = shift(near, "c", 2, 1)
-    two_o = shift(two, "c", 2, 1)
-
     bias = jnp.concatenate([bias_in, bias_out])
     p_in, p_out, bias, _ = lax.optimization_barrier((proj_in.T, proj_out, bias, part))
     p_in_o, p_out_o, bias_o = [shift(v, "c", 2, 1) for v in (p_in, p_out, bias)]
+    near, two, bias_o = lax.optimization_barrier((near, two, bias_o))
+    near_o = shift(near, "c", 2, 1)
+    two_o = shift(two, "c", 2, 1)
     hid = embed_hidden(
         px,
         (wx, near, near_o, two, two_o),
@@ -218,8 +248,8 @@
     )
     hs = ring(lax.all_gather(hid, "zh", axis=0))
     o_own, o_oth = project_out(hs, p_out, p_out_o, bias, bias_o)
-    o_got = shift(o_oth, "c", 2, 1)
-    result = jnp.stack([jnp.where(first, o_own, o_got), jnp.where(first, o_got, o_own)])
+    o_got = lax.all_gather(o_oth, "c", axis=0)
+    result = jnp.stack([jnp.where(first, o_own, o_got[0]), jnp.where(first, o_got[1], o_own)])
     return result.reshape(2, 16, 16, 256)
 
 

time: 164 us -> 156 us (0.951)
  waiting for transfers between devices: 32.8 us -> 24.2 us
  starting transfers between devices: 53.3 us -> 47 us
  blocking collectives: 44.3 us -> 49.8 us
    ppermute x13 -> x12, starting transfers between devices: 46 us -> 39.8 us  [shift(): return lax.ppermute(v, axis, [(i, (i + by) % n) for i in range(n)])]
    all_gather x0 -> x1, blocking collectives: none -> 5.51 us  [per_device(): o_got = lax.all_gather(o_oth, 'c', axis=0)]
    ppermute x2, waiting for transfers between devices: 9.5 us -> 4.98 us  [shift_cores(): return lax.ppermute(v, ('zl', 'zh', 'c'), pairs)]
    ppermute x13 -> x12, waiting for transfers between devices: 23.2 us -> 19.2 us  [shift(): return lax.ppermute(v, axis, [(i, (i + by) % n) for i in range(n)])]
    pallas_call x1 -> x2, Pallas kernels: 4.45 us -> 5.64 us  [the longest x1 5.23 us: project_out(): pl.pallas_call(most_kernel, out_shape=[jax.ShapeDtypeStruct((2, TOK, 256)...]
  transfers between devices with their start and end apart: 16 -> 15, of which waited for: 7 -> 7; matrix products, arithmetic and copies ran while one was open for 0% -> 0% of each run, Pallas kernels for 6% -> 9%
where the time goes in v3:
time: 156 us
  blocking collectives  49.8 us (32%)
  starting transfers between devices  47 us (30%)
  waiting for transfers between devices  24.2 us (16%)
  Pallas kernels  14.8 us (9%)
  between operations  13.6 us (9%)
  local copies, waits for them, and re-layouts  4.86 us (3%)
    ppermute x12, starting transfers between devices, shift(): return lax.ppermute(v, axis, [(i, (i + by) % n) for i in range(n)])  39.8 us
    ppermute x12, waiting for transfers between devices, shift(): return lax.ppermute(v, axis, [(i, (i + by) % n) for i in range(n)])  19.2 us
    all_gather x1, blocking collectives, per_device(): lax.all_gather(pixels.reshape(2, 32, KP), ('zh', 'c'), axis=0)  17.9 us
    all_gather x1, blocking collectives, per_device(): hs = ring(lax.all_gather(hid, 'zh', axis=0))  14.3 us
    all_gather x1, blocking collectives, per_device(): wx = lax.all_gather(wt, 'x', axis=0)  12 us
    pallas_call x1, Pallas kernels, embed_hidden(): pl.pallas_call(embed_kernel, out_shape=jax.ShapeDtypeStruct((NY, 16, 2 *...  9.2 us
    ppermute x2, starting transfers between devices, shift_cores(): return lax.ppermute(v, ('zl', 'zh', 'c'), pairs)  7.26 us
    all_gather x1, blocking collectives, per_device(): o_got = lax.all_gather(o_oth, 'c', axis=0)  5.51 us
  transfers between devices with their start and end apart: 15, of which 7 were waited for; matrix products, arithmetic and copies ran while one was open for 0% of the time, Pallas kernels for 9%

profile of v3, /device:TPU:135, one launch (start us, length us, event | category | flops | bytes accessed | tf_op | source)
XLA Modules:
  0.0 155.8 jit_solution(5339788810730473190)
XLA Ops:
  6.5 0.0 copy-start.6
  6.5 0.0 copy-start.7
  6.5 0.0 all-gather.5.cloned.1.call-start
  6.5 17.9 %all-gather = bf16[8,1,32,1176]{3,2,1,0:T(8,128)(2,1)S(1)} all-gather(bf16[2,1,32,1176]{3,2,1,0:T(8,128)(2,1)} %param.8), channel_id=2, replica_groups=mesh['x'=4,'zl'=4,'zh'=2,'y'=8,'c'=2] {'zh','c'}, dimensions={0}, use_global_device_ids=true | all-gather | bytes 752640 | tf_op jit(solution)/shard_map/all_gather | solution.py:222
  24.5 0.0 copy-start
  24.5 0.6 broadcast_select_fusion
  25.1 0.8 copy.16
  25.9 0.0 all-gather.5.cloned.1.call-update
  25.9 0.0 copy-done.6
  25.9 0.0 copy-done.7
  25.9 0.1 pad_maximum_fusion.1.refs_9_
  26.0 0.0 copy-start.1
  26.0 12.0 %all-gather.1 = bf16[320,1176]{1,0:T(8,128)(2,1)S(1)} all-gather(bf16[80,1176]{1,0:T(8,128)(2,1)} %bitcast.20), channel_id=3, replica_groups=mesh['x'=4,'zl'=4,'zh'=2,'y'=8,'c'=2] {'x'}, dimensions={0}, use_global_device_ids=true | all-gather | bytes 940800 | tf_op jit(solution)/shard_map/all_gather | solution.py:228
  38.0 0.0 copy-start.5
  38.1 4.8 %collective-permute-start.5 = (bf16[160,5120]{1,0:T(8,128)(2,1)}, bf16[160,5120]{1,0:T(8,128)(2,1)}, u32[]{:S(2)}, u32[]{:S(2)}) collective-permute-start(bf16[160,5120]{1,0:T(8,128)(2,1)} %bitcast.22), channel_id=1, source_target_pairs={{0,1},{1,0},{2,3},{3,2},{4,5},{5,4},{6,7},{7,6},{8,9},{9,8},{10,11... | collective-permute-start | bytes 4915208 | tf_op jit(solution)/shard_map/ppermute | solution.py:18
  42.9 2.0 %collective-permute-start = (bf16[4,80,1176]{2,1,0:T(8,128)(2,1)S(1)}, bf16[4,80,1176]{2,1,0:T(8,128)(2,1)S(1)}, u32[]{:S(2)}, u32[]{:S(2)}) collective-permute-start(bf16[4,80,1176]{2,1,0:T(8,128)(2,1)S(1)} %bitcast.12), channel_id=1, source_target_pairs={{0,112},{1,33},{32,0},{33,65},{64,32},{65,97},{96,64},{97,17},{16,... | collective-permute-start | bytes 2257928 | tf_op jit(solution)/shard_map/ppermute | solution.py:27
  44.9 5.2 %collective-permute-start.1 = (bf16[2,80,1176]{2,1,0:T(8,128)(2,1)S(1)}, bf16[2,80,1176]{2,1,0:T(8,128)(2,1)S(1)}, u32[]{:S(2)}, u32[]{:S(2)}) collective-permute-start(bf16[2,80,1176]{2,1,0:T(8,128)(2,1)S(1)} %bitcast.19), channel_id=1, source_target_pairs={{0,80},{1,65},{32,112},{33,97},{64,0},{65,17},{96,32},{97,49},{16,... | collective-permute-start | bytes 1128968 | tf_op jit(solution)/shard_map/ppermute | solution.py:27
  50.2 0.0 copy-done
  50.2 2.7 %collective-permute-start.13 = (bf16[5120,256]{1,0:T(8,128)(2,1)S(1)}, bf16[5120,256]{1,0:T(8,128)(2,1)}, u32[]{:S(2)}, u32[]{:S(2)}) collective-permute-start(bf16[5120,256]{1,0:T(8,128)(2,1)S(1)} %copy-done), channel_id=1, source_target_pairs={{0,1},{1,0},{2,3},{3,2},{4,5},{5,4},{6,7},{7,6},{8,9},{9,8},{10,11... | collective-permute-start | bytes 7864328 | tf_op jit(solution)/shard_map/ppermute | solution.py:18
  52.9 1.9 %collective-permute-start.2 = (f32[416]{0:T(512)S(1)}, f32[416]{0:T(512)S(1)}, u32[]{:S(2)}, u32[]{:S(2)}) collective-permute-start(f32[416]{0:T(512)S(1)} %pad_maximum_fusion.1.refs_9_), channel_id=1, source_target_pairs={{0,1},{1,0},{2,3},{3,2},{4,5},{5,4},{6,7},{7,6},{8,9},{9,8},{10,11... | collective-permute-start | bytes 5000 | tf_op jit(solution)/shard_map/ppermute | solution.py:18
  54.8 2.6 %collective-permute-done.2.refs_10_ = f32[416]{0:T(512)S(1)} collective-permute-done((f32[416]{0:T(512)S(1)}, f32[416]{0:T(512)S(1)}, u32[]{:S(2)}, u32[]{:S(2)}) %collective-permute-start.2) | collective-permute-done | bytes 1696 | tf_op jit(solution)/shard_map/ppermute | solution.py:18
  57.4 0.0 copy-start.3
  57.4 5.0 %collective-permute-done.1.refs_3_ = bf16[2,80,1176]{2,1,0:T(8,128)(2,1)S(1)} collective-permute-done((bf16[2,80,1176]{2,1,0:T(8,128)(2,1)S(1)}, bf16[2,80,1176]{2,1,0:T(8,128)(2,1)S(1)}, u32[]{:S(2)}, u32[]{:S(2)}) %collective-permute-start.1) | collective-permute-done | bytes 376352 | tf_op jit(solution)/shard_map/ppermute | solution.py:27
  62.4 0.0 copy-start.10
  62.4 0.0 collective-permute-done.refs_1_
  62.4 0.0 copy-start.8
  62.4 1.0 copy-done.8
  63.4 6.5 %collective-permute-start.3 = (bf16[4,80,1176]{2,1,0:T(8,128)(2,1)S(1)}, bf16[4,80,1176]{2,1,0:T(8,128)(2,1)S(1)}, u32[]{:S(2)}, u32[]{:S(2)}) collective-permute-start(bf16[4,80,1176]{2,1,0:T(8,128)(2,1)S(1)} %collective-permute-done.refs_1_), channel_id=1, source_target_pairs={{0,1},{1,0},{2,3},{3,2},{4,5},{5,4},{6,7},{7,6},{8,9},{9,8},{10,11... | collective-permute-start | bytes 2257928 | tf_op jit(solution)/shard_map/ppermute | solution.py:18
  69.9 1.9 %collective-permute-start.4 = (bf16[2,80,1176]{2,1,0:T(8,128)(2,1)S(1)}, bf16[2,80,1176]{2,1,0:T(8,128)(2,1)S(1)}, u32[]{:S(2)}, u32[]{:S(2)}) collective-permute-start(bf16[2,80,1176]{2,1,0:T(8,128)(2,1)S(1)} %collective-permute-done.1.refs_3_), channel_id=1, source_target_pairs={{0,1},{1,0},{2,3},{3,2},{4,5},{5,4},{6,7},{7,6},{8,9},{9,8},{10,11... | collective-permute-start | bytes 1128968 | tf_op jit(solution)/shard_map/ppermute | solution.py:18
  71.8 1.7 %collective-permute-done.4.refs_4_ = bf16[2,80,1176]{2,1,0:T(8,128)(2,1)S(1)} collective-permute-done((bf16[2,80,1176]{2,1,0:T(8,128)(2,1)S(1)}, bf16[2,80,1176]{2,1,0:T(8,128)(2,1)S(1)}, u32[]{:S(2)}, u32[]{:S(2)}) %collective-permute-start.4) | collective-permute-done | bytes 376352 | tf_op jit(solution)/shard_map/ppermute | solution.py:18
  73.5 0.0 copy-start.11
  73.5 0.0 collective-permute-done.3.refs_2_
  73.5 0.0 copy-done.10
  73.5 0.8 copy-done.11
  74.3 0.0 copy-start.9
  74.3 1.0 copy-done.9
  75.3 0.0 collective-permute-done.5.refs_6_
  75.3 0.0 copy-done.1
  75.3 0.0 copy-done.5
  75.3 0.0 copy-done.3
  75.3 9.2 %embed_hidden.1 = bf16[8,16,640]{2,1,0:T(8,128)(2,1)} custom-call(bf16[8,2,4,16,1176]{4,3,2,1,0:T(8,128)(2,1)} %all-gather.5.cloned.1.call-done.px, bf16[4,80,1176]{2,1,0:T(8,128)(2,1)} %bitcast.13, bf16[4,80,1176]{2,1,0:T(8,128)(2,1)} %copy-done.8, bf16[4,80,1176]{2,1,0:T(8,128)(2,1)} %copy-done.9, bf16[2,80,1176]{2,1,0:T(8,128)(2,1)} %copy-done.10, ...), custom_call_target="tpu_custom_call" | custom-call | flops 3921674240 | bytes 9437184 | tf_op jit(solution)/shard_map/embed_hidden/pallas_call | solution.py:97
  84.5 14.3 %all_gather.25.refs_0_ = bf16[2,128,640]{2,1,0:T(8,128)(2,1)S(1)} all-gather(bf16[1,128,640]{2,1,0:T(8,128)(2,1)} %bitcast.21), channel_id=1, replica_groups=mesh['x'=4,'zl'=4,'zh'=2,'y'=8,'c'=2] {'zh'}, dimensions={0}, use_global_device_ids=true | all-gather | bytes 491520 | tf_op jit(solution)/shard_map/all_gather | solution.py:249
  98.8 3.2 %collective-permute-start.6 = (bf16[2,128,640]{2,1,0:T(8,128)(2,1)S(1)}, bf16[2,128,640]{2,1,0:T(8,128)(2,1)S(1)}, u32[]{:S(2)}, u32[]{:S(2)}) collective-permute-start(bf16[2,128,640]{2,1,0:T(8,128)(2,1)S(1)} %all_gather.25.refs_0_), channel_id=1, source_target_pairs={{0,2},{2,4},{4,6},{6,8},{8,10},{10,12},{12,14},{14,0},{1,3},{3,5},... | collective-permute-start | bytes 983048 | tf_op jit(solution)/shard_map/ppermute | solution.py:18
  102.0 3.8 %collective-permute-start.10 = (bf16[2,128,640]{2,1,0:T(8,128)(2,1)S(1)}, bf16[2,128,640]{2,1,0:T(8,128)(2,1)S(1)}, u32[]{:S(2)}, u32[]{:S(2)}) collective-permute-start(bf16[2,128,640]{2,1,0:T(8,128)(2,1)S(1)} %all_gather.25.refs_0_), channel_id=1, source_target_pairs={{0,14},{2,0},{4,2},{6,4},{8,6},{10,8},{12,10},{14,12},{1,15},{3,1}... | collective-permute-start | bytes 983048 | tf_op jit(solution)/shard_map/ppermute | solution.py:18
  105.9 5.6 %collective-permute-done.6.refs_1_ = bf16[2,128,640]{2,1,0:T(8,128)(2,1)S(1)} collective-permute-done((bf16[2,128,640]{2,1,0:T(8,128)(2,1)S(1)}, bf16[2,128,640]{2,1,0:T(8,128)(2,1)S(1)}, u32[]{:S(2)}, u32[]{:S(2)}) %collective-permute-start.6) | collective-permute-done | bytes 327712 | tf_op jit(solution)/shard_map/ppermute | solution.py:18
  111.5 1.9 %collective-permute-start.7 = (bf16[2,128,640]{2,1,0:T(8,128)(2,1)S(1)}, bf16[2,128,640]{2,1,0:T(8,128)(2,1)S(1)}, u32[]{:S(2)}, u32[]{:S(2)}) collective-permute-start(bf16[2,128,640]{2,1,0:T(8,128)(2,1)S(1)} %collective-permute-done.6.refs_1_), channel_id=1, source_target_pairs={{0,2},{2,4},{4,6},{6,8},{8,10},{10,12},{12,14},{14,0},{1,3},{3,5},... | collective-permute-start | bytes 983048 | tf_op jit(solution)/shard_map/ppermute | solution.py:18
  113.4 0.0 collective-permute-done.10.refs_4_
  113.4 4.6 %collective-permute-start.11 = (bf16[2,128,640]{2,1,0:T(8,128)(2,1)S(1)}, bf16[2,128,640]{2,1,0:T(8,128)(2,1)S(1)}, u32[]{:S(2)}, u32[]{:S(2)}) collective-permute-start(bf16[2,128,640]{2,1,0:T(8,128)(2,1)S(1)} %collective-permute-done.10.refs_4_), channel_id=1, source_target_pairs={{0,14},{2,0},{4,2},{6,4},{8,6},{10,8},{12,10},{14,12},{1,15},{3,1}... | collective-permute-start | bytes 983048 | tf_op jit(solution)/shard_map/ppermute | solution.py:18
  118.0 4.7 %collective-permute-done.7.refs_2_ = bf16[2,128,640]{2,1,0:T(8,128)(2,1)S(1)} collective-permute-done((bf16[2,128,640]{2,1,0:T(8,128)(2,1)S(1)}, bf16[2,128,640]{2,1,0:T(8,128)(2,1)S(1)}, u32[]{:S(2)}, u32[]{:S(2)}) %collective-permute-start.7) | collective-permute-done | bytes 327712 | tf_op jit(solution)/shard_map/ppermute | solution.py:18
  122.7 1.9 %collective-permute-start.8 = (bf16[2,128,640]{2,1,0:T(8,128)(2,1)S(1)}, bf16[2,128,640]{2,1,0:T(8,128)(2,1)S(1)}, u32[]{:S(2)}, u32[]{:S(2)}) collective-permute-start(bf16[2,128,640]{2,1,0:T(8,128)(2,1)S(1)} %collective-permute-done.7.refs_2_), channel_id=1, source_target_pairs={{0,2},{2,4},{4,6},{6,8},{8,10},{10,12},{12,14},{14,0},{1,3},{3,5},... | collective-permute-start | bytes 983048 | tf_op jit(solution)/shard_map/ppermute | solution.py:18
  124.6 0.0 collective-permute-done.11.refs_5_
  124.6 4.6 %collective-permute-start.12 = (bf16[2,128,640]{2,1,0:T(8,128)(2,1)S(1)}, bf16[2,128,640]{2,1,0:T(8,128)(2,1)S(1)}, u32[]{:S(2)}, u32[]{:S(2)}) collective-permute-start(bf16[2,128,640]{2,1,0:T(8,128)(2,1)S(1)} %collective-permute-done.11.refs_5_), channel_id=1, source_target_pairs={{0,14},{2,0},{4,2},{6,4},{8,6},{10,8},{12,10},{14,12},{1,15},{3,1}... | collective-permute-start | bytes 983048 | tf_op jit(solution)/shard_map/ppermute | solution.py:18
  129.2 3.8 %collective-permute-done.8.refs_3_ = bf16[2,128,640]{2,1,0:T(8,128)(2,1)S(1)} collective-permute-done((bf16[2,128,640]{2,1,0:T(8,128)(2,1)S(1)}, bf16[2,128,640]{2,1,0:T(8,128)(2,1)S(1)}, u32[]{:S(2)}, u32[]{:S(2)}) %collective-permute-start.8) | collective-permute-done | bytes 327712 | tf_op jit(solution)/shard_map/ppermute | solution.py:18
  132.9 1.9 %collective-permute-start.9 = (bf16[2,128,640]{2,1,0:T(8,128)(2,1)S(1)}, bf16[2,128,640]{2,1,0:T(8,128)(2,1)S(1)}, u32[]{:S(2)}, u32[]{:S(2)}) collective-permute-start(bf16[2,128,640]{2,1,0:T(8,128)(2,1)S(1)} %collective-permute-done.8.refs_3_), channel_id=1, source_target_pairs={{0,2},{2,4},{4,6},{6,8},{8,10},{10,12},{12,14},{14,0},{1,3},{3,5},... | collective-permute-start | bytes 983048 | tf_op jit(solution)/shard_map/ppermute | solution.py:18
  134.9 0.0 collective-permute-done.13.refs_8_
  134.9 0.0 collective-permute-done.12.refs_6_
  134.9 0.0 copy-start.2
  134.9 0.6 copy-done.2
  135.5 0.7 copy-done.4
  136.2 5.2 %project_most.1 = (f32[2,256,256]{2,1,0:T(8,128)S(1)}, bf16[2,2,320,256]{3,2,1,0:T(8,128)(2,1)S(1)}) custom-call(bf16[2,128,640]{2,1,0:T(8,128)(2,1)S(1)} %all_gather.25.refs_0_, bf16[2,128,640]{2,1,0:T(8,128)(2,1)S(1)} %collective-permute-done.6.refs_1_, bf16[2,128,640]{2,1,0:T(8,128)(2,1)S(1)} %collective-permute-done.7.refs_2_, ...), custom_call_target="tpu_custom_call" | custom-call | flops 1342177280 | bytes 1048576 | tf_op jit(solution)/shard_map/project_most/pallas_call | solution.py:177
  141.4 0.9 collective-permute-done.9.h
  142.3 0.4 project_last.1
  142.7 5.5 %all-gather.2 = bf16[512,256]{1,0:T(8,128)(2,1)S(1)} all-gather(bf16[256,256]{1,0:T(8,128)(2,1)S(1)} %get-tuple-element.24), channel_id=4, replica_groups=mesh['x'=4,'zl'=4,'zh'=2,'y'=8,'c'=2] {'c'}, dimensions={0}, use_global_device_ids=true | all-gather | bytes 393216 | tf_op jit(solution)/shard_map/all_gather | solution.py:251
  148.2 0.7 pad_maximum_fusion
  (5 shorter events, 0.1 us)
Async XLA Ops:
  6.5 19.4 %copy-start.6 = (f32[256]{0:T(256)S(1)}, f32[256]{0:T(256)}, u32[]{:S(2)}) copy-start(f32[256]{0:T(256)} %param.15) | copy-start | bytes 3076
  6.5 19.4 %copy-start.7 = (f32[160]{0:T(256)S(1)}, f32[160]{0:T(256)}, u32[]{:S(2)}) copy-start(f32[160]{0:T(256)} %param.13) | copy-start | bytes 1924
  6.5 68.7 %all-gather.5.cloned.1.call-start = ((), (), s32[]{:S(2)}) async-start(), calls=%async_computation | async-start | bytes 2949120 | tf_op jit(solution)/shard_map/all_gather | solution.py:225
  24.5 25.7 %copy-start = (bf16[5120,256]{1,0:T(8,128)(2,1)S(1)}, bf16[5120,256]{1,0:T(8,128)(2,1)}, u32[]{:S(2)}) copy-start(bf16[5120,256]{1,0:T(8,128)(2,1)} %refs_7_.2) | copy-start | bytes 7864324
  26.0 49.3 %copy-start.1 = (f32[416]{0:T(512)}, f32[416]{0:T(512)S(1)}, u32[]{:S(2)}) copy-start(f32[416]{0:T(512)S(1)} %pad_maximum_fusion.1.refs_9_) | copy-start | bytes 4996
  38.0 37.3 %copy-start.5 = (bf16[320,1176]{1,0:T(8,128)(2,1)}, bf16[320,1176]{1,0:T(8,128)(2,1)S(1)}, u32[]{:S(2)}) copy-start(bf16[320,1176]{1,0:T(8,128)(2,1)S(1)} %all-gather.1) | copy-start | bytes 2257924
  38.1 37.2 %collective-permute-start.5 = (bf16[160,5120]{1,0:T(8,128)(2,1)}, bf16[160,5120]{1,0:T(8,128)(2,1)}, u32[]{:S(2)}, u32[]{:S(2)}) collective-permute-start(bf16[160,5120]{1,0:T(8,128)(2,1)} %bitcast.22), channel_id=1, source_target_pairs={{0,1},{1,0},{2,3},{3,2},{4,5},{5,4},{6,7},{7,6},{8,9},{9,8},{10,11... | collective-permute-start | bytes 4915208 | tf_op jit(solution)/shard_map/ppermute | solution.py:18
  42.9 19.5 %collective-permute-start = (bf16[4,80,1176]{2,1,0:T(8,128)(2,1)S(1)}, bf16[4,80,1176]{2,1,0:T(8,128)(2,1)S(1)}, u32[]{:S(2)}, u32[]{:S(2)}) collective-permute-start(bf16[4,80,1176]{2,1,0:T(8,128)(2,1)S(1)} %bitcast.12), channel_id=1, source_target_pairs={{0,112},{1,33},{32,0},{33,65},{64,32},{65,97},{96,64},{97,17},{16,... | collective-permute-start | bytes 2257928 | tf_op jit(solution)/shard_map/ppermute | solution.py:27
  44.9 17.4 %collective-permute-start.1 = (bf16[2,80,1176]{2,1,0:T(8,128)(2,1)S(1)}, bf16[2,80,1176]{2,1,0:T(8,128)(2,1)S(1)}, u32[]{:S(2)}, u32[]{:S(2)}) collective-permute-start(bf16[2,80,1176]{2,1,0:T(8,128)(2,1)S(1)} %bitcast.19), channel_id=1, source_target_pairs={{0,80},{1,65},{32,112},{33,97},{64,0},{65,17},{96,32},{97,49},{16,... | collective-permute-start | bytes 1128968 | tf_op jit(solution)/shard_map/ppermute | solution.py:27
  50.2 84.7 %collective-permute-start.13 = (bf16[5120,256]{1,0:T(8,128)(2,1)S(1)}, bf16[5120,256]{1,0:T(8,128)(2,1)}, u32[]{:S(2)}, u32[]{:S(2)}) collective-permute-start(bf16[5120,256]{1,0:T(8,128)(2,1)S(1)} %copy-done), channel_id=1, source_target_pairs={{0,1},{1,0},{2,3},{3,2},{4,5},{5,4},{6,7},{7,6},{8,9},{9,8},{10,11... | collective-permute-start | bytes 7864328 | tf_op jit(solution)/shard_map/ppermute | solution.py:18
  52.9 4.5 %collective-permute-start.2 = (f32[416]{0:T(512)S(1)}, f32[416]{0:T(512)S(1)}, u32[]{:S(2)}, u32[]{:S(2)}) collective-permute-start(f32[416]{0:T(512)S(1)} %pad_maximum_fusion.1.refs_9_), channel_id=1, source_target_pairs={{0,1},{1,0},{2,3},{3,2},{4,5},{5,4},{6,7},{7,6},{8,9},{9,8},{10,11... | collective-permute-start | bytes 5000 | tf_op jit(solution)/shard_map/ppermute | solution.py:18
  57.4 17.9 %copy-start.3 = (f32[416]{0:T(512)}, f32[416]{0:T(512)S(1)}, u32[]{:S(2)}) copy-start(f32[416]{0:T(512)S(1)} %collective-permute-done.2.refs_10_) | copy-start | bytes 4996
  62.4 11.2 %copy-start.10 = (bf16[2,80,1176]{2,1,0:T(8,128)(2,1)}, bf16[2,80,1176]{2,1,0:T(8,128)(2,1)S(1)}, u32[]{:S(2)}) copy-start(bf16[2,80,1176]{2,1,0:T(8,128)(2,1)S(1)} %collective-permute-done.1.refs_3_) | copy-start | bytes 1128964
  62.4 1.0 copy-start.8
  63.4 10.2 %collective-permute-start.3 = (bf16[4,80,1176]{2,1,0:T(8,128)(2,1)S(1)}, bf16[4,80,1176]{2,1,0:T(8,128)(2,1)S(1)}, u32[]{:S(2)}, u32[]{:S(2)}) collective-permute-start(bf16[4,80,1176]{2,1,0:T(8,128)(2,1)S(1)} %collective-permute-done.refs_1_), channel_id=1, source_target_pairs={{0,1},{1,0},{2,3},{3,2},{4,5},{5,4},{6,7},{7,6},{8,9},{9,8},{10,11... | collective-permute-start | bytes 2257928 | tf_op jit(solution)/shard_map/ppermute | solution.py:18
  69.9 3.6 %collective-permute-start.4 = (bf16[2,80,1176]{2,1,0:T(8,128)(2,1)S(1)}, bf16[2,80,1176]{2,1,0:T(8,128)(2,1)S(1)}, u32[]{:S(2)}, u32[]{:S(2)}) collective-permute-start(bf16[2,80,1176]{2,1,0:T(8,128)(2,1)S(1)} %collective-permute-done.1.refs_3_), channel_id=1, source_target_pairs={{0,1},{1,0},{2,3},{3,2},{4,5},{5,4},{6,7},{7,6},{8,9},{9,8},{10,11... | collective-permute-start | bytes 1128968 | tf_op jit(solution)/shard_map/ppermute | solution.py:18
  73.5 0.8 copy-start.11
  74.3 1.0 copy-start.9
  98.8 12.7 %collective-permute-start.6 = (bf16[2,128,640]{2,1,0:T(8,128)(2,1)S(1)}, bf16[2,128,640]{2,1,0:T(8,128)(2,1)S(1)}, u32[]{:S(2)}, u32[]{:S(2)}) collective-permute-start(bf16[2,128,640]{2,1,0:T(8,128)(2,1)S(1)} %all_gather.25.refs_0_), channel_id=1, source_target_pairs={{0,2},{2,4},{4,6},{6,8},{8,10},{10,12},{12,14},{14,0},{1,3},{3,5},... | collective-permute-start | bytes 983048 | tf_op jit(solution)/shard_map/ppermute | solution.py:18
  102.0 11.4 %collective-permute-start.10 = (bf16[2,128,640]{2,1,0:T(8,128)(2,1)S(1)}, bf16[2,128,640]{2,1,0:T(8,128)(2,1)S(1)}, u32[]{:S(2)}, u32[]{:S(2)}) collective-permute-start(bf16[2,128,640]{2,1,0:T(8,128)(2,1)S(1)} %all_gather.25.refs_0_), channel_id=1, source_target_pairs={{0,14},{2,0},{4,2},{6,4},{8,6},{10,8},{12,10},{14,12},{1,15},{3,1}... | collective-permute-start | bytes 983048 | tf_op jit(solution)/shard_map/ppermute | solution.py:18
  111.5 11.2 %collective-permute-start.7 = (bf16[2,128,640]{2,1,0:T(8,128)(2,1)S(1)}, bf16[2,128,640]{2,1,0:T(8,128)(2,1)S(1)}, u32[]{:S(2)}, u32[]{:S(2)}) collective-permute-start(bf16[2,128,640]{2,1,0:T(8,128)(2,1)S(1)} %collective-permute-done.6.refs_1_), channel_id=1, source_target_pairs={{0,2},{2,4},{4,6},{6,8},{8,10},{10,12},{12,14},{14,0},{1,3},{3,5},... | collective-permute-start | bytes 983048 | tf_op jit(solution)/shard_map/ppermute | solution.py:18
  113.4 11.2 %collective-permute-start.11 = (bf16[2,128,640]{2,1,0:T(8,128)(2,1)S(1)}, bf16[2,128,640]{2,1,0:T(8,128)(2,1)S(1)}, u32[]{:S(2)}, u32[]{:S(2)}) collective-permute-start(bf16[2,128,640]{2,1,0:T(8,128)(2,1)S(1)} %collective-permute-done.10.refs_4_), channel_id=1, source_target_pairs={{0,14},{2,0},{4,2},{6,4},{8,6},{10,8},{12,10},{14,12},{1,15},{3,1}... | collective-permute-start | bytes 983048 | tf_op jit(solution)/shard_map/ppermute | solution.py:18
  122.7 10.3 %collective-permute-start.8 = (bf16[2,128,640]{2,1,0:T(8,128)(2,1)S(1)}, bf16[2,128,640]{2,1,0:T(8,128)(2,1)S(1)}, u32[]{:S(2)}, u32[]{:S(2)}) collective-permute-start(bf16[2,128,640]{2,1,0:T(8,128)(2,1)S(1)} %collective-permute-done.7.refs_2_), channel_id=1, source_target_pairs={{0,2},{2,4},{4,6},{6,8},{8,10},{10,12},{12,14},{14,0},{1,3},{3,5},... | collective-permute-start | bytes 983048 | tf_op jit(solution)/shard_map/ppermute | solution.py:18
  124.6 10.3 %collective-permute-start.12 = (bf16[2,128,640]{2,1,0:T(8,128)(2,1)S(1)}, bf16[2,128,640]{2,1,0:T(8,128)(2,1)S(1)}, u32[]{:S(2)}, u32[]{:S(2)}) collective-permute-start(bf16[2,128,640]{2,1,0:T(8,128)(2,1)S(1)} %collective-permute-done.11.refs_5_), channel_id=1, source_target_pairs={{0,14},{2,0},{4,2},{6,4},{8,6},{10,8},{12,10},{14,12},{1,15},{3,1}... | collective-permute-start | bytes 983048 | tf_op jit(solution)/shard_map/ppermute | solution.py:18
  132.9 9.3 %collective-permute-start.9 = (bf16[2,128,640]{2,1,0:T(8,128)(2,1)S(1)}, bf16[2,128,640]{2,1,0:T(8,128)(2,1)S(1)}, u32[]{:S(2)}, u32[]{:S(2)}) collective-permute-start(bf16[2,128,640]{2,1,0:T(8,128)(2,1)S(1)} %collective-permute-done.8.refs_3_), channel_id=1, source_target_pairs={{0,2},{2,4},{4,6},{6,8},{8,10},{10,12},{12,14},{14,0},{1,3},{3,5},... | collective-permute-start | bytes 983048 | tf_op jit(solution)/shard_map/ppermute | solution.py:18
  134.9 0.6 copy-start.2
  135.5 0.7 copy-start.4
Sparse Core Ops, SparseCore 0:
  26.0 42.2 all-gather.4

commit v4 on v3

--- a/solution.py
+++ b/solution.py
@@ -233,8 +233,8 @@
     bias = jnp.concatenate([bias_in, bias_out])
     p_in, p_out, bias, _ = lax.optimization_barrier((proj_in.T, proj_out, bias, part))
     p_in_o, p_out_o, bias_o = [shift(v, "c", 2, 1) for v in (p_in, p_out, bias)]
-    near, two, bias_o = lax.optimization_barrier((near, two, bias_o))
     near_o = shift(near, "c", 2, 1)
+    two, bias_o = lax.optimization_barrier((two, bias_o))
     two_o = shift(two, "c", 2, 1)
     hid = embed_hidden(
         px,

time: 156 us -> 153 us (0.981)
  starting transfers between devices: 47 us -> 45 us
    ppermute x12, waiting for transfers between devices: 19.2 us -> 17 us  [shift(): return lax.ppermute(v, axis, [(i, (i + by) % n) for i in range(n)])]
    ppermute x12, starting transfers between devices: 39.8 us -> 37.7 us  [shift(): return lax.ppermute(v, axis, [(i, (i + by) % n) for i in range(n)])]
    ppermute x2, waiting for transfers between devices: 4.98 us -> 6.85 us  [shift_cores(): return lax.ppermute(v, ('zl', 'zh', 'c'), pairs)]
where the time goes in v4:
time: 153 us; the launch traced here: 152 us
  blocking collectives  49.8 us (33%)
  starting transfers between devices  45 us (29%)
  waiting for transfers between devices  23.9 us (16%)
  Pallas kernels  14.8 us (10%)
  between operations  13.6 us (9%)
  local copies, waits for them, and re-layouts  3.87 us (3%)
    ppermute x12, starting transfers between devices, shift(): return lax.ppermute(v, axis, [(i, (i + by) % n) for i in range(n)])  37.7 us
    all_gather x1, blocking collectives, per_device(): lax.all_gather(pixels.reshape(2, 32, KP), ('zh', 'c'), axis=0)  17.9 us
    ppermute x12, waiting for transfers between devices, shift(): return lax.ppermute(v, axis, [(i, (i + by) % n) for i in range(n)])  17 us
    all_gather x1, blocking collectives, per_device(): hs = ring(lax.all_gather(hid, 'zh', axis=0))  14.3 us
    all_gather x1, blocking collectives, per_device(): wx = lax.all_gather(wt, 'x', axis=0)  12 us
    pallas_call x1, Pallas kernels, embed_hidden(): pl.pallas_call(embed_kernel, out_shape=jax.ShapeDtypeStruct((NY, 16, 2 *...  9.21 us
    ppermute x2, starting transfers between devices, shift_cores(): return lax.ppermute(v, ('zl', 'zh', 'c'), pairs)  7.26 us
    ppermute x2, waiting for transfers between devices, shift_cores(): return lax.ppermute(v, ('zl', 'zh', 'c'), pairs)  6.85 us
  transfers between devices with their start and end apart: 15, of which 7 were waited for; matrix products, arithmetic and copies ran while one was open for 0% of the time, Pallas kernels for 9%

profile of v4, /device:TPU:135, one launch (start us, length us, event | category | flops | bytes accessed | tf_op | source)
XLA Modules:
  0.0 152.4 jit_solution(18110055804390733486)
XLA Ops:
  6.5 0.0 copy-start.6
  6.5 0.0 copy-start.7
  6.5 0.0 all-gather.5.cloned.1.call-start
  6.5 17.9 %all-gather = bf16[8,1,32,1176]{3,2,1,0:T(8,128)(2,1)S(1)} all-gather(bf16[2,1,32,1176]{3,2,1,0:T(8,128)(2,1)} %param.8), channel_id=2, replica_groups=mesh['x'=4,'zl'=4,'zh'=2,'y'=8,'c'=2] {'zh','c'}, dimensions={0}, use_global_device_ids=true | all-gather | bytes 752640 | tf_op jit(solution)/shard_map/all_gather | solution.py:222
  24.5 0.0 copy-start
  24.5 0.6 broadcast_select_fusion
  25.1 0.8 copy.16
  25.9 0.0 all-gather.5.cloned.1.call-update
  25.9 0.0 copy-done.6
  25.9 0.0 copy-done.7
  25.9 0.1 pad_maximum_fusion.1.refs_9_
  26.0 0.0 copy-start.1
  26.0 12.0 %all-gather.1 = bf16[320,1176]{1,0:T(8,128)(2,1)S(1)} all-gather(bf16[80,1176]{1,0:T(8,128)(2,1)} %bitcast.20), channel_id=3, replica_groups=mesh['x'=4,'zl'=4,'zh'=2,'y'=8,'c'=2] {'x'}, dimensions={0}, use_global_device_ids=true | all-gather | bytes 940800 | tf_op jit(solution)/shard_map/all_gather | solution.py:228
  38.0 0.0 copy-start.5
  38.1 4.8 %collective-permute-start.5 = (bf16[160,5120]{1,0:T(8,128)(2,1)}, bf16[160,5120]{1,0:T(8,128)(2,1)}, u32[]{:S(2)}, u32[]{:S(2)}) collective-permute-start(bf16[160,5120]{1,0:T(8,128)(2,1)} %bitcast.22), channel_id=1, source_target_pairs={{0,1},{1,0},{2,3},{3,2},{4,5},{5,4},{6,7},{7,6},{8,9},{9,8},{10,11... | collective-permute-start | bytes 4915208 | tf_op jit(solution)/shard_map/ppermute | solution.py:18
  42.9 2.0 %collective-permute-start = (bf16[4,80,1176]{2,1,0:T(8,128)(2,1)S(1)}, bf16[4,80,1176]{2,1,0:T(8,128)(2,1)S(1)}, u32[]{:S(2)}, u32[]{:S(2)}) collective-permute-start(bf16[4,80,1176]{2,1,0:T(8,128)(2,1)S(1)} %bitcast.12), channel_id=1, source_target_pairs={{0,112},{1,33},{32,0},{33,65},{64,32},{65,97},{96,64},{97,17},{16,... | collective-permute-start | bytes 2257928 | tf_op jit(solution)/shard_map/ppermute | solution.py:27
  44.9 0.0 copy-done
  45.0 1.9 %collective-permute-start.13 = (bf16[5120,256]{1,0:T(8,128)(2,1)S(1)}, bf16[5120,256]{1,0:T(8,128)(2,1)}, u32[]{:S(2)}, u32[]{:S(2)}) collective-permute-start(bf16[5120,256]{1,0:T(8,128)(2,1)S(1)} %copy-done), channel_id=1, source_target_pairs={{0,1},{1,0},{2,3},{3,2},{4,5},{5,4},{6,7},{7,6},{8,9},{9,8},{10,11... | collective-permute-start | bytes 7864328 | tf_op jit(solution)/shard_map/ppermute | solution.py:18
  46.9 5.2 %collective-permute-start.2 = (bf16[2,80,1176]{2,1,0:T(8,128)(2,1)S(1)}, bf16[2,80,1176]{2,1,0:T(8,128)(2,1)S(1)}, u32[]{:S(2)}, u32[]{:S(2)}) collective-permute-start(bf16[2,80,1176]{2,1,0:T(8,128)(2,1)S(1)} %bitcast.19), channel_id=1, source_target_pairs={{0,80},{1,65},{32,112},{33,97},{64,0},{65,17},{96,32},{97,49},{16,... | collective-permute-start | bytes 1128968 | tf_op jit(solution)/shard_map/ppermute | solution.py:27
  52.1 6.8 %collective-permute-done.refs_1_ = bf16[4,80,1176]{2,1,0:T(8,128)(2,1)S(1)} collective-permute-done((bf16[4,80,1176]{2,1,0:T(8,128)(2,1)S(1)}, bf16[4,80,1176]{2,1,0:T(8,128)(2,1)S(1)}, u32[]{:S(2)}, u32[]{:S(2)}) %collective-permute-start) | collective-permute-done | bytes 752672 | tf_op jit(solution)/shard_map/ppermute | solution.py:27
  59.0 0.0 copy-start.8
  59.0 1.9 %collective-permute-start.1 = (bf16[4,80,1176]{2,1,0:T(8,128)(2,1)S(1)}, bf16[4,80,1176]{2,1,0:T(8,128)(2,1)S(1)}, u32[]{:S(2)}, u32[]{:S(2)}) collective-permute-start(bf16[4,80,1176]{2,1,0:T(8,128)(2,1)S(1)} %collective-permute-done.refs_1_), channel_id=1, source_target_pairs={{0,1},{1,0},{2,3},{3,2},{4,5},{5,4},{6,7},{7,6},{8,9},{9,8},{10,11... | collective-permute-start | bytes 2257928 | tf_op jit(solution)/shard_map/ppermute | solution.py:18
  60.9 2.4 %collective-permute-start.3 = (f32[416]{0:T(512)S(1)}, f32[416]{0:T(512)S(1)}, u32[]{:S(2)}, u32[]{:S(2)}) collective-permute-start(f32[416]{0:T(512)S(1)} %pad_maximum_fusion.1.refs_9_), channel_id=1, source_target_pairs={{0,1},{1,0},{2,3},{3,2},{4,5},{5,4},{6,7},{7,6},{8,9},{9,8},{10,11... | collective-permute-start | bytes 5000 | tf_op jit(solution)/shard_map/ppermute | solution.py:18
  63.3 0.8 collective-permute-done.3.refs_10_
  64.1 0.0 copy-start.3
  64.1 0.0 collective-permute-done.2.refs_3_
  64.1 0.0 copy-done.8
  64.1 0.0 copy-start.10
  64.1 4.8 %collective-permute-start.4 = (bf16[2,80,1176]{2,1,0:T(8,128)(2,1)S(1)}, bf16[2,80,1176]{2,1,0:T(8,128)(2,1)S(1)}, u32[]{:S(2)}, u32[]{:S(2)}) collective-permute-start(bf16[2,80,1176]{2,1,0:T(8,128)(2,1)S(1)} %collective-permute-done.2.refs_3_), channel_id=1, source_target_pairs={{0,1},{1,0},{2,3},{3,2},{4,5},{5,4},{6,7},{7,6},{8,9},{9,8},{10,11... | collective-permute-start | bytes 1128968 | tf_op jit(solution)/shard_map/ppermute | solution.py:18
  68.9 1.4 collective-permute-done.4.refs_4_
  70.2 0.0 copy-start.11
  70.2 0.0 collective-permute-done.1.refs_2_
  70.3 0.0 copy-done.10
  70.3 0.8 copy-done.11
  71.0 0.0 copy-start.9
  71.0 1.0 copy-done.9
  72.0 0.0 collective-permute-done.5.refs_6_
  72.0 0.0 copy-done.1
  72.0 0.0 copy-done.5
  72.0 0.0 copy-done.3
  72.0 9.2 %embed_hidden.1 = bf16[8,16,640]{2,1,0:T(8,128)(2,1)} custom-call(bf16[8,2,4,16,1176]{4,3,2,1,0:T(8,128)(2,1)} %all-gather.5.cloned.1.call-done.px, bf16[4,80,1176]{2,1,0:T(8,128)(2,1)} %bitcast.13, bf16[4,80,1176]{2,1,0:T(8,128)(2,1)} %copy-done.8, bf16[4,80,1176]{2,1,0:T(8,128)(2,1)} %copy-done.9, bf16[2,80,1176]{2,1,0:T(8,128)(2,1)} %copy-done.10, ...), custom_call_target="tpu_custom_call" | custom-call | flops 3921674240 | bytes 9437184 | tf_op jit(solution)/shard_map/embed_hidden/pallas_call | solution.py:97
  81.2 14.3 %all_gather.25.refs_0_ = bf16[2,128,640]{2,1,0:T(8,128)(2,1)S(1)} all-gather(bf16[1,128,640]{2,1,0:T(8,128)(2,1)} %bitcast.21), channel_id=1, replica_groups=mesh['x'=4,'zl'=4,'zh'=2,'y'=8,'c'=2] {'zh'}, dimensions={0}, use_global_device_ids=true | all-gather | bytes 491520 | tf_op jit(solution)/shard_map/all_gather | solution.py:249
  95.5 3.2 %collective-permute-start.6 = (bf16[2,128,640]{2,1,0:T(8,128)(2,1)S(1)}, bf16[2,128,640]{2,1,0:T(8,128)(2,1)S(1)}, u32[]{:S(2)}, u32[]{:S(2)}) collective-permute-start(bf16[2,128,640]{2,1,0:T(8,128)(2,1)S(1)} %all_gather.25.refs_0_), channel_id=1, source_target_pairs={{0,2},{2,4},{4,6},{6,8},{8,10},{10,12},{12,14},{14,0},{1,3},{3,5},... | collective-permute-start | bytes 983048 | tf_op jit(solution)/shard_map/ppermute | solution.py:18
  98.8 3.8 %collective-permute-start.10 = (bf16[2,128,640]{2,1,0:T(8,128)(2,1)S(1)}, bf16[2,128,640]{2,1,0:T(8,128)(2,1)S(1)}, u32[]{:S(2)}, u32[]{:S(2)}) collective-permute-start(bf16[2,128,640]{2,1,0:T(8,128)(2,1)S(1)} %all_gather.25.refs_0_), channel_id=1, source_target_pairs={{0,14},{2,0},{4,2},{6,4},{8,6},{10,8},{12,10},{14,12},{1,15},{3,1}... | collective-permute-start | bytes 983048 | tf_op jit(solution)/shard_map/ppermute | solution.py:18
  102.6 5.6 %collective-permute-done.6.refs_1_ = bf16[2,128,640]{2,1,0:T(8,128)(2,1)S(1)} collective-permute-done((bf16[2,128,640]{2,1,0:T(8,128)(2,1)S(1)}, bf16[2,128,640]{2,1,0:T(8,128)(2,1)S(1)}, u32[]{:S(2)}, u32[]{:S(2)}) %collective-permute-start.6) | collective-permute-done | bytes 327712 | tf_op jit(solution)/shard_map/ppermute | solution.py:18
  108.1 1.9 %collective-permute-start.7 = (bf16[2,128,640]{2,1,0:T(8,128)(2,1)S(1)}, bf16[2,128,640]{2,1,0:T(8,128)(2,1)S(1)}, u32[]{:S(2)}, u32[]{:S(2)}) collective-permute-start(bf16[2,128,640]{2,1,0:T(8,128)(2,1)S(1)} %collective-permute-done.6.refs_1_), channel_id=1, source_target_pairs={{0,2},{2,4},{4,6},{6,8},{8,10},{10,12},{12,14},{14,0},{1,3},{3,5},... | collective-permute-start | bytes 983048 | tf_op jit(solution)/shard_map/ppermute | solution.py:18
  110.1 0.0 collective-permute-done.10.refs_4_
  110.1 4.6 %collective-permute-start.11 = (bf16[2,128,640]{2,1,0:T(8,128)(2,1)S(1)}, bf16[2,128,640]{2,1,0:T(8,128)(2,1)S(1)}, u32[]{:S(2)}, u32[]{:S(2)}) collective-permute-start(bf16[2,128,640]{2,1,0:T(8,128)(2,1)S(1)} %collective-permute-done.10.refs_4_), channel_id=1, source_target_pairs={{0,14},{2,0},{4,2},{6,4},{8,6},{10,8},{12,10},{14,12},{1,15},{3,1}... | collective-permute-start | bytes 983048 | tf_op jit(solution)/shard_map/ppermute | solution.py:18
  114.7 4.7 %collective-permute-done.7.refs_2_ = bf16[2,128,640]{2,1,0:T(8,128)(2,1)S(1)} collective-permute-done((bf16[2,128,640]{2,1,0:T(8,128)(2,1)S(1)}, bf16[2,128,640]{2,1,0:T(8,128)(2,1)S(1)}, u32[]{:S(2)}, u32[]{:S(2)}) %collective-permute-start.7) | collective-permute-done | bytes 327712 | tf_op jit(solution)/shard_map/ppermute | solution.py:18
  119.3 1.9 %collective-permute-start.8 = (bf16[2,128,640]{2,1,0:T(8,128)(2,1)S(1)}, bf16[2,128,640]{2,1,0:T(8,128)(2,1)S(1)}, u32[]{:S(2)}, u32[]{:S(2)}) collective-permute-start(bf16[2,128,640]{2,1,0:T(8,128)(2,1)S(1)} %collective-permute-done.7.refs_2_), channel_id=1, source_target_pairs={{0,2},{2,4},{4,6},{6,8},{8,10},{10,12},{12,14},{14,0},{1,3},{3,5},... | collective-permute-start | bytes 983048 | tf_op jit(solution)/shard_map/ppermute | solution.py:18
  121.2 0.0 collective-permute-done.11.refs_5_
  121.2 4.6 %collective-permute-start.12 = (bf16[2,128,640]{2,1,0:T(8,128)(2,1)S(1)}, bf16[2,128,640]{2,1,0:T(8,128)(2,1)S(1)}, u32[]{:S(2)}, u32[]{:S(2)}) collective-permute-start(bf16[2,128,640]{2,1,0:T(8,128)(2,1)S(1)} %collective-permute-done.11.refs_5_), channel_id=1, source_target_pairs={{0,14},{2,0},{4,2},{6,4},{8,6},{10,8},{12,10},{14,12},{1,15},{3,1}... | collective-permute-start | bytes 983048 | tf_op jit(solution)/shard_map/ppermute | solution.py:18
  125.8 3.7 %collective-permute-done.8.refs_3_ = bf16[2,128,640]{2,1,0:T(8,128)(2,1)S(1)} collective-permute-done((bf16[2,128,640]{2,1,0:T(8,128)(2,1)S(1)}, bf16[2,128,640]{2,1,0:T(8,128)(2,1)S(1)}, u32[]{:S(2)}, u32[]{:S(2)}) %collective-permute-start.8) | collective-permute-done | bytes 327712 | tf_op jit(solution)/shard_map/ppermute | solution.py:18
  129.6 1.9 %collective-permute-start.9 = (bf16[2,128,640]{2,1,0:T(8,128)(2,1)S(1)}, bf16[2,128,640]{2,1,0:T(8,128)(2,1)S(1)}, u32[]{:S(2)}, u32[]{:S(2)}) collective-permute-start(bf16[2,128,640]{2,1,0:T(8,128)(2,1)S(1)} %collective-permute-done.8.refs_3_), channel_id=1, source_target_pairs={{0,2},{2,4},{4,6},{6,8},{8,10},{10,12},{12,14},{14,0},{1,3},{3,5},... | collective-permute-start | bytes 983048 | tf_op jit(solution)/shard_map/ppermute | solution.py:18
  131.5 0.0 collective-permute-done.13.refs_8_
  131.5 0.0 collective-permute-done.12.refs_6_
  131.5 0.0 copy-start.2
  131.5 0.6 copy-done.2
  132.1 0.7 copy-done.4
  132.8 5.2 %project_most.1 = (f32[2,256,256]{2,1,0:T(8,128)S(1)}, bf16[2,2,320,256]{3,2,1,0:T(8,128)(2,1)S(1)}) custom-call(bf16[2,128,640]{2,1,0:T(8,128)(2,1)S(1)} %all_gather.25.refs_0_, bf16[2,128,640]{2,1,0:T(8,128)(2,1)S(1)} %collective-permute-done.6.refs_1_, bf16[2,128,640]{2,1,0:T(8,128)(2,1)S(1)} %collective-permute-done.7.refs_2_, ...), custom_call_target="tpu_custom_call" | custom-call | flops 1342177280 | bytes 1048576 | tf_op jit(solution)/shard_map/project_most/pallas_call | solution.py:177
  138.0 0.9 collective-permute-done.9.h
  138.9 0.4 project_last.1
  139.3 5.5 %all-gather.2 = bf16[512,256]{1,0:T(8,128)(2,1)S(1)} all-gather(bf16[256,256]{1,0:T(8,128)(2,1)S(1)} %get-tuple-element.22), channel_id=4, replica_groups=mesh['x'=4,'zl'=4,'zh'=2,'y'=8,'c'=2] {'c'}, dimensions={0}, use_global_device_ids=true | all-gather | bytes 393216 | tf_op jit(solution)/shard_map/all_gather | solution.py:251
  144.8 0.7 pad_maximum_fusion
  (5 shorter events, 0.1 us)
Async XLA Ops:
  6.5 19.4 %copy-start.6 = (f32[256]{0:T(256)S(1)}, f32[256]{0:T(256)}, u32[]{:S(2)}) copy-start(f32[256]{0:T(256)} %param.15) | copy-start | bytes 3076
  6.5 19.4 %copy-start.7 = (f32[160]{0:T(256)S(1)}, f32[160]{0:T(256)}, u32[]{:S(2)}) copy-start(f32[160]{0:T(256)} %param.13) | copy-start | bytes 1924
  6.5 65.4 %all-gather.5.cloned.1.call-start = ((), (), s32[]{:S(2)}) async-start(), calls=%async_computation | async-start | bytes 2949120 | tf_op jit(solution)/shard_map/all_gather | solution.py:225
  24.5 20.5 %copy-start = (bf16[5120,256]{1,0:T(8,128)(2,1)S(1)}, bf16[5120,256]{1,0:T(8,128)(2,1)}, u32[]{:S(2)}) copy-start(bf16[5120,256]{1,0:T(8,128)(2,1)} %refs_7_.2) | copy-start | bytes 7864324
  26.0 46.0 %copy-start.1 = (f32[416]{0:T(512)}, f32[416]{0:T(512)S(1)}, u32[]{:S(2)}) copy-start(f32[416]{0:T(512)S(1)} %pad_maximum_fusion.1.refs_9_) | copy-start | bytes 4996
  38.0 34.0 %copy-start.5 = (bf16[320,1176]{1,0:T(8,128)(2,1)}, bf16[320,1176]{1,0:T(8,128)(2,1)S(1)}, u32[]{:S(2)}) copy-start(bf16[320,1176]{1,0:T(8,128)(2,1)S(1)} %all-gather.1) | copy-start | bytes 2257924
  38.1 33.9 %collective-permute-start.5 = (bf16[160,5120]{1,0:T(8,128)(2,1)}, bf16[160,5120]{1,0:T(8,128)(2,1)}, u32[]{:S(2)}, u32[]{:S(2)}) collective-permute-start(bf16[160,5120]{1,0:T(8,128)(2,1)} %bitcast.22), channel_id=1, source_target_pairs={{0,1},{1,0},{2,3},{3,2},{4,5},{5,4},{6,7},{7,6},{8,9},{9,8},{10,11... | collective-permute-start | bytes 4915208 | tf_op jit(solution)/shard_map/ppermute | solution.py:18
  42.9 16.1 %collective-permute-start = (bf16[4,80,1176]{2,1,0:T(8,128)(2,1)S(1)}, bf16[4,80,1176]{2,1,0:T(8,128)(2,1)S(1)}, u32[]{:S(2)}, u32[]{:S(2)}) collective-permute-start(bf16[4,80,1176]{2,1,0:T(8,128)(2,1)S(1)} %bitcast.12), channel_id=1, source_target_pairs={{0,112},{1,33},{32,0},{33,65},{64,32},{65,97},{96,64},{97,17},{16,... | collective-permute-start | bytes 2257928 | tf_op jit(solution)/shard_map/ppermute | solution.py:27
  45.0 86.5 %collective-permute-start.13 = (bf16[5120,256]{1,0:T(8,128)(2,1)S(1)}, bf16[5120,256]{1,0:T(8,128)(2,1)}, u32[]{:S(2)}, u32[]{:S(2)}) collective-permute-start(bf16[5120,256]{1,0:T(8,128)(2,1)S(1)} %copy-done), channel_id=1, source_target_pairs={{0,1},{1,0},{2,3},{3,2},{4,5},{5,4},{6,7},{7,6},{8,9},{9,8},{10,11... | collective-permute-start | bytes 7864328 | tf_op jit(solution)/shard_map/ppermute | solution.py:18
  46.9 17.2 %collective-permute-start.2 = (bf16[2,80,1176]{2,1,0:T(8,128)(2,1)S(1)}, bf16[2,80,1176]{2,1,0:T(8,128)(2,1)S(1)}, u32[]{:S(2)}, u32[]{:S(2)}) collective-permute-start(bf16[2,80,1176]{2,1,0:T(8,128)(2,1)S(1)} %bitcast.19), channel_id=1, source_target_pairs={{0,80},{1,65},{32,112},{33,97},{64,0},{65,17},{96,32},{97,49},{16,... | collective-permute-start | bytes 1128968 | tf_op jit(solution)/shard_map/ppermute | solution.py:27
  59.0 5.1 %copy-start.8 = (bf16[4,80,1176]{2,1,0:T(8,128)(2,1)}, bf16[4,80,1176]{2,1,0:T(8,128)(2,1)S(1)}, u32[]{:S(2)}) copy-start(bf16[4,80,1176]{2,1,0:T(8,128)(2,1)S(1)} %collective-permute-done.refs_1_) | copy-start | bytes 2257924
  59.0 11.3 %collective-permute-start.1 = (bf16[4,80,1176]{2,1,0:T(8,128)(2,1)S(1)}, bf16[4,80,1176]{2,1,0:T(8,128)(2,1)S(1)}, u32[]{:S(2)}, u32[]{:S(2)}) collective-permute-start(bf16[4,80,1176]{2,1,0:T(8,128)(2,1)S(1)} %collective-permute-done.refs_1_), channel_id=1, source_target_pairs={{0,1},{1,0},{2,3},{3,2},{4,5},{5,4},{6,7},{7,6},{8,9},{9,8},{10,11... | collective-permute-start | bytes 2257928 | tf_op jit(solution)/shard_map/ppermute | solution.py:18
  60.9 3.2 %collective-permute-start.3 = (f32[416]{0:T(512)S(1)}, f32[416]{0:T(512)S(1)}, u32[]{:S(2)}, u32[]{:S(2)}) collective-permute-start(f32[416]{0:T(512)S(1)} %pad_maximum_fusion.1.refs_9_), channel_id=1, source_target_pairs={{0,1},{1,0},{2,3},{3,2},{4,5},{5,4},{6,7},{7,6},{8,9},{9,8},{10,11... | collective-permute-start | bytes 5000 | tf_op jit(solution)/shard_map/ppermute | solution.py:18
  64.1 7.9 %copy-start.3 = (f32[416]{0:T(512)}, f32[416]{0:T(512)S(1)}, u32[]{:S(2)}) copy-start(f32[416]{0:T(512)S(1)} %collective-permute-done.3.refs_10_) | copy-start | bytes 4996
  64.1 6.2 %copy-start.10 = (bf16[2,80,1176]{2,1,0:T(8,128)(2,1)}, bf16[2,80,1176]{2,1,0:T(8,128)(2,1)S(1)}, u32[]{:S(2)}) copy-start(bf16[2,80,1176]{2,1,0:T(8,128)(2,1)S(1)} %collective-permute-done.2.refs_3_) | copy-start | bytes 1128964
  64.1 6.1 %collective-permute-start.4 = (bf16[2,80,1176]{2,1,0:T(8,128)(2,1)S(1)}, bf16[2,80,1176]{2,1,0:T(8,128)(2,1)S(1)}, u32[]{:S(2)}, u32[]{:S(2)}) collective-permute-start(bf16[2,80,1176]{2,1,0:T(8,128)(2,1)S(1)} %collective-permute-done.2.refs_3_), channel_id=1, source_target_pairs={{0,1},{1,0},{2,3},{3,2},{4,5},{5,4},{6,7},{7,6},{8,9},{9,8},{10,11... | collective-permute-start | bytes 1128968 | tf_op jit(solution)/shard_map/ppermute | solution.py:18
  70.2 0.8 copy-start.11
  71.0 1.0 copy-start.9
  95.5 12.6 %collective-permute-start.6 = (bf16[2,128,640]{2,1,0:T(8,128)(2,1)S(1)}, bf16[2,128,640]{2,1,0:T(8,128)(2,1)S(1)}, u32[]{:S(2)}, u32[]{:S(2)}) collective-permute-start(bf16[2,128,640]{2,1,0:T(8,128)(2,1)S(1)} %all_gather.25.refs_0_), channel_id=1, source_target_pairs={{0,2},{2,4},{4,6},{6,8},{8,10},{10,12},{12,14},{14,0},{1,3},{3,5},... | collective-permute-start | bytes 983048 | tf_op jit(solution)/shard_map/ppermute | solution.py:18
  98.8 11.3 %collective-permute-start.10 = (bf16[2,128,640]{2,1,0:T(8,128)(2,1)S(1)}, bf16[2,128,640]{2,1,0:T(8,128)(2,1)S(1)}, u32[]{:S(2)}, u32[]{:S(2)}) collective-permute-start(bf16[2,128,640]{2,1,0:T(8,128)(2,1)S(1)} %all_gather.25.refs_0_), channel_id=1, source_target_pairs={{0,14},{2,0},{4,2},{6,4},{8,6},{10,8},{12,10},{14,12},{1,15},{3,1}... | collective-permute-start | bytes 983048 | tf_op jit(solution)/shard_map/ppermute | solution.py:18
  108.1 11.2 %collective-permute-start.7 = (bf16[2,128,640]{2,1,0:T(8,128)(2,1)S(1)}, bf16[2,128,640]{2,1,0:T(8,128)(2,1)S(1)}, u32[]{:S(2)}, u32[]{:S(2)}) collective-permute-start(bf16[2,128,640]{2,1,0:T(8,128)(2,1)S(1)} %collective-permute-done.6.refs_1_), channel_id=1, source_target_pairs={{0,2},{2,4},{4,6},{6,8},{8,10},{10,12},{12,14},{14,0},{1,3},{3,5},... | collective-permute-start | bytes 983048 | tf_op jit(solution)/shard_map/ppermute | solution.py:18
  110.1 11.2 %collective-permute-start.11 = (bf16[2,128,640]{2,1,0:T(8,128)(2,1)S(1)}, bf16[2,128,640]{2,1,0:T(8,128)(2,1)S(1)}, u32[]{:S(2)}, u32[]{:S(2)}) collective-permute-start(bf16[2,128,640]{2,1,0:T(8,128)(2,1)S(1)} %collective-permute-done.10.refs_4_), channel_id=1, source_target_pairs={{0,14},{2,0},{4,2},{6,4},{8,6},{10,8},{12,10},{14,12},{1,15},{3,1}... | collective-permute-start | bytes 983048 | tf_op jit(solution)/shard_map/ppermute | solution.py:18
  119.3 10.2 %collective-permute-start.8 = (bf16[2,128,640]{2,1,0:T(8,128)(2,1)S(1)}, bf16[2,128,640]{2,1,0:T(8,128)(2,1)S(1)}, u32[]{:S(2)}, u32[]{:S(2)}) collective-permute-start(bf16[2,128,640]{2,1,0:T(8,128)(2,1)S(1)} %collective-permute-done.7.refs_2_), channel_id=1, source_target_pairs={{0,2},{2,4},{4,6},{6,8},{8,10},{10,12},{12,14},{14,0},{1,3},{3,5},... | collective-permute-start | bytes 983048 | tf_op jit(solution)/shard_map/ppermute | solution.py:18
  121.2 10.2 %collective-permute-start.12 = (bf16[2,128,640]{2,1,0:T(8,128)(2,1)S(1)}, bf16[2,128,640]{2,1,0:T(8,128)(2,1)S(1)}, u32[]{:S(2)}, u32[]{:S(2)}) collective-permute-start(bf16[2,128,640]{2,1,0:T(8,128)(2,1)S(1)} %collective-permute-done.11.refs_5_), channel_id=1, source_target_pairs={{0,14},{2,0},{4,2},{6,4},{8,6},{10,8},{12,10},{14,12},{1,15},{3,1}... | collective-permute-start | bytes 983048 | tf_op jit(solution)/shard_map/ppermute | solution.py:18
  129.6 9.3 %collective-permute-start.9 = (bf16[2,128,640]{2,1,0:T(8,128)(2,1)S(1)}, bf16[2,128,640]{2,1,0:T(8,128)(2,1)S(1)}, u32[]{:S(2)}, u32[]{:S(2)}) collective-permute-start(bf16[2,128,640]{2,1,0:T(8,128)(2,1)S(1)} %collective-permute-done.8.refs_3_), channel_id=1, source_target_pairs={{0,2},{2,4},{4,6},{6,8},{8,10},{10,12},{12,14},{14,0},{1,3},{3,5},... | collective-permute-start | bytes 983048 | tf_op jit(solution)/shard_map/ppermute | solution.py:18
  131.5 0.6 copy-start.2
  132.1 0.7 copy-start.4
Sparse Core Ops, SparseCore 0:
  26.0 42.2 all-gather.4

commit v5 on v4

--- a/solution.py
+++ b/solution.py
@@ -29,7 +29,7 @@
 
 def embed_kernel(px, *refs):
     w_here, w_near, w_near_o, w_two, w_two_o, p_own, p_oth, gain, beta, b_own, b_oth = refs[:11]
-    out, xs, ws, ps, es, gs, bs, os, ts, sems = refs[11:]
+    out, later, xs, ws, ps, es, gs, bs, os, ts, sems = refs[11:]
     zl, core = lax.axis_index("zl"), lax.axis_index("c")
     loads = []
 
@@ -80,7 +80,10 @@
             normed, p[:, ij * C : (ij + 1) * C], dims, preferred_element_type=F32
         )
         pre = part if ij == 0 else pre + part
-    bias = [r[...].reshape(1, -1)[:, : PART // 2] for r in (os, ts)]
+    bias = [r[...].reshape(1, -1) for r in (os, ts)]
+    for n in range(2):
+        later[n : n + 1, :] = bias[n][:, PART // 2 :]
+    bias = [r[:, : PART // 2] for r in bias]
     bias = [jnp.where(core == n, bias[0], bias[1]) for n in range(2)]
     pre += jnp.concatenate(bias, axis=1)
     h = 0.5 * pre * (1.0 + lax.erf(pre * (0.5**0.5)))
@@ -94,11 +97,14 @@
 def embed_hidden(px, w, p_own, p_oth, gain, beta, b_own, b_oth):
     vmem = pl.BlockSpec(memory_space=pltpu.VMEM)
     any_ = pl.BlockSpec(memory_space=pl.ANY)
-    out = pl.pallas_call(
+    out, later = pl.pallas_call(
         embed_kernel,
-        out_shape=jax.ShapeDtypeStruct((NY, 16, 2 * PART), BF),
+        out_shape=[
+            jax.ShapeDtypeStruct((NY, 16, 2 * PART), BF),
+            jax.ShapeDtypeStruct((2, 256), F32),
+        ],
         in_specs=[any_] * 12,
-        out_specs=vmem,
+        out_specs=[vmem] * 2,
         scratch_shapes=[
             pltpu.VMEM((NY, 2, 4, 16, KP), BF),
             pltpu.VMEM((NX, NZ, 80, KP), BF),
@@ -116,7 +122,7 @@
         ),
         name="embed_hidden",
     )(px, *w, p_own, p_oth, gain, beta, b_own, b_oth)
-    return out.reshape(TOK // 2, 2 * PART)
+    return out.reshape(TOK // 2, 2 * PART), later
 
 
 def hidden_dot(h, lane, w):
@@ -132,14 +138,14 @@
 
 def most_kernel(*refs):
     hs = refs[: NY - 1]
-    p_own, p_oth, b_own, b_oth, acc, far, hv, bs, sems = refs[NY - 1 :]
+    p_own, p_oth, bs, acc, far, hv, sems = refs[NY - 1 :]
     y = lax.axis_index("y")
-    loads = [pltpu.make_async_copy(b, bs.at[n], sems.at[n]) for n, b in enumerate((b_own, b_oth))]
+    loads = []
     last = lax.rem(y + NY // 2, NY)
     for k, p in enumerate((p_own, p_oth)):
         for zh in range(2):
             rows = pl.ds(pl.multiple_of((zh * NY + last) * PART, 64), PART)
-            loads.append(pltpu.make_async_copy(p.at[rows], far.at[k, zh], sems.at[2 + 2 * k + zh]))
+            loads.append(pltpu.make_async_copy(p.at[rows], far.at[k, zh], sems.at[2 * k + zh]))
     for c in loads:
         c.start()
     hv[last] = jnp.zeros_like(hs[0])
@@ -159,7 +165,7 @@
     for c in loads:
         c.wait()
     for k in range(2):
-        acc[k] += bs[k : k + 1, PART // 2 :]
+        acc[k] += bs[k : k + 1, :]
 
 
 def last_kernel(h, acc, far, o_own, o_oth):
@@ -171,8 +177,7 @@
         o[...] = total.astype(BF)
 
 
-def project_out(hs, p_own, p_oth, b_own, b_oth):
-    any_ = pl.BlockSpec(memory_space=pl.ANY)
+def project_out(hs, p_own, p_oth, bias):
     vmem = pl.BlockSpec(memory_space=pltpu.VMEM)
     acc, far = pl.pallas_call(
         most_kernel,
@@ -180,19 +185,18 @@
             jax.ShapeDtypeStruct((2, TOK, 256), F32),
             jax.ShapeDtypeStruct((2, 2, PART, 256), BF),
         ],
-        in_specs=[vmem] * 9 + [any_] * 2,
+        in_specs=[vmem] * 10,
         out_specs=[vmem] * 2,
         scratch_shapes=[
             pltpu.VMEM((NY, 2, TOK // 2, 2 * PART), BF),
-            pltpu.VMEM((2, 160 + 256), F32),
-            pltpu.SemaphoreType.DMA((6,)),
+            pltpu.SemaphoreType.DMA((4,)),
         ],
         compiler_params=pltpu.CompilerParams(vmem_limit_bytes=12 << 20),
         cost_estimate=pl.CostEstimate(
             flops=2 * TOK * HID * 512, bytes_accessed=1 << 20, transcendentals=0
         ),
         name="project_most",
-    )(*hs[:-1], p_own, p_oth, b_own, b_oth)
+    )(*hs[:-1], p_own, p_oth, bias)
     return pl.pallas_call(
         last_kernel,
         out_shape=[jax.ShapeDtypeStruct((TOK, 256), BF)] * 2,
@@ -236,7 +240,7 @@
     near_o = shift(near, "c", 2, 1)
     two, bias_o = lax.optimization_barrier((two, bias_o))
     two_o = shift(two, "c", 2, 1)
-    hid = embed_hidden(
+    hid, later = embed_hidden(
         px,
         (wx, near, near_o, two, two_o),
         p_in,
@@ -247,7 +251,7 @@
         bias_o,
     )
     hs = ring(lax.all_gather(hid, "zh", axis=0))
-    o_own, o_oth = project_out(hs, p_out, p_out_o, bias, bias_o)
+    o_own, o_oth = project_out(hs, p_out, p_out_o, later)
     o_got = lax.all_gather(o_oth, "c", axis=0)
     result = jnp.stack([jnp.where(first, o_own, o_got[0]), jnp.where(first, o_got[1], o_own)])
     return result.reshape(2, 16, 16, 256)

time: 153 us -> 154 us (level)
  the two profiles are of different devices: /device:TPU:135 before, /device:TPU:67 now
where the time goes in v5:
time: 154 us; the launch traced here: 153 us
  blocking collectives  50.8 us (33%)
  starting transfers between devices  41.5 us (27%)
  waiting for transfers between devices  27.8 us (18%)
  Pallas kernels  14.7 us (10%)
  between operations  13.6 us (9%)
  local copies, waits for them, and re-layouts  3.2 us (2%)
    ppermute x12, starting transfers between devices, shift(): return lax.ppermute(v, axis, [(i, (i + by) % n) for i in range(n)])  34.4 us
    all_gather x1, blocking collectives, per_device(): lax.all_gather(pixels.reshape(2, 32, KP), ('zh', 'c'), axis=0)  18.2 us
    ppermute x12, waiting for transfers between devices, shift(): return lax.ppermute(v, axis, [(i, (i + by) % n) for i in range(n)])  17.5 us
    all_gather x1, blocking collectives, per_device(): hs = ring(lax.all_gather(hid, 'zh', axis=0))  14.4 us
    all_gather x1, blocking collectives, per_device(): wx = lax.all_gather(wt, 'x', axis=0)  12.4 us
    ppermute x2, waiting for transfers between devices, shift_cores(): return lax.ppermute(v, ('zl', 'zh', 'c'), pairs)  10.3 us
    pallas_call x1, Pallas kernels, embed_hidden(): pl.pallas_call(embed_kernel, out_shape=[jax.ShapeDtypeStruct((NY, 16, 2 *...  9.2 us
    ppermute x2, starting transfers between devices, shift_cores(): return lax.ppermute(v, ('zl', 'zh', 'c'), pairs)  7.09 us
  transfers between devices with their start and end apart: 15, of which 8 were waited for; matrix products, arithmetic and copies ran while one was open for 0% of the time, Pallas kernels for 9%

profile of v5, /device:TPU:67, one launch (start us, length us, event | category | flops | bytes accessed | tf_op | source)
XLA Modules:
  0.0 153.1 jit_solution(2994053070946546227)
XLA Ops:
  6.5 0.0 copy-start.4
  6.5 0.0 copy-start.5
  6.5 0.0 all-gather.5.cloned.1.call-start
  6.5 18.2 %all-gather = bf16[8,1,32,1176]{3,2,1,0:T(8,128)(2,1)S(1)} all-gather(bf16[2,1,32,1176]{3,2,1,0:T(8,128)(2,1)} %param.8), channel_id=2, replica_groups=mesh['x'=4,'zl'=4,'zh'=2,'y'=8,'c'=2] {'zh','c'}, dimensions={0}, use_global_device_ids=true | all-gather | bytes 752640 | tf_op jit(solution)/shard_map/all_gather | solution.py:226
  24.8 0.0 copy-start
  24.8 0.6 broadcast_select_fusion
  25.4 0.8 copy.16
  26.2 0.0 all-gather.5.cloned.1.call-update
  26.2 0.0 copy-done.4
  26.2 0.0 copy-done.5
  26.2 0.1 pad_maximum_fusion.1.refs_9_
  26.3 0.0 copy-start.3
  26.3 12.4 %all-gather.1 = bf16[320,1176]{1,0:T(8,128)(2,1)S(1)} all-gather(bf16[80,1176]{1,0:T(8,128)(2,1)} %bitcast.20), channel_id=3, replica_groups=mesh['x'=4,'zl'=4,'zh'=2,'y'=8,'c'=2] {'x'}, dimensions={0}, use_global_device_ids=true | all-gather | bytes 940800 | tf_op jit(solution)/shard_map/all_gather | solution.py:232
  38.7 0.0 copy-start.2
  38.7 4.5 %collective-permute-start.5 = (bf16[160,5120]{1,0:T(8,128)(2,1)}, bf16[160,5120]{1,0:T(8,128)(2,1)}, u32[]{:S(2)}, u32[]{:S(2)}) collective-permute-start(bf16[160,5120]{1,0:T(8,128)(2,1)} %bitcast.22), channel_id=1, source_target_pairs={{0,1},{1,0},{2,3},{3,2},{4,5},{5,4},{6,7},{7,6},{8,9},{9,8},{10,11... | collective-permute-start | bytes 4915208 | tf_op jit(solution)/shard_map/ppermute | solution.py:18
  43.2 3.7 %collective-permute-start = (bf16[4,80,1176]{2,1,0:T(8,128)(2,1)S(1)}, bf16[4,80,1176]{2,1,0:T(8,128)(2,1)S(1)}, u32[]{:S(2)}, u32[]{:S(2)}) collective-permute-start(bf16[4,80,1176]{2,1,0:T(8,128)(2,1)S(1)} %bitcast.12), channel_id=1, source_target_pairs={{0,112},{1,33},{32,0},{33,65},{64,32},{65,97},{96,64},{97,17},{16,... | collective-permute-start | bytes 2257928 | tf_op jit(solution)/shard_map/ppermute | solution.py:27
  47.0 0.0 copy-done
  47.0 1.9 %collective-permute-start.13 = (bf16[5120,256]{1,0:T(8,128)(2,1)S(1)}, bf16[5120,256]{1,0:T(8,128)(2,1)}, u32[]{:S(2)}, u32[]{:S(2)}) collective-permute-start(bf16[5120,256]{1,0:T(8,128)(2,1)S(1)} %copy-done), channel_id=1, source_target_pairs={{0,1},{1,0},{2,3},{3,2},{4,5},{5,4},{6,7},{7,6},{8,9},{9,8},{10,11... | collective-permute-start | bytes 7864328 | tf_op jit(solution)/shard_map/ppermute | solution.py:18
  48.9 3.4 %collective-permute-start.2 = (bf16[2,80,1176]{2,1,0:T(8,128)(2,1)S(1)}, bf16[2,80,1176]{2,1,0:T(8,128)(2,1)S(1)}, u32[]{:S(2)}, u32[]{:S(2)}) collective-permute-start(bf16[2,80,1176]{2,1,0:T(8,128)(2,1)S(1)} %bitcast.19), channel_id=1, source_target_pairs={{0,80},{1,65},{32,112},{33,97},{64,0},{65,17},{96,32},{97,49},{16,... | collective-permute-start | bytes 1128968 | tf_op jit(solution)/shard_map/ppermute | solution.py:27
  52.3 6.5 %collective-permute-done.refs_1_ = bf16[4,80,1176]{2,1,0:T(8,128)(2,1)S(1)} collective-permute-done((bf16[4,80,1176]{2,1,0:T(8,128)(2,1)S(1)}, bf16[4,80,1176]{2,1,0:T(8,128)(2,1)S(1)}, u32[]{:S(2)}, u32[]{:S(2)}) %collective-permute-start) | collective-permute-done | bytes 752672 | tf_op jit(solution)/shard_map/ppermute | solution.py:27
  58.8 0.0 copy-start.6
  58.8 1.9 %collective-permute-start.1 = (bf16[4,80,1176]{2,1,0:T(8,128)(2,1)S(1)}, bf16[4,80,1176]{2,1,0:T(8,128)(2,1)S(1)}, u32[]{:S(2)}, u32[]{:S(2)}) collective-permute-start(bf16[4,80,1176]{2,1,0:T(8,128)(2,1)S(1)} %collective-permute-done.refs_1_), channel_id=1, source_target_pairs={{0,1},{1,0},{2,3},{3,2},{4,5},{5,4},{6,7},{7,6},{8,9},{9,8},{10,11... | collective-permute-start | bytes 2257928 | tf_op jit(solution)/shard_map/ppermute | solution.py:18
  60.7 2.4 %collective-permute-start.3 = (f32[416]{0:T(512)S(1)}, f32[416]{0:T(512)S(1)}, u32[]{:S(2)}, u32[]{:S(2)}) collective-permute-start(f32[416]{0:T(512)S(1)} %pad_maximum_fusion.1.refs_9_), channel_id=1, source_target_pairs={{0,1},{1,0},{2,3},{3,2},{4,5},{5,4},{6,7},{7,6},{8,9},{9,8},{10,11... | collective-permute-start | bytes 5000 | tf_op jit(solution)/shard_map/ppermute | solution.py:18
  63.1 0.8 collective-permute-done.3.refs_10_
  63.9 0.0 copy-start.10
  63.9 3.7 %collective-permute-done.2.refs_3_ = bf16[2,80,1176]{2,1,0:T(8,128)(2,1)S(1)} collective-permute-done((bf16[2,80,1176]{2,1,0:T(8,128)(2,1)S(1)}, bf16[2,80,1176]{2,1,0:T(8,128)(2,1)S(1)}, u32[]{:S(2)}, u32[]{:S(2)}) %collective-permute-start.2) | collective-permute-done | bytes 376352 | tf_op jit(solution)/shard_map/ppermute | solution.py:27
  67.7 0.0 copy-done.6
  67.7 0.0 copy-start.8
  67.7 1.9 %collective-permute-start.4 = (bf16[2,80,1176]{2,1,0:T(8,128)(2,1)S(1)}, bf16[2,80,1176]{2,1,0:T(8,128)(2,1)S(1)}, u32[]{:S(2)}, u32[]{:S(2)}) collective-permute-start(bf16[2,80,1176]{2,1,0:T(8,128)(2,1)S(1)} %collective-permute-done.2.refs_3_), channel_id=1, source_target_pairs={{0,1},{1,0},{2,3},{3,2},{4,5},{5,4},{6,7},{7,6},{8,9},{9,8},{10,11... | collective-permute-start | bytes 1128968 | tf_op jit(solution)/shard_map/ppermute | solution.py:18
  69.6 1.7 %collective-permute-done.4.refs_4_ = bf16[2,80,1176]{2,1,0:T(8,128)(2,1)S(1)} collective-permute-done((bf16[2,80,1176]{2,1,0:T(8,128)(2,1)S(1)}, bf16[2,80,1176]{2,1,0:T(8,128)(2,1)S(1)}, u32[]{:S(2)}, u32[]{:S(2)}) %collective-permute-start.4) | collective-permute-done | bytes 376352 | tf_op jit(solution)/shard_map/ppermute | solution.py:18
  71.3 0.0 copy-start.9
  71.3 0.0 collective-permute-done.1.refs_2_
  71.3 0.0 copy-done.8
  71.3 0.8 copy-done.9
  72.1 0.0 copy-start.7
  72.1 1.0 copy-done.7
  73.0 0.0 collective-permute-done.5.refs_6_
  73.0 0.0 all-gather.5.cloned.1.call-done.px
  73.0 0.0 copy-done.3
  73.0 0.0 copy-done.2
  73.0 0.0 copy-done.10
  73.1 9.2 %embed_hidden.1 = (bf16[8,16,640]{2,1,0:T(8,128)(2,1)}, f32[2,256]{1,0:T(2,128)}) custom-call(bf16[8,2,4,16,1176]{4,3,2,1,0:T(8,128)(2,1)} %all-gather.5.cloned.1.call-done.px, bf16[4,80,1176]{2,1,0:T(8,128)(2,1)} %bitcast.13, bf16[4,80,1176]{2,1,0:T(8,128)(2,1)} %copy-done.6, bf16[4,80,1176]{2,1,0:T(8,128)(2,1)} %copy-done.7, ...), custom_call_target="tpu_custom_call" | custom-call | flops 3921674240 | bytes 9437184 | tf_op jit(solution)/shard_map/embed_hidden/pallas_call | solution.py:100
  82.3 14.4 %all_gather.25.refs_0_ = bf16[2,128,640]{2,1,0:T(8,128)(2,1)S(1)} all-gather(bf16[1,128,640]{2,1,0:T(8,128)(2,1)} %bitcast.21), channel_id=1, replica_groups=mesh['x'=4,'zl'=4,'zh'=2,'y'=8,'c'=2] {'zh'}, dimensions={0}, use_global_device_ids=true | all-gather | bytes 491520 | tf_op jit(solution)/shard_map/all_gather | solution.py:253
  96.6 3.2 %collective-permute-start.6 = (bf16[2,128,640]{2,1,0:T(8,128)(2,1)S(1)}, bf16[2,128,640]{2,1,0:T(8,128)(2,1)S(1)}, u32[]{:S(2)}, u32[]{:S(2)}) collective-permute-start(bf16[2,128,640]{2,1,0:T(8,128)(2,1)S(1)} %all_gather.25.refs_0_), channel_id=1, source_target_pairs={{0,2},{2,4},{4,6},{6,8},{8,10},{10,12},{12,14},{14,0},{1,3},{3,5},... | collective-permute-start | bytes 983048 | tf_op jit(solution)/shard_map/ppermute | solution.py:18
  99.8 3.7 %collective-permute-start.10 = (bf16[2,128,640]{2,1,0:T(8,128)(2,1)S(1)}, bf16[2,128,640]{2,1,0:T(8,128)(2,1)S(1)}, u32[]{:S(2)}, u32[]{:S(2)}) collective-permute-start(bf16[2,128,640]{2,1,0:T(8,128)(2,1)S(1)} %all_gather.25.refs_0_), channel_id=1, source_target_pairs={{0,14},{2,0},{4,2},{6,4},{8,6},{10,8},{12,10},{14,12},{1,15},{3,1}... | collective-permute-start | bytes 983048 | tf_op jit(solution)/shard_map/ppermute | solution.py:18
  103.5 5.5 %collective-permute-done.6.refs_1_ = bf16[2,128,640]{2,1,0:T(8,128)(2,1)S(1)} collective-permute-done((bf16[2,128,640]{2,1,0:T(8,128)(2,1)S(1)}, bf16[2,128,640]{2,1,0:T(8,128)(2,1)S(1)}, u32[]{:S(2)}, u32[]{:S(2)}) %collective-permute-start.6) | collective-permute-done | bytes 327712 | tf_op jit(solution)/shard_map/ppermute | solution.py:18
  109.0 1.9 %collective-permute-start.7 = (bf16[2,128,640]{2,1,0:T(8,128)(2,1)S(1)}, bf16[2,128,640]{2,1,0:T(8,128)(2,1)S(1)}, u32[]{:S(2)}, u32[]{:S(2)}) collective-permute-start(bf16[2,128,640]{2,1,0:T(8,128)(2,1)S(1)} %collective-permute-done.6.refs_1_), channel_id=1, source_target_pairs={{0,2},{2,4},{4,6},{6,8},{8,10},{10,12},{12,14},{14,0},{1,3},{3,5},... | collective-permute-start | bytes 983048 | tf_op jit(solution)/shard_map/ppermute | solution.py:18
  110.9 0.0 collective-permute-done.10.refs_4_
  110.9 4.6 %collective-permute-start.11 = (bf16[2,128,640]{2,1,0:T(8,128)(2,1)S(1)}, bf16[2,128,640]{2,1,0:T(8,128)(2,1)S(1)}, u32[]{:S(2)}, u32[]{:S(2)}) collective-permute-start(bf16[2,128,640]{2,1,0:T(8,128)(2,1)S(1)} %collective-permute-done.10.refs_4_), channel_id=1, source_target_pairs={{0,14},{2,0},{4,2},{6,4},{8,6},{10,8},{12,10},{14,12},{1,15},{3,1}... | collective-permute-start | bytes 983048 | tf_op jit(solution)/shard_map/ppermute | solution.py:18
  115.5 4.5 %collective-permute-done.7.refs_2_ = bf16[2,128,640]{2,1,0:T(8,128)(2,1)S(1)} collective-permute-done((bf16[2,128,640]{2,1,0:T(8,128)(2,1)S(1)}, bf16[2,128,640]{2,1,0:T(8,128)(2,1)S(1)}, u32[]{:S(2)}, u32[]{:S(2)}) %collective-permute-start.7) | collective-permute-done | bytes 327712 | tf_op jit(solution)/shard_map/ppermute | solution.py:18
  120.1 1.9 %collective-permute-start.8 = (bf16[2,128,640]{2,1,0:T(8,128)(2,1)S(1)}, bf16[2,128,640]{2,1,0:T(8,128)(2,1)S(1)}, u32[]{:S(2)}, u32[]{:S(2)}) collective-permute-start(bf16[2,128,640]{2,1,0:T(8,128)(2,1)S(1)} %collective-permute-done.7.refs_2_), channel_id=1, source_target_pairs={{0,2},{2,4},{4,6},{6,8},{8,10},{10,12},{12,14},{14,0},{1,3},{3,5},... | collective-permute-start | bytes 983048 | tf_op jit(solution)/shard_map/ppermute | solution.py:18
  122.0 0.0 collective-permute-done.11.refs_5_
  122.0 4.6 %collective-permute-start.12 = (bf16[2,128,640]{2,1,0:T(8,128)(2,1)S(1)}, bf16[2,128,640]{2,1,0:T(8,128)(2,1)S(1)}, u32[]{:S(2)}, u32[]{:S(2)}) collective-permute-start(bf16[2,128,640]{2,1,0:T(8,128)(2,1)S(1)} %collective-permute-done.11.refs_5_), channel_id=1, source_target_pairs={{0,14},{2,0},{4,2},{6,4},{8,6},{10,8},{12,10},{14,12},{1,15},{3,1}... | collective-permute-start | bytes 983048 | tf_op jit(solution)/shard_map/ppermute | solution.py:18
  126.6 3.6 %collective-permute-done.8.refs_3_ = bf16[2,128,640]{2,1,0:T(8,128)(2,1)S(1)} collective-permute-done((bf16[2,128,640]{2,1,0:T(8,128)(2,1)S(1)}, bf16[2,128,640]{2,1,0:T(8,128)(2,1)S(1)}, u32[]{:S(2)}, u32[]{:S(2)}) %collective-permute-start.8) | collective-permute-done | bytes 327712 | tf_op jit(solution)/shard_map/ppermute | solution.py:18
  130.2 1.9 %collective-permute-start.9 = (bf16[2,128,640]{2,1,0:T(8,128)(2,1)S(1)}, bf16[2,128,640]{2,1,0:T(8,128)(2,1)S(1)}, u32[]{:S(2)}, u32[]{:S(2)}) collective-permute-start(bf16[2,128,640]{2,1,0:T(8,128)(2,1)S(1)} %collective-permute-done.8.refs_3_), channel_id=1, source_target_pairs={{0,2},{2,4},{4,6},{6,8},{8,10},{10,12},{12,14},{14,0},{1,3},{3,5},... | collective-permute-start | bytes 983048 | tf_op jit(solution)/shard_map/ppermute | solution.py:18
  132.1 0.0 collective-permute-done.13.refs_8_
  132.1 0.0 collective-permute-done.12.refs_6_
  132.1 0.0 copy-start.1
  132.1 0.6 copy-done.1
  132.8 5.1 %project_most.1 = (f32[2,256,256]{2,1,0:T(8,128)S(1)}, bf16[2,2,320,256]{3,2,1,0:T(8,128)(2,1)S(1)}) custom-call(bf16[2,128,640]{2,1,0:T(8,128)(2,1)S(1)} %all_gather.25.refs_0_, bf16[2,128,640]{2,1,0:T(8,128)(2,1)S(1)} %collective-permute-done.6.refs_1_, bf16[2,128,640]{2,1,0:T(8,128)(2,1)S(1)} %collective-permute-done.7.refs_2_, ...), custom_call_target="tpu_custom_call" | custom-call | flops 1342177280 | bytes 1048576 | tf_op jit(solution)/shard_map/project_most/pallas_call | solution.py:182
  137.9 1.3 collective-permute-done.9.h
  139.2 0.4 project_last.1
  139.6 5.9 %all-gather.2 = bf16[512,256]{1,0:T(8,128)(2,1)S(1)} all-gather(bf16[256,256]{1,0:T(8,128)(2,1)S(1)} %get-tuple-element.26), channel_id=4, replica_groups=mesh['x'=4,'zl'=4,'zh'=2,'y'=8,'c'=2] {'c'}, dimensions={0}, use_global_device_ids=true | all-gather | bytes 393216 | tf_op jit(solution)/shard_map/all_gather | solution.py:255
  145.5 0.7 pad_maximum_fusion
  (3 shorter events, 0.1 us)
Async XLA Ops:
  6.5 19.7 %copy-start.4 = (f32[256]{0:T(256)S(1)}, f32[256]{0:T(256)}, u32[]{:S(2)}) copy-start(f32[256]{0:T(256)} %param.15) | copy-start | bytes 3076
  6.5 19.7 %copy-start.5 = (f32[160]{0:T(256)S(1)}, f32[160]{0:T(256)}, u32[]{:S(2)}) copy-start(f32[160]{0:T(256)} %param.13) | copy-start | bytes 1924
  6.5 66.5 %all-gather.5.cloned.1.call-start = ((), (), s32[]{:S(2)}) async-start(), calls=%async_computation | async-start | bytes 2949120 | tf_op jit(solution)/shard_map/all_gather | solution.py:229
  24.8 22.2 %copy-start = (bf16[5120,256]{1,0:T(8,128)(2,1)S(1)}, bf16[5120,256]{1,0:T(8,128)(2,1)}, u32[]{:S(2)}) copy-start(bf16[5120,256]{1,0:T(8,128)(2,1)} %refs_7_.2) | copy-start | bytes 7864324
  26.3 46.8 %copy-start.3 = (f32[416]{0:T(512)}, f32[416]{0:T(512)S(1)}, u32[]{:S(2)}) copy-start(f32[416]{0:T(512)S(1)} %pad_maximum_fusion.1.refs_9_) | copy-start | bytes 4996
  38.7 34.4 %copy-start.2 = (bf16[320,1176]{1,0:T(8,128)(2,1)}, bf16[320,1176]{1,0:T(8,128)(2,1)S(1)}, u32[]{:S(2)}) copy-start(bf16[320,1176]{1,0:T(8,128)(2,1)S(1)} %all-gather.1) | copy-start | bytes 2257924
  38.7 34.3 %collective-permute-start.5 = (bf16[160,5120]{1,0:T(8,128)(2,1)}, bf16[160,5120]{1,0:T(8,128)(2,1)}, u32[]{:S(2)}, u32[]{:S(2)}) collective-permute-start(bf16[160,5120]{1,0:T(8,128)(2,1)} %bitcast.22), channel_id=1, source_target_pairs={{0,1},{1,0},{2,3},{3,2},{4,5},{5,4},{6,7},{7,6},{8,9},{9,8},{10,11... | collective-permute-start | bytes 4915208 | tf_op jit(solution)/shard_map/ppermute | solution.py:18
  43.2 15.6 %collective-permute-start = (bf16[4,80,1176]{2,1,0:T(8,128)(2,1)S(1)}, bf16[4,80,1176]{2,1,0:T(8,128)(2,1)S(1)}, u32[]{:S(2)}, u32[]{:S(2)}) collective-permute-start(bf16[4,80,1176]{2,1,0:T(8,128)(2,1)S(1)} %bitcast.12), channel_id=1, source_target_pairs={{0,112},{1,33},{32,0},{33,65},{64,32},{65,97},{96,64},{97,17},{16,... | collective-permute-start | bytes 2257928 | tf_op jit(solution)/shard_map/ppermute | solution.py:27
  47.0 85.1 %collective-permute-start.13 = (bf16[5120,256]{1,0:T(8,128)(2,1)S(1)}, bf16[5120,256]{1,0:T(8,128)(2,1)}, u32[]{:S(2)}, u32[]{:S(2)}) collective-permute-start(bf16[5120,256]{1,0:T(8,128)(2,1)S(1)} %copy-done), channel_id=1, source_target_pairs={{0,1},{1,0},{2,3},{3,2},{4,5},{5,4},{6,7},{7,6},{8,9},{9,8},{10,11... | collective-permute-start | bytes 7864328 | tf_op jit(solution)/shard_map/ppermute | solution.py:18
  48.9 18.8 %collective-permute-start.2 = (bf16[2,80,1176]{2,1,0:T(8,128)(2,1)S(1)}, bf16[2,80,1176]{2,1,0:T(8,128)(2,1)S(1)}, u32[]{:S(2)}, u32[]{:S(2)}) collective-permute-start(bf16[2,80,1176]{2,1,0:T(8,128)(2,1)S(1)} %bitcast.19), channel_id=1, source_target_pairs={{0,80},{1,65},{32,112},{33,97},{64,0},{65,17},{96,32},{97,49},{16,... | collective-permute-start | bytes 1128968 | tf_op jit(solution)/shard_map/ppermute | solution.py:27
  58.8 8.9 %copy-start.6 = (bf16[4,80,1176]{2,1,0:T(8,128)(2,1)}, bf16[4,80,1176]{2,1,0:T(8,128)(2,1)S(1)}, u32[]{:S(2)}) copy-start(bf16[4,80,1176]{2,1,0:T(8,128)(2,1)S(1)} %collective-permute-done.refs_1_) | copy-start | bytes 2257924
  58.8 12.5 %collective-permute-start.1 = (bf16[4,80,1176]{2,1,0:T(8,128)(2,1)S(1)}, bf16[4,80,1176]{2,1,0:T(8,128)(2,1)S(1)}, u32[]{:S(2)}, u32[]{:S(2)}) collective-permute-start(bf16[4,80,1176]{2,1,0:T(8,128)(2,1)S(1)} %collective-permute-done.refs_1_), channel_id=1, source_target_pairs={{0,1},{1,0},{2,3},{3,2},{4,5},{5,4},{6,7},{7,6},{8,9},{9,8},{10,11... | collective-permute-start | bytes 2257928 | tf_op jit(solution)/shard_map/ppermute | solution.py:18
  60.7 3.2 %collective-permute-start.3 = (f32[416]{0:T(512)S(1)}, f32[416]{0:T(512)S(1)}, u32[]{:S(2)}, u32[]{:S(2)}) collective-permute-start(f32[416]{0:T(512)S(1)} %pad_maximum_fusion.1.refs_9_), channel_id=1, source_target_pairs={{0,1},{1,0},{2,3},{3,2},{4,5},{5,4},{6,7},{7,6},{8,9},{9,8},{10,11... | collective-permute-start | bytes 5000 | tf_op jit(solution)/shard_map/ppermute | solution.py:18
  63.9 9.1 %copy-start.10 = (f32[416]{0:T(512)}, f32[416]{0:T(512)S(1)}, u32[]{:S(2)}) copy-start(f32[416]{0:T(512)S(1)} %collective-permute-done.3.refs_10_) | copy-start | bytes 4996
  67.7 3.6 %copy-start.8 = (bf16[2,80,1176]{2,1,0:T(8,128)(2,1)}, bf16[2,80,1176]{2,1,0:T(8,128)(2,1)S(1)}, u32[]{:S(2)}) copy-start(bf16[2,80,1176]{2,1,0:T(8,128)(2,1)S(1)} %collective-permute-done.2.refs_3_) | copy-start | bytes 1128964
  67.7 3.6 %collective-permute-start.4 = (bf16[2,80,1176]{2,1,0:T(8,128)(2,1)S(1)}, bf16[2,80,1176]{2,1,0:T(8,128)(2,1)S(1)}, u32[]{:S(2)}, u32[]{:S(2)}) collective-permute-start(bf16[2,80,1176]{2,1,0:T(8,128)(2,1)S(1)} %collective-permute-done.2.refs_3_), channel_id=1, source_target_pairs={{0,1},{1,0},{2,3},{3,2},{4,5},{5,4},{6,7},{7,6},{8,9},{9,8},{10,11... | collective-permute-start | bytes 1128968 | tf_op jit(solution)/shard_map/ppermute | solution.py:18
  71.3 0.8 copy-start.9
  72.1 1.0 copy-start.7
  96.6 12.4 %collective-permute-start.6 = (bf16[2,128,640]{2,1,0:T(8,128)(2,1)S(1)}, bf16[2,128,640]{2,1,0:T(8,128)(2,1)S(1)}, u32[]{:S(2)}, u32[]{:S(2)}) collective-permute-start(bf16[2,128,640]{2,1,0:T(8,128)(2,1)S(1)} %all_gather.25.refs_0_), channel_id=1, source_target_pairs={{0,2},{2,4},{4,6},{6,8},{8,10},{10,12},{12,14},{14,0},{1,3},{3,5},... | collective-permute-start | bytes 983048 | tf_op jit(solution)/shard_map/ppermute | solution.py:18
  99.8 11.1 %collective-permute-start.10 = (bf16[2,128,640]{2,1,0:T(8,128)(2,1)S(1)}, bf16[2,128,640]{2,1,0:T(8,128)(2,1)S(1)}, u32[]{:S(2)}, u32[]{:S(2)}) collective-permute-start(bf16[2,128,640]{2,1,0:T(8,128)(2,1)S(1)} %all_gather.25.refs_0_), channel_id=1, source_target_pairs={{0,14},{2,0},{4,2},{6,4},{8,6},{10,8},{12,10},{14,12},{1,15},{3,1}... | collective-permute-start | bytes 983048 | tf_op jit(solution)/shard_map/ppermute | solution.py:18
  109.0 11.1 %collective-permute-start.7 = (bf16[2,128,640]{2,1,0:T(8,128)(2,1)S(1)}, bf16[2,128,640]{2,1,0:T(8,128)(2,1)S(1)}, u32[]{:S(2)}, u32[]{:S(2)}) collective-permute-start(bf16[2,128,640]{2,1,0:T(8,128)(2,1)S(1)} %collective-permute-done.6.refs_1_), channel_id=1, source_target_pairs={{0,2},{2,4},{4,6},{6,8},{8,10},{10,12},{12,14},{14,0},{1,3},{3,5},... | collective-permute-start | bytes 983048 | tf_op jit(solution)/shard_map/ppermute | solution.py:18
  110.9 11.0 %collective-permute-start.11 = (bf16[2,128,640]{2,1,0:T(8,128)(2,1)S(1)}, bf16[2,128,640]{2,1,0:T(8,128)(2,1)S(1)}, u32[]{:S(2)}, u32[]{:S(2)}) collective-permute-start(bf16[2,128,640]{2,1,0:T(8,128)(2,1)S(1)} %collective-permute-done.10.refs_4_), channel_id=1, source_target_pairs={{0,14},{2,0},{4,2},{6,4},{8,6},{10,8},{12,10},{14,12},{1,15},{3,1}... | collective-permute-start | bytes 983048 | tf_op jit(solution)/shard_map/ppermute | solution.py:18
  120.1 10.1 %collective-permute-start.8 = (bf16[2,128,640]{2,1,0:T(8,128)(2,1)S(1)}, bf16[2,128,640]{2,1,0:T(8,128)(2,1)S(1)}, u32[]{:S(2)}, u32[]{:S(2)}) collective-permute-start(bf16[2,128,640]{2,1,0:T(8,128)(2,1)S(1)} %collective-permute-done.7.refs_2_), channel_id=1, source_target_pairs={{0,2},{2,4},{4,6},{6,8},{8,10},{10,12},{12,14},{14,0},{1,3},{3,5},... | collective-permute-start | bytes 983048 | tf_op jit(solution)/shard_map/ppermute | solution.py:18
  122.0 10.1 %collective-permute-start.12 = (bf16[2,128,640]{2,1,0:T(8,128)(2,1)S(1)}, bf16[2,128,640]{2,1,0:T(8,128)(2,1)S(1)}, u32[]{:S(2)}, u32[]{:S(2)}) collective-permute-start(bf16[2,128,640]{2,1,0:T(8,128)(2,1)S(1)} %collective-permute-done.11.refs_5_), channel_id=1, source_target_pairs={{0,14},{2,0},{4,2},{6,4},{8,6},{10,8},{12,10},{14,12},{1,15},{3,1}... | collective-permute-start | bytes 983048 | tf_op jit(solution)/shard_map/ppermute | solution.py:18
  130.2 9.0 %collective-permute-start.9 = (bf16[2,128,640]{2,1,0:T(8,128)(2,1)S(1)}, bf16[2,128,640]{2,1,0:T(8,128)(2,1)S(1)}, u32[]{:S(2)}, u32[]{:S(2)}) collective-permute-start(bf16[2,128,640]{2,1,0:T(8,128)(2,1)S(1)} %collective-permute-done.8.refs_3_), channel_id=1, source_target_pairs={{0,2},{2,4},{4,6},{6,8},{8,10},{10,12},{12,14},{14,0},{1,3},{3,5},... | collective-permute-start | bytes 983048 | tf_op jit(solution)/shard_map/ppermute | solution.py:18
  132.1 0.6 copy-start.1
Sparse Core Ops, SparseCore 0:
  26.3 42.7 all-gather.4
